TPU v7x, 32 devices: a whole 2x2x4 slice. The times are simulated.
32 devices in a mesh: tm: 8 (over y, x, core), sta: 4 (over z).
Axes of the slice: x: 2, y: 2, z: 4, core: 2. Of those that a mesh axis runs over, the one named last changes fastest.
Arguments:
- spectra: bfloat16 [16, 128, 6, 1024], P('tm', 'sta'), may hold values from -6 to 6
- pairs: int32 [4, 4, 2, 16], P('sta'), may hold values from 0 to 31
- counts: int32 [4, 4], P('sta'), may hold values from 3 to 16, as said below
Outputs:
- correlations: bfloat16 [4, 4, 16, 9, 4001], P('sta', None, 'tm')
Inputs may be any that keep to these rules, and one draw needn't show every extreme that they name: `counts`: pair slots at or after a tile's count are ignored; the tiles of shift 0 use all 16 slots.
All inputs are finite; a program needn't handle non-finite values.
Results may differ from a plain program's by a relative error of at most 0.014.
Values may be sent and summed in bfloat16 or wider, within the bound.
A program may use at most 64 MiB of HBM per device.

v0:
```python
import math

import jax
import jax.numpy as jnp
from jax import lax
from jax.sharding import PartitionSpec as P

NF = 1024
NFFT = 8192
LAGS = 4001
BAND = 64


def from_behind(value, axis, steps):
    count = lax.axis_size(axis)
    pairs = [(source, (source + steps) % count) for source in range(count)]
    return lax.ppermute(value, axis, pairs)


def whiten(spectra):
    lead = spectra.shape[:-2]
    values = spectra.astype(jnp.float32).reshape(lead + (3, 2, NF // BAND, BAND))
    power = jnp.mean(values[..., 0, :, :] ** 2 + values[..., 1, :, :] ** 2, axis=-1)
    scaled = values * lax.rsqrt(power[..., None, :, None] + 1e-06)
    return scaled.reshape(lead + (6, NF)).astype(jnp.bfloat16)


def cross(own_rows, visit_rows):
    hours_n, slots, bins = (own_rows.shape[0], own_rows.shape[1], own_rows.shape[-1])
    first = own_rows.astype(jnp.float32).reshape(hours_n, slots, 3, 2, bins)
    second = visit_rows.astype(jnp.float32).reshape(hours_n, slots, 3, 2, bins)
    are, aim = (first[:, :, :, 0][:, :, :, None], first[:, :, :, 1][:, :, :, None])
    bre, bim = (second[:, :, :, 0][:, :, None], second[:, :, :, 1][:, :, None])
    real_part = jnp.sum(are * bre + aim * bim, axis=0).reshape(slots, 9, bins)
    imag_part = jnp.sum(are * bim - aim * bre, axis=0).reshape(slots, 9, bins)
    return jnp.concatenate([real_part, imag_part], axis=-1)


def per_device(spectra, pairs, counts):
    n_tm = lax.axis_size("tm")
    n_sta = lax.axis_size("sta")
    hours_dev = spectra.shape[0]
    p_tile = pairs.shape[3]
    owned = p_tile // n_tm
    white = whiten(spectra)

    def reduce_tile(visiting, shift):
        first_idx = pairs[0, shift, 0]
        second_idx = pairs[0, shift, 1]
        limit = counts[0, shift]
        value = cross(jnp.take(white, first_idx, axis=1), jnp.take(visiting, second_idx, axis=1))
        slots = jnp.arange(lax.axis_size("tm") * owned, dtype=jnp.int32)
        value = value * (slots < limit).astype(jnp.float32)[:, None, None]
        return lax.psum_scatter(
            lax.optimization_barrier(value.astype(jnp.bfloat16))
            .astype(jnp.float32)
            .astype(jnp.bfloat16),
            "tm",
            scatter_dimension=0,
            tiled=True,
        ).astype(jnp.float32)

    reduced = [None] * n_sta
    reduced[0] = reduce_tile(white, 0)
    moving = white
    for step in range(1, n_sta):
        moving = from_behind(moving, "sta", 1)
        reduced[step] = reduce_tile(moving, step)
    rows = jnp.stack(reduced, axis=0).astype(jnp.bfloat16).reshape(n_sta * owned * 9, 2 * NF)
    fblk = min(NF, 256)
    shifts = jnp.arange(LAGS, dtype=jnp.int32) - (LAGS - 1) // 2

    def add_block(index, total):
        start = index * fblk
        freqs = start + jnp.arange(fblk, dtype=jnp.int32)
        phase = jnp.mod(freqs[:, None] * shifts[None, :], NFFT)
        angle = 2.0 * math.pi / NFFT * phase.astype(jnp.float32)
        cosine = jnp.cos(angle).astype(jnp.bfloat16)
        sine = (-jnp.sin(angle)).astype(jnp.bfloat16)
        real_rows = lax.dynamic_slice_in_dim(rows, start, fblk, 1)
        imag_rows = lax.dynamic_slice_in_dim(rows, NF + start, fblk, 1)
        total = total + jnp.dot(real_rows, cosine, preferred_element_type=jnp.float32)
        return total + jnp.dot(imag_rows, sine, preferred_element_type=jnp.float32)

    lagged = lax.fori_loop(0, NF // fblk, add_block, jnp.zeros((rows.shape[0], LAGS), jnp.float32))
    scale = 1.0 / math.sqrt(hours_dev * n_tm * NF)
    result = (lagged * scale).astype(jnp.bfloat16)
    return result.reshape(1, n_sta, owned, 9, LAGS)


def solution(mesh):
    return jax.shard_map(
        per_device,
        mesh=mesh,
        in_specs=(P("tm", "sta", None, None), P("sta", None, None, None), P("sta", None)),
        out_specs=P("sta", None, "tm", None, None),
        check_vma=False,
    )
```

profile of v0, /device:TPU:8, one launch (start us, length us, event | category | flops | bytes accessed | tf_op | source)
XLA Modules:
  0.0 325.0 jit_solution(17896505962292196768)
XLA Ops:
  6.5 3.1 copy_convert_fusion
  9.6 3.0 reshape.131
  12.6 0.6 fusion.18
  13.5 0.5 mul.322
  14.0 2.5 mul.323
  16.5 2.7 multiply_convert_fusion
  19.2 1.8 collective-permute-start
  21.0 0.6 compare_and_fusion.7
  21.6 1.3 gather_fusion.2
  23.0 1.3 gather_fusion.1
  24.3 0.8 broadcast_select_fusion.5
  25.1 0.4 convert.14
  25.9 1.3 gather_fusion
  27.3 0.4 broadcast_select_fusion.7
  27.7 0.4 convert.13
  28.4 0.9 copy.102
  29.2 0.7 fusion.23
  29.9 1.2 compare_convert_fusion.3
  31.1 0.4 convert.15
  31.7 1.3 gather_fusion.4
  33.0 1.3 gather_fusion.6
  34.4 0.8 broadcast_select_fusion.1
  35.2 0.4 convert.17
  35.7 0.4 convert.19
  36.1 0.5 copy-done
  37.3 1.0 fusion.19
  39.2 0.6 compare_convert_fusion.2
  39.8 0.6 compare_convert_fusion.1
  40.4 0.6 compare_convert_fusion
  41.2 2.5 gather_fusion.3
  43.6 0.4 broadcast_select_fusion.4
  44.1 0.4 convert.16
  44.5 2.0 collective-permute-start.1
  46.9 0.4 add_reduce_fusion.2
  47.2 1.0 fusion.20
  48.2 16.0 %collective-permute-done.1 = bf16[2,32,6,1024]{3,0,2,1:T(2,128)(2,1)} collective-permute-done((bf16[2,32,6,1024]{3,0,2,1:T(2,128)(2,1)}, bf16[2,32,6,1024]{3,0,2,1:T(2,128)(2,1)}, u32[]{:S(2)}, u32[]{:S(2)}) %collective-permute-start.1) | collective-permute-done | bytes 786464 | tf_op jit(solution)/shard_map/ppermute | solution.py:17
  64.3 2.5 gather_fusion.5
  66.7 0.4 broadcast_select_fusion.2
  67.2 0.4 convert.18
  67.6 1.6 collective-permute-start.2
  70.0 1.0 fusion.21
  70.9 15.6 %collective-permute-done.2 = bf16[2,32,6,1024]{3,0,2,1:T(2,128)(2,1)S(1)} collective-permute-done((bf16[2,32,6,1024]{3,0,2,1:T(2,128)(2,1)}, bf16[2,32,6,1024]{3,0,2,1:T(2,128)(2,1)S(1)}, u32[]{:S(2)}, u32[]{:S(2)}) %collective-permute-start.2) | collective-permute-done | bytes 786464 | tf_op jit(solution)/shard_map/ppermute | solution.py:17
  86.5 1.3 gather_fusion.7
  87.8 0.4 broadcast_select_fusion
  88.3 0.4 convert.20
  89.4 1.0 fusion.22
  90.4 0.6 copy-done.10
  91.0 0.6 dynamic-slice
  92.3 62.7 %all-reduce.7.cloned.1.call-done = (bf16[16,9,2048]{2,0,1:T(8,128)(2,1)}, bf16[16,9,2048]{2,0,1:T(8,128)(2,1)}, bf16[16,9,2048]{2,0,1:T(8,128)(2,1)}, bf16[16,9,2048]{2,0,1:T(8,128)(2,1)}) async-done(((bf16[16,9,2048]{2,0,1:T(8,128)(2,1)}, bf16[16,9,2048]{2,0,1:T(8,128)(2,1)}, bf16[16,9,2048]{2,0,1:T(8,128)(2,1)}, bf16[16,9,2048]{2,0,1:T(8,128)(2,1)}), (bf16[16,9,2048]{2,0,1:T(8,128)(2,1)}, ...) | async-done | bytes 2359312
  155.0 1.0 dynamic-slice_bitcast_fusion
  156.1 1.0 dynamic-slice_bitcast_fusion.1
  157.1 1.0 dynamic-slice_bitcast_fusion.2
  158.2 1.0 dynamic-slice_bitcast_fusion.3
  159.2 0.5 pad_maximum_fusion
  160.1 155.9 %while.16 = (s32[]{:T(128)}, f32[72,4001]{1,0:T(8,128)S(1)}, bf16[72,2048]{1,0:T(8,128)(2,1)S(1)}, s32[]{:T(128)}, s32[]{:T(128)}, /*index=5*/s32[]{:T(128)}, s32[]{:T(128)}, s32[]{:T(128)}, s32[]{:T(128)}) while((s32[]{:T(128)}, f32[72,4001]{1,0:T(8,128)S(1)}, bf16[72,2048]{1,0:T(8,128)(2,1)S(1)}, s32[]{:T(128)}, s32[]{:T(128)}, ...), condition=%wide.region_14.16_spmd.clone, body=%wide.region_13.15_spmd.clone.sunk | while | flops 327606112 | bytes 4762291 | solution.py:85
  182.5 16.4 %convolution_add_fusion.4 = f32[72,4001]{1,0:T(8,128)} fusion(s32[4001]{0:T(1024)S(1)} %iota_add_fusion.4, s32[256]{0:T(256)S(1)} %iota_add_fusion.5, f32[72,4001]{1,0:T(8,128)S(1)} %get-tuple-element.234, pred[]{:T(512)S(6)} %compare.4, bf16[72,2048]{1,0:T(8,128)(2,1)S(1)} %get-tuple-element.244, s32[]{:T(128)S(6)} %select_n.129), kind=kOutput, calls=%fused_computation.15.clone.1 | convolution fusion | flops 163432832 | bytes 2386213 | tf_op jit(solution)/shard_map/while/body/eval_jaxpr/dot_general | solution.py:82
  198.9 16.9 %convolution_add_fusion.5 = f32[72,4001]{1,0:T(8,128)S(1)} fusion(f32[72,4001]{1,0:T(8,128)} %convolution_add_fusion.4, s32[4001]{0:T(1024)S(1)} %iota_add_fusion.4, s32[256]{0:T(256)S(1)} %iota_add_fusion.5, bf16[72,2048]{1,0:T(8,128)(2,1)S(1)} %get-tuple-element.244, s32[]{:T(128)S(6)} %select_n.130), kind=kOutput, calls=%fused_computation.14.clone.1 | convolution fusion | flops 164169024 | bytes 2358852 | tf_op jit(solution)/shard_map/while/body/eval_jaxpr/dot_general | solution.py:83
  215.9 16.4 %convolution_add_fusion.4 = f32[72,4001]{1,0:T(8,128)} fusion(s32[4001]{0:T(1024)S(1)} %iota_add_fusion.4, s32[256]{0:T(256)S(1)} %iota_add_fusion.5, f32[72,4001]{1,0:T(8,128)S(1)} %get-tuple-element.234, pred[]{:T(512)S(6)} %compare.4, bf16[72,2048]{1,0:T(8,128)(2,1)S(1)} %get-tuple-element.244, s32[]{:T(128)S(6)} %select_n.129), kind=kOutput, calls=%fused_computation.15.clone.1 | convolution fusion | flops 163432832 | bytes 2386213 | tf_op jit(solution)/shard_map/while/body/eval_jaxpr/dot_general | solution.py:82
  232.3 16.9 %convolution_add_fusion.5 = f32[72,4001]{1,0:T(8,128)S(1)} fusion(f32[72,4001]{1,0:T(8,128)} %convolution_add_fusion.4, s32[4001]{0:T(1024)S(1)} %iota_add_fusion.4, s32[256]{0:T(256)S(1)} %iota_add_fusion.5, bf16[72,2048]{1,0:T(8,128)(2,1)S(1)} %get-tuple-element.244, s32[]{:T(128)S(6)} %select_n.130), kind=kOutput, calls=%fused_computation.14.clone.1 | convolution fusion | flops 164169024 | bytes 2358852 | tf_op jit(solution)/shard_map/while/body/eval_jaxpr/dot_general | solution.py:83
  249.3 16.4 %convolution_add_fusion.4 = f32[72,4001]{1,0:T(8,128)} fusion(s32[4001]{0:T(1024)S(1)} %iota_add_fusion.4, s32[256]{0:T(256)S(1)} %iota_add_fusion.5, f32[72,4001]{1,0:T(8,128)S(1)} %get-tuple-element.234, pred[]{:T(512)S(6)} %compare.4, bf16[72,2048]{1,0:T(8,128)(2,1)S(1)} %get-tuple-element.244, s32[]{:T(128)S(6)} %select_n.129), kind=kOutput, calls=%fused_computation.15.clone.1 | convolution fusion | flops 163432832 | bytes 2386213 | tf_op jit(solution)/shard_map/while/body/eval_jaxpr/dot_general | solution.py:82
  265.7 16.9 %convolution_add_fusion.5 = f32[72,4001]{1,0:T(8,128)S(1)} fusion(f32[72,4001]{1,0:T(8,128)} %convolution_add_fusion.4, s32[4001]{0:T(1024)S(1)} %iota_add_fusion.4, s32[256]{0:T(256)S(1)} %iota_add_fusion.5, bf16[72,2048]{1,0:T(8,128)(2,1)S(1)} %get-tuple-element.244, s32[]{:T(128)S(6)} %select_n.130), kind=kOutput, calls=%fused_computation.14.clone.1 | convolution fusion | flops 164169024 | bytes 2358852 | tf_op jit(solution)/shard_map/while/body/eval_jaxpr/dot_general | solution.py:83
  282.7 16.4 %convolution_add_fusion.4 = f32[72,4001]{1,0:T(8,128)} fusion(s32[4001]{0:T(1024)S(1)} %iota_add_fusion.4, s32[256]{0:T(256)S(1)} %iota_add_fusion.5, f32[72,4001]{1,0:T(8,128)S(1)} %get-tuple-element.234, pred[]{:T(512)S(6)} %compare.4, bf16[72,2048]{1,0:T(8,128)(2,1)S(1)} %get-tuple-element.244, s32[]{:T(128)S(6)} %select_n.129), kind=kOutput, calls=%fused_computation.15.clone.1 | convolution fusion | flops 163432832 | bytes 2386213 | tf_op jit(solution)/shard_map/while/body/eval_jaxpr/dot_general | solution.py:82
  299.1 16.9 %convolution_add_fusion.5 = f32[72,4001]{1,0:T(8,128)S(1)} fusion(f32[72,4001]{1,0:T(8,128)} %convolution_add_fusion.4, s32[4001]{0:T(1024)S(1)} %iota_add_fusion.4, s32[256]{0:T(256)S(1)} %iota_add_fusion.5, bf16[72,2048]{1,0:T(8,128)(2,1)S(1)} %get-tuple-element.244, s32[]{:T(128)S(6)} %select_n.130), kind=kOutput, calls=%fused_computation.14.clone.1 | convolution fusion | flops 164169024 | bytes 2358852 | tf_op jit(solution)/shard_map/while/body/eval_jaxpr/dot_general | solution.py:83
  316.4 1.5 copy.117
  (73 shorter events, 4.8 us)
Async XLA Ops:
  6.5 148.5 %all-reduce.7.cloned.1.call-start = ((), (), s32[]{:S(2)}) async-start(), calls=%async_computation | async-start | bytes 4718592
  16.5 4.6 %copy-start.2 = (s32[1,4,2,16]{3,2,1,0:T(2,128)S(1)}, s32[1,4,2,16]{3,2,1,0:T(2,128)}, u32[]{:S(2)}) copy-start(s32[1,4,2,16]{3,2,1,0:T(2,128)} %param.8) | copy-start | bytes 1540
  19.2 22.0 %collective-permute-start = (bf16[2,32,6,1024]{3,0,2,1:T(2,128)(2,1)S(1)}, bf16[2,32,6,1024]{3,0,2,1:T(2,128)(2,1)}, u32[]{:S(2)}, u32[]{:S(2)}) collective-permute-start(bf16[2,32,6,1024]{3,0,2,1:T(2,128)(2,1)S(1)} %multiply_convert_fusion), channel_id=1, source_target_pairs={{0,1},{1,2},{2,3},{3,0},{4,5},{5,6},{6,7},{7,4},{8,9},{9,10},{10,1... | collective-permute-start | bytes 2359304 | tf_op jit(solution)/shard_map/ppermute | solution.py:17
  28.2 1.0 copy-start.1
  31.6 1.4 copy-start.5
  35.6 1.0 copy-start
  36.6 0.7 copy-start.9
  38.7 2.4 copy-start.4
  38.7 2.4 copy-start.3
  38.9 4.7 %copy-start.8 = (pred[16]{0:T(512)(128)(4,1)S(1)}, pred[16]{0:T(512)(128)(4,1)}, u32[]{:S(2)}) copy-start(pred[16]{0:T(512)(128)(4,1)} %get-tuple-element.187) | copy-start | bytes 52
  44.5 19.7 %collective-permute-start.1 = (bf16[2,32,6,1024]{3,0,2,1:T(2,128)(2,1)}, bf16[2,32,6,1024]{3,0,2,1:T(2,128)(2,1)}, u32[]{:S(2)}, u32[]{:S(2)}) collective-permute-start(bf16[2,32,6,1024]{3,0,2,1:T(2,128)(2,1)} %collective-permute-done), channel_id=1, source_target_pairs={{0,1},{1,2},{2,3},{3,0},{4,5},{5,6},{6,7},{7,4},{8,9},{9,10},{10,1... | collective-permute-start | bytes 2359304 | tf_op jit(solution)/shard_map/ppermute | solution.py:17
  47.2 19.5 %copy-start.7 = (pred[16]{0:T(512)(128)(4,1)S(1)}, pred[16]{0:T(512)(128)(4,1)}, u32[]{:S(2)}) copy-start(pred[16]{0:T(512)(128)(4,1)} %get-tuple-element.183) | copy-start | bytes 52
  67.6 18.9 %collective-permute-start.2 = (bf16[2,32,6,1024]{3,0,2,1:T(2,128)(2,1)}, bf16[2,32,6,1024]{3,0,2,1:T(2,128)(2,1)S(1)}, u32[]{:S(2)}, u32[]{:S(2)}) collective-permute-start(bf16[2,32,6,1024]{3,0,2,1:T(2,128)(2,1)} %collective-permute-done.1), channel_id=1, source_target_pairs={{0,1},{1,2},{2,3},{3,0},{4,5},{5,6},{6,7},{7,4},{8,9},{9,10},{10,1... | collective-permute-start | bytes 2359304 | tf_op jit(solution)/shard_map/ppermute | solution.py:17
  69.9 17.9 %copy-start.6 = (pred[16]{0:T(512)(128)(4,1)S(1)}, pred[16]{0:T(512)(128)(4,1)}, u32[]{:S(2)}) copy-start(pred[16]{0:T(512)(128)(4,1)} %get-tuple-element.193) | copy-start | bytes 52
  90.4 0.7 copy-start.10
Sparse Core Ops, SparseCore 0:
  90.5 64.4 all-reduce.6
where the time goes:
time: 331 us; the launch traced here: 325 us
  matrix products  133 us (40%)
  waiting for transfers between devices  94.4 us (29%)
  local copies, waits for them, and re-layouts  31.3 us (9%)
  other arithmetic  22.9 us (7%)
  loops' own time  22.6 us (7%)
  between operations  15.1 us (5%)
  starting transfers between devices  5.48 us (2%)
    dot_general x4, matrix products, add_block(): return total + jnp.dot(imag_rows, sine, preferred_element_type=jnp.float32)  67.7 us
    dot_general x4, matrix products, add_block(): jnp.dot(real_rows, cosine, preferred_element_type=jnp.float32)  65.6 us
    unnamed x2, waiting for transfers between devices  62.8 us
    ppermute x3, waiting for transfers between devices, from_behind(): return lax.ppermute(value, axis, pairs)  31.6 us
    another operation x1, loops' own time, per_device(): lax.fori_loop(0, NF // fblk, add_block, jnp.zeros((rows.shape[0], LAGS),...  22.6 us
    gather x4, local copies, waits for them, and re-layouts, reduce_tile(): jnp.take(visiting, second_idx, axis=1)  7.61 us
  transfers between devices with their start and end apart: 4, of which 3 were waited for; matrix products, arithmetic and copies ran while one was open for 7% of the time, Pallas kernels for 0%

commit v1 on v0

v1 whole, which is shorter than its diff:
```python
import math

import jax
import jax.numpy as jnp
import ml_dtypes
import numpy as np
from jax import lax
from jax.sharding import PartitionSpec as P

NF = 1024
NFFT = 8192
LAGS = 4001
BAND = 64


def shifted(value, axis, steps):
    count = lax.axis_size(axis)
    pairs = [(source, (source + steps) % count) for source in range(count)]
    return lax.ppermute(value, axis, pairs)


def make_table():
    freqs = np.arange(NF, dtype=np.int64)
    shifts = np.arange(LAGS, dtype=np.int64) - (LAGS - 1) // 2
    phase = np.mod(freqs[:, None] * shifts[None, :], NFFT)
    steps = np.arange(NFFT, dtype=np.float64) * (2.0 * math.pi / NFFT)
    cosine = np.cos(steps).astype(np.float32).astype(ml_dtypes.bfloat16)
    sine = (-np.sin(steps)).astype(np.float32).astype(ml_dtypes.bfloat16)
    return np.concatenate([cosine[phase], sine[phase]], axis=0)


def whiten(spectra):
    lead = spectra.shape[:-2]
    values = spectra.astype(jnp.float32).reshape(lead + (3, 2, NF // BAND, BAND))
    power = jnp.mean(values[..., 0, :, :] ** 2 + values[..., 1, :, :] ** 2, axis=-1)
    scaled = values * lax.rsqrt(power[..., None, :, None] + 1e-06)
    return scaled.reshape(lead + (6, NF)).astype(jnp.bfloat16)


def pick(white, idx):
    hot = (idx[:, None] == jnp.arange(white.shape[1], dtype=jnp.int32)[None, :]).astype(jnp.bfloat16)
    flat = white.reshape(white.shape[0], white.shape[1], -1)
    hot = jnp.broadcast_to(hot[None], (white.shape[0],) + hot.shape)
    out = jnp.einsum("hps,hsx->hpx", hot, flat, preferred_element_type=jnp.float32)
    return out.astype(jnp.bfloat16).reshape(white.shape[0], idx.shape[0], 6, -1)


def cross(own_rows, visit_rows):
    hours_n, slots, bins = (own_rows.shape[0], own_rows.shape[1], own_rows.shape[-1])
    first = own_rows.astype(jnp.float32).reshape(hours_n, slots, 3, 2, bins)
    second = visit_rows.astype(jnp.float32).reshape(hours_n, slots, 3, 2, bins)
    are, aim = (first[:, :, :, 0][:, :, :, None], first[:, :, :, 1][:, :, :, None])
    bre, bim = (second[:, :, :, 0][:, :, None], second[:, :, :, 1][:, :, None])
    real_part = jnp.sum(are * bre + aim * bim, axis=0).reshape(slots, 9, bins)
    imag_part = jnp.sum(are * bim - aim * bre, axis=0).reshape(slots, 9, bins)
    return jnp.concatenate([real_part, imag_part], axis=-1)


def per_device(table, spectra, pairs, counts):
    n_tm = lax.axis_size("tm")
    n_sta = lax.axis_size("sta")
    hours_dev = spectra.shape[0]
    p_tile = pairs.shape[3]
    owned = p_tile // n_tm
    asked = [pairs[0, 0, 1]] + [
        shifted(pairs[0, step, 1], "sta", -step) for step in range(1, n_sta)
    ]
    white = whiten(spectra)
    visits = [pick(white, asked[0])] + [
        shifted(pick(white, asked[step]), "sta", step) for step in range(1, n_sta)
    ]

    def reduce_tile(shift):
        limit = counts[0, shift]
        value = cross(pick(white, pairs[0, shift, 0]), visits[shift])
        slots = jnp.arange(p_tile, dtype=jnp.int32)
        value = jnp.where((slots < limit)[:, None, None], value, 0.0)
        return lax.psum_scatter(
            value.astype(jnp.bfloat16), "tm", scatter_dimension=0, tiled=True
        )

    reduced = [reduce_tile(shift) for shift in range(n_sta)]
    rows = jnp.stack(reduced, axis=0).reshape(n_sta * owned * 9, 2 * NF)
    lagged = jnp.dot(rows, table, preferred_element_type=jnp.float32)
    scale = 1.0 / math.sqrt(hours_dev * n_tm * NF)
    return (lagged * scale).astype(jnp.bfloat16).reshape(1, n_sta, owned, 9, LAGS)


def solution(mesh):
    mapped = jax.shard_map(
        per_device,
        mesh=mesh,
        in_specs=(
            P(None, None),
            P("tm", "sta", None, None),
            P("sta", None, None, None),
            P("sta", None),
        ),
        out_specs=P("sta", None, "tm", None, None),
        check_vma=False,
    )
    table = make_table()

    def run(spectra, pairs, counts):
        return mapped(jnp.asarray(table), spectra, pairs, counts)

    return run
```

time: 331 us -> 167 us (0.50); the launches traced: 325 us -> 165 us
  matrix products: 133 us -> 10.8 us
  loops' own time: 22.6 us -> 0 us
  other arithmetic: 22.9 us -> 14.5 us
  local copies, waits for them, and re-layouts: 31.3 us -> 25.9 us
    dot_general x8 -> x9, matrix products: 133 us -> 10.8 us  [the longest x1 8.82 us: per_device(): lagged = jnp.dot(rows, table, preferred_element_type=jnp.float32)]
    another operation x1 -> x0, loops' own time: 22.6 us -> none  [per_device(): lax.fori_loop(0, NF // fblk, add_block, jnp.zeros((rows.shape[0], LAGS),...]
    gather x8 -> x0, local copies, waits for them, and re-layouts: 13 us -> none  [the longest x4 7.61 us: reduce_tile(): jnp.take(visiting, second_idx, axis=1)]
    convert_element_type x7 -> x6, other arithmetic: 9 us -> 2.39 us  [pick(): (idx[:, None] == jnp.arange(white.shape[1], dtype=jnp.int32)[None, :]).as...]
    slice x0 -> x5, local copies, waits for them, and re-layouts: none -> 3.79 us  [the longest x4 3.18 us: cross(): first[:, :, :, 0][:, :, :, None]]
    lt x0 -> x4, other arithmetic: none -> 3.62 us  [reduce_tile(): value = jnp.where((slots < limit)[:, None, None], value, 0.0)]
    unnamed x23 -> x27, local copies, waits for them, and re-layouts: 2.08 us -> 5.4 us
    ppermute x3 -> x6, waiting for transfers between devices: 31.6 us -> 28.4 us  [shifted(): return lax.ppermute(value, axis, pairs)]
  transfers between devices with their start and end apart: 4 -> 7, of which waited for: 3 -> 3; matrix products, arithmetic and copies ran while one was open for 7% -> 17% of each run, Pallas kernels for 0% -> 0%
where the time goes in v1:
time: 167 us; the launch traced here: 165 us
  waiting for transfers between devices  91.2 us (55%)
  local copies, waits for them, and re-layouts  25.9 us (16%)
  other arithmetic  14.5 us (9%)
  between operations  14.4 us (9%)
  matrix products  10.8 us (6%)
  starting transfers between devices  8.23 us (5%)
    unnamed x2, waiting for transfers between devices  62.8 us
    ppermute x6, waiting for transfers between devices, shifted(): return lax.ppermute(value, axis, pairs)  28.4 us
    dot_general x1, matrix products, per_device(): lagged = jnp.dot(rows, table, preferred_element_type=jnp.float32)  8.82 us
    ppermute x6, starting transfers between devices, shifted(): return lax.ppermute(value, axis, pairs)  8.22 us
    unnamed x27, local copies, waits for them, and re-layouts  5.4 us
    another operation x5, local copies, waits for them, and re-layouts, per_device(): rows = jnp.stack(reduced, axis=0).reshape(n_sta * owned * 9, 2 * NF)  4.3 us
    convert_element_type x4, other arithmetic, reduce_tile(): value.astype(jnp.bfloat16)  3.99 us
    lt x4, other arithmetic, reduce_tile(): value = jnp.where((slots < limit)[:, None, None], value, 0.0)  3.62 us
  transfers between devices with their start and end apart: 7, of which 3 were waited for; matrix products, arithmetic and copies ran while one was open for 17% of the time, Pallas kernels for 0%

profile of v1, /device:TPU:8, one launch (start us, length us, event | category | flops | bytes accessed | tf_op | source)
XLA Modules:
  0.0 165.0 jit_solution(17220671912495701604)
XLA Ops:
  6.5 1.4 slice_bitcast_fusion.13
  7.9 1.6 collective-permute-start.4
  9.5 1.0 collective-permute-start.2
  10.5 2.0 %collective-permute-start = (s32[16]{0:T(128)}, s32[16]{0:T(128)}, u32[]{:S(2)}, u32[]{:S(2)}) collective-permute-start(s32[16]{0:T(128)} %get-tuple-element.36), channel_id=1, source_target_pairs={{0,3},{1,0},{2,1},{3,2},{4,7},{5,4},{6,5},{7,6},{8,11},{9,8},{10,9... | collective-permute-start | bytes 200 | tf_op jit(solution)/shard_map/ppermute | solution.py:19
  12.5 2.4 %reshape.298 = f32[2,32,3,2,16,64]{5,4,1,3,2,0:T(8,128)S(1)} reshape(bf16[2,32,6,1024]{3,1,2,0:T(8,128)(2,1)} %param.4) | data formatting | bytes 2359296 | tf_op jit(solution)/shard_map/reshape | solution.py:34
  14.9 0.5 fusion.7
  15.5 0.5 mul.107
  15.9 1.8 %mul.108 = f32[2,32,6,1024]{3,1,2,0:T(8,128)} reshape(f32[2,32,3,2,16,64]{5,4,1,3,2,0:T(8,128)S(1)} %mul.107) | data formatting | bytes 3145728 | tf_op jit(solution)/shard_map/mul | solution.py:36
  17.8 1.9 %fusion.12 = bf16[2,6,4,8,1024]{4,3,2,1,0:T(8,128)(2,1)S(1)} fusion(f32[2,32,6,1024]{3,1,2,0:T(8,128)} %mul.108, bf16[2,32,6,1024]{3,1,2,0:T(8,128)(2,1)} %param.4), kind=kLoop, calls=%fused_computation.36 | loop fusion | flops 1179648 | bytes 3145728
  19.8 0.2 fusion
  20.0 0.7 reshape.327
  20.7 1.4 fusion.33
  22.1 0.7 fusion.34
  22.7 1.1 iota_compare_fusion.8
  23.9 0.2 fusion.1
  24.1 0.7 reshape.324
  24.8 0.6 fusion.32
  25.4 0.8 copy.140
  26.2 0.8 copy.141
  27.1 0.6 iota_compare_fusion.9
  27.7 0.2 fusion.2
  28.0 0.7 reshape.321
  28.6 0.6 fusion.31
  29.3 0.8 copy.142
  30.1 1.1 iota_compare_fusion.10
  31.3 0.2 fusion.3
  31.5 0.7 reshape.320
  32.2 0.6 fusion.30
  32.8 0.8 copy.144
  33.7 0.2 fusion.4
  33.9 0.7 reshape.319
  34.6 0.6 fusion.29
  35.5 0.7 iota_compare_fusion.11
  36.4 0.3 add_reduce_fusion.3
  36.7 1.0 fusion.8
  37.8 0.7 fusion.20
  38.6 0.2 convolution_convert_fusion
  38.8 1.6 collective-permute-start.5
  40.4 0.7 fusion.18
  41.1 0.2 convolution_convert_fusion.2
  41.6 0.7 fusion.16
  42.3 0.2 convolution_convert_fusion.4
  42.6 1.8 %collective-permute-start.1 = (bf16[2,16,6,1024]{3,1,2,0:T(8,128)(2,1)S(1)}, bf16[2,16,6,1024]{3,1,2,0:T(8,128)(2,1)S(1)}, u32[]{:S(2)}, u32[]{:S(2)}) collective-permute-start(bf16[2,16,6,1024]{3,1,2,0:T(8,128)(2,1)S(1)} %bitcast.145), channel_id=1, source_target_pairs={{0,1},{1,2},{2,3},{3,0},{4,5},{5,6},{6,7},{7,4},{8,9},{9,10},{10,1... | collective-permute-start | bytes 1179656 | tf_op jit(solution)/shard_map/ppermute | solution.py:19
  44.5 23.5 %collective-permute-done.5 = bf16[2,16,6,1024]{3,1,2,0:T(8,128)(2,1)S(1)} collective-permute-done((bf16[2,16,6,1024]{3,1,2,0:T(8,128)(2,1)S(1)}, bf16[2,16,6,1024]{3,1,2,0:T(8,128)(2,1)S(1)}, u32[]{:S(2)}, u32[]{:S(2)}) %collective-permute-start.5) | collective-permute-done | bytes 393248 | tf_op jit(solution)/shard_map/ppermute | solution.py:19
  68.3 4.9 %collective-permute-done.1 = bf16[2,16,6,1024]{3,1,2,0:T(8,128)(2,1)S(1)} collective-permute-done((bf16[2,16,6,1024]{3,1,2,0:T(8,128)(2,1)S(1)}, bf16[2,16,6,1024]{3,1,2,0:T(8,128)(2,1)S(1)}, u32[]{:S(2)}, u32[]{:S(2)}) %collective-permute-start.1) | collective-permute-done | bytes 393248 | tf_op jit(solution)/shard_map/ppermute | solution.py:19
  73.4 0.3 add_reduce_fusion
  73.7 0.3 copy-done.6
  74.0 1.0 fusion.11
  75.0 0.3 add_reduce_fusion.1
  75.3 1.0 fusion.10
  76.3 0.3 add_reduce_fusion.2
  76.7 0.3 copy-done.7
  77.0 1.0 fusion.9
  78.0 0.6 copy-done.8
  78.6 0.6 dynamic-slice
  79.8 62.8 %all-reduce.7.cloned.1.call-done = (bf16[16,9,2048]{2,0,1:T(8,128)(2,1)}, bf16[16,9,2048]{2,0,1:T(8,128)(2,1)}, bf16[16,9,2048]{2,0,1:T(8,128)(2,1)}, bf16[16,9,2048]{2,0,1:T(8,128)(2,1)}) async-done(((bf16[16,9,2048]{2,0,1:T(8,128)(2,1)}, bf16[16,9,2048]{2,0,1:T(8,128)(2,1)}, bf16[16,9,2048]{2,0,1:T(8,128)(2,1)}, bf16[16,9,2048]{2,0,1:T(8,128)(2,1)}), (bf16[16,9,2048]{2,0,1:T(8,128)(2,1)}, ...) | async-done | bytes 2359312
  142.5 1.0 dynamic-slice_bitcast_fusion
  143.6 1.0 dynamic-slice_bitcast_fusion.1
  144.6 1.0 dynamic-slice_bitcast_fusion.2
  145.7 1.0 dynamic-slice_bitcast_fusion.3
  146.7 0.5 pad_maximum_fusion
  147.5 8.8 %fusion.5 = bf16[72,4001]{1,0:T(8,128)(2,1)S(1)} fusion(bf16[72,2048]{1,0:T(8,128)(2,1)S(1)} %reshape.317, bf16[2048,4001]{1,0:T(8,128)(2,1)} %constant.11.clone), kind=kOutput, calls=%fused_computation.14 | convolution fusion | flops 1180519168 | bytes 17259152 | tf_op jit(solution)/shard_map/dot_general | solution.py:84
  156.4 0.3 reshape.318
  156.7 1.5 copy.101
  (43 shorter events, 1.7 us)
Async XLA Ops:
  6.5 136.0 %all-reduce.7.cloned.1.call-start = ((), (), s32[]{:S(2)}) async-start(), calls=%async_computation | async-start | bytes 4718592
  7.9 29.9 %collective-permute-start.4 = (s32[16]{0:T(128)}, s32[16]{0:T(128)}, u32[]{:S(2)}, u32[]{:S(2)}) collective-permute-start(s32[16]{0:T(128)} %get-tuple-element.39), channel_id=1, source_target_pairs={{0,1},{1,2},{2,3},{3,0},{4,5},{5,6},{6,7},{7,4},{8,9},{9,10},{10,1... | collective-permute-start | bytes 200 | tf_op jit(solution)/shard_map/ppermute | solution.py:19
  9.5 30.9 %collective-permute-start.2 = (s32[16]{0:T(128)}, s32[16]{0:T(128)}, u32[]{:S(2)}, u32[]{:S(2)}) collective-permute-start(s32[16]{0:T(128)} %get-tuple-element.34), channel_id=1, source_target_pairs={{0,2},{1,3},{2,0},{3,1},{4,6},{5,7},{6,4},{7,5},{8,10},{9,11},{10,... | collective-permute-start | bytes 200 | tf_op jit(solution)/shard_map/ppermute | solution.py:19
  10.5 31.1 %collective-permute-start = (s32[16]{0:T(128)}, s32[16]{0:T(128)}, u32[]{:S(2)}, u32[]{:S(2)}) collective-permute-start(s32[16]{0:T(128)} %get-tuple-element.36), channel_id=1, source_target_pairs={{0,3},{1,0},{2,1},{3,2},{4,7},{5,4},{6,5},{7,6},{8,11},{9,8},{10,9... | collective-permute-start | bytes 200 | tf_op jit(solution)/shard_map/ppermute | solution.py:19
  20.7 1.4 copy-start.5
  35.2 1.0 copy-start
  35.4 1.0 copy-start.4
  38.8 29.1 %collective-permute-start.5 = (bf16[2,16,6,1024]{3,1,2,0:T(8,128)(2,1)S(1)}, bf16[2,16,6,1024]{3,1,2,0:T(8,128)(2,1)S(1)}, u32[]{:S(2)}, u32[]{:S(2)}) collective-permute-start(bf16[2,16,6,1024]{3,1,2,0:T(8,128)(2,1)S(1)} %bitcast.143), channel_id=1, source_target_pairs={{0,3},{1,0},{2,1},{3,2},{4,7},{5,4},{6,5},{7,6},{8,11},{9,8},{10,9... | collective-permute-start | bytes 1179656 | tf_op jit(solution)/shard_map/ppermute | solution.py:19
  41.4 26.7 %collective-permute-start.3 = (bf16[2,16,6,1024]{3,1,2,0:T(8,128)(2,1)S(1)}, bf16[2,16,6,1024]{3,1,2,0:T(8,128)(2,1)S(1)}, u32[]{:S(2)}, u32[]{:S(2)}) collective-permute-start(bf16[2,16,6,1024]{3,1,2,0:T(8,128)(2,1)S(1)} %bitcast.144), channel_id=1, source_target_pairs={{0,2},{1,3},{2,0},{3,1},{4,6},{5,7},{6,4},{7,5},{8,10},{9,11},{10,... | collective-permute-start | bytes 1179656 | tf_op jit(solution)/shard_map/ppermute | solution.py:19
  42.6 30.5 %collective-permute-start.1 = (bf16[2,16,6,1024]{3,1,2,0:T(8,128)(2,1)S(1)}, bf16[2,16,6,1024]{3,1,2,0:T(8,128)(2,1)S(1)}, u32[]{:S(2)}, u32[]{:S(2)}) collective-permute-start(bf16[2,16,6,1024]{3,1,2,0:T(8,128)(2,1)S(1)} %bitcast.145), channel_id=1, source_target_pairs={{0,1},{1,2},{2,3},{3,0},{4,5},{5,6},{6,7},{7,4},{8,9},{9,10},{10,1... | collective-permute-start | bytes 1179656 | tf_op jit(solution)/shard_map/ppermute | solution.py:19
  73.3 0.6 copy-start.6
  73.3 1.6 copy-start.1
  73.3 1.6 copy-start.2
  75.0 1.4 copy-start.3
  76.3 0.7 copy-start.7
  78.0 0.7 copy-start.8
Sparse Core Ops, SparseCore 0:
  78.1 64.3 all-reduce.6

commit v2 on v1

--- a/solution.py
+++ b/solution.py
@@ -47,13 +47,37 @@
 
 def cross(own_rows, visit_rows):
     hours_n, slots, bins = (own_rows.shape[0], own_rows.shape[1], own_rows.shape[-1])
-    first = own_rows.astype(jnp.float32).reshape(hours_n, slots, 3, 2, bins)
-    second = visit_rows.astype(jnp.float32).reshape(hours_n, slots, 3, 2, bins)
+    first = own_rows.astype(jnp.float32).reshape(hours_n, slots, 3, 2, bins // 128, 128)
+    second = visit_rows.astype(jnp.float32).reshape(hours_n, slots, 3, 2, bins // 128, 128)
     are, aim = (first[:, :, :, 0][:, :, :, None], first[:, :, :, 1][:, :, :, None])
     bre, bim = (second[:, :, :, 0][:, :, None], second[:, :, :, 1][:, :, None])
-    real_part = jnp.sum(are * bre + aim * bim, axis=0).reshape(slots, 9, bins)
-    imag_part = jnp.sum(are * bim - aim * bre, axis=0).reshape(slots, 9, bins)
-    return jnp.concatenate([real_part, imag_part], axis=-1)
+    real_part = jnp.sum(are * bre + aim * bim, axis=0).reshape(slots, 9, bins // 128, 128)
+    imag_part = jnp.sum(are * bim - aim * bre, axis=0).reshape(slots, 9, bins // 128, 128)
+    return jnp.concatenate([real_part, imag_part], axis=-2)
+
+
+def sum_at_owner(value, axis, turn):
+    count = lax.axis_size(axis)
+    if count & (count - 1):
+        return lax.psum_scatter(value, axis, scatter_dimension=0, tiled=True)
+    owned, tail = value.shape[0] // count, value.shape[1:]
+    bits = list(range(count.bit_length() - 1))
+    others = bits[1:]
+    if others:
+        cut = turn % len(others)
+        bits = bits[:1] + others[cut:] + others[:cut]
+    me = lax.axis_index(axis)
+    left = count.bit_length() - 1
+    value = value.reshape((2,) * left + (owned,) + tail)
+    for bit in bits:
+        mine = lax.rem(lax.div(me, jnp.int32(1 << bit)), jnp.int32(2))
+        dim = left - 1 - bit
+        keep = lax.dynamic_slice_in_dim(value, mine, 1, dim)
+        give = lax.dynamic_slice_in_dim(value, 1 - mine, 1, dim)
+        swap = [(source, source ^ (1 << bit)) for source in range(count)]
+        got = lax.ppermute(give.astype(jnp.bfloat16), axis, swap)
+        value = keep.astype(jnp.float32) + got.astype(jnp.float32)
+    return value.reshape((owned,) + tail)
 
 
 def per_device(table, spectra, pairs, counts):
@@ -74,13 +98,11 @@
         limit = counts[0, shift]
         value = cross(pick(white, pairs[0, shift, 0]), visits[shift])
         slots = jnp.arange(p_tile, dtype=jnp.int32)
-        value = jnp.where((slots < limit)[:, None, None], value, 0.0)
-        return lax.psum_scatter(
-            value.astype(jnp.bfloat16), "tm", scatter_dimension=0, tiled=True
-        )
+        value = jnp.where((slots < limit)[:, None, None, None], value, 0.0)
+        return sum_at_owner(value.astype(jnp.bfloat16), "tm", shift)
 
     reduced = [reduce_tile(shift) for shift in range(n_sta)]
-    rows = jnp.stack(reduced, axis=0).reshape(n_sta * owned * 9, 2 * NF)
+    rows = jnp.stack(reduced, axis=0).astype(jnp.bfloat16).reshape(n_sta * owned * 9, 2 * NF)
     lagged = jnp.dot(rows, table, preferred_element_type=jnp.float32)
     scale = 1.0 / math.sqrt(hours_dev * n_tm * NF)
     return (lagged * scale).astype(jnp.bfloat16).reshape(1, n_sta, owned, 9, LAGS)

time: 167 us -> 87.6 us (0.52)
  the two profiles are of different devices: /device:TPU:8 before, /device:TPU:0 now
where the time goes in v2:
time: 87.6 us; the launch traced here: 87.2 us
  waiting for transfers between devices  37.5 us (43%)
  starting transfers between devices  21.7 us (25%)
  local copies, waits for them, and re-layouts  12.9 us (15%)
  other arithmetic  9.46 us (11%)
  matrix products  5.09 us (6%)
    ppermute x6, waiting for transfers between devices, shifted(): return lax.ppermute(value, axis, pairs)  28.9 us
    ppermute x12, starting transfers between devices, sum_at_owner(): got = lax.ppermute(give.astype(jnp.bfloat16), axis, swap)  12.1 us
    ppermute x6, starting transfers between devices, shifted(): return lax.ppermute(value, axis, pairs)  9.55 us
    ppermute x12, waiting for transfers between devices, sum_at_owner(): got = lax.ppermute(give.astype(jnp.bfloat16), axis, swap)  8.55 us
    dot_general x1, matrix products, per_device(): lagged = jnp.dot(rows, table, preferred_element_type=jnp.float32)  3.1 us
    unnamed x20, local copies, waits for them, and re-layouts  2.69 us
    lt x4, other arithmetic, reduce_tile(): value = jnp.where((slots < limit)[:, None, None, None], value, 0.0)  2.52 us
    reshape x1, local copies, waits for them, and re-layouts, whiten(): spectra.astype(jnp.float32).reshape(lead + (3, 2, NF // BAND, BAND))  2.39 us
  transfers between devices with their start and end apart: 18, of which 7 were waited for; matrix products, arithmetic and copies ran while one was open for 23% of the time, Pallas kernels for 0%

profile of v2, /device:TPU:0, one launch (start us, length us, event | category | flops | bytes accessed | tf_op | source)
XLA Modules:
  0.0 87.2 jit_solution(5930080197754314886)
XLA Ops:
  0.0 0.8 slice_bitcast_fusion.23
  0.8 3.1 %collective-permute-start.13 = (s32[16]{0:T(128)S(1)}, s32[16]{0:T(128)S(1)}, u32[]{:S(2)}, u32[]{:S(2)}) collective-permute-start(s32[16]{0:T(128)S(1)} %get-tuple-element.35), channel_id=1, source_target_pairs={{0,1},{1,2},{2,3},{3,0},{4,5},{5,6},{6,7},{7,4},{8,9},{9,10},{10,1... | collective-permute-start | bytes 200 | tf_op jit(solution)/shard_map/ppermute | solution.py:19
  3.9 2.6 %collective-permute-start.8 = (s32[16]{0:T(128)S(1)}, s32[16]{0:T(128)S(1)}, u32[]{:S(2)}, u32[]{:S(2)}) collective-permute-start(s32[16]{0:T(128)S(1)} %get-tuple-element.30), channel_id=1, source_target_pairs={{0,2},{1,3},{2,0},{3,1},{4,6},{5,7},{6,4},{7,5},{8,10},{9,11},{10,... | collective-permute-start | bytes 200 | tf_op jit(solution)/shard_map/ppermute | solution.py:19
  6.4 1.3 %collective-permute-start.3 = (s32[16]{0:T(128)S(1)}, s32[16]{0:T(128)S(1)}, u32[]{:S(2)}, u32[]{:S(2)}) collective-permute-start(s32[16]{0:T(128)S(1)} %get-tuple-element.32), channel_id=1, source_target_pairs={{0,3},{1,0},{2,1},{3,2},{4,7},{5,4},{6,5},{7,6},{8,11},{9,8},{10,9... | collective-permute-start | bytes 200 | tf_op jit(solution)/shard_map/ppermute | solution.py:19
  7.8 2.4 %reshape.310 = f32[2,32,3,2,16,64]{5,4,1,3,2,0:T(8,128)S(1)} reshape(bf16[2,32,6,1024]{3,1,2,0:T(8,128)(2,1)} %param.4) | data formatting | bytes 2359296 | tf_op jit(solution)/shard_map/reshape | solution.py:34
  10.2 0.5 fusion.7
  10.7 0.5 mul.107
  11.2 1.8 %mul.108 = f32[2,32,6,1024]{3,1,2,0:T(8,128)} reshape(f32[2,32,3,2,16,64]{5,4,1,3,2,0:T(8,128)S(1)} %mul.107) | data formatting | bytes 3145728 | tf_op jit(solution)/shard_map/mul | solution.py:36
  13.0 1.9 %fusion.12 = bf16[2,6,4,8,1024]{4,3,2,1,0:T(8,128)(2,1)S(1)} fusion(f32[2,32,6,1024]{3,1,2,0:T(8,128)} %mul.108, bf16[2,32,6,1024]{3,1,2,0:T(8,128)(2,1)} %param.4), kind=kLoop, calls=%fused_computation.36 | loop fusion | flops 1179648 | bytes 3145728
  15.0 0.6 copy-done.1
  15.6 0.7 fusion.33
  16.3 0.2 fusion.3
  16.5 0.1 copy.44
  16.8 0.2 fusion.4
  17.0 0.1 copy.43
  17.2 0.7 broadcast_compare_fusion.3
  17.9 0.4 add_reduce_fusion.3
  18.3 0.2 fusion.8
  18.5 0.7 constant_dynamic-slice_fusion.3
  19.3 0.2 fusion
  19.5 0.1 copy.49
  19.7 0.8 slice_bitcast_fusion.3
  20.5 0.7 broadcast_compare_fusion
  21.2 0.2 fusion.1
  21.5 0.1 copy.47
  21.7 0.6 broadcast_compare_fusion.1
  22.3 0.2 fusion.2
  22.8 0.6 broadcast_compare_fusion.2
  23.5 0.3 convolution_convert_fusion
  23.8 0.5 collective-permute-start.14
  24.3 0.2 convolution_convert_fusion.2
  24.6 1.8 %collective-permute-start.9 = (bf16[2,16,6,1024]{3,1,2,0:T(8,128)(2,1)S(1)}, bf16[2,16,6,1024]{3,1,2,0:T(8,128)(2,1)S(1)}, u32[]{:S(2)}, u32[]{:S(2)}) collective-permute-start(bf16[2,16,6,1024]{3,1,2,0:T(8,128)(2,1)S(1)} %bitcast.185), channel_id=1, source_target_pairs={{0,2},{1,3},{2,0},{3,1},{4,6},{5,7},{6,4},{7,5},{8,10},{9,11},{10,... | collective-permute-start | bytes 1179656 | tf_op jit(solution)/shard_map/ppermute | solution.py:19
  26.4 0.2 convolution_convert_fusion.4
  26.7 0.3 collective-permute-start.4
  27.0 1.0 %convert_add_fusion.3 = f32[2,2,1,2,9,16,128]{6,5,4,3,2,1,0:T(8,128)S(1)} fusion(bf16[2,2,1,2,9,16,128]{6,5,4,3,2,1,0:T(8,128)(2,1)} %collective-permute-done, bf16[2,2,2,2,9,16,128]{6,5,4,3,2,1,0:T(8,128)(2,1)S(1)} %fusion.8, s32[]{:T(128)S(6)} %select_n.54), kind=kLoop, calls=%fused_computation.40 | loop fusion | flops 442368 | bytes 1179652 | tf_op jit(solution)/shard_map/add | solution.py:79
  28.1 1.7 %collective-permute-start.1 = (bf16[2,1,1,2,9,16,128]{6,5,4,3,2,1,0:T(8,128)(2,1)S(1)}, bf16[2,1,1,2,9,16,128]{6,5,4,3,2,1,0:T(8,128)(2,1)S(1)}, u32[]{:S(2)}, u32[]{:S(2)}) collective-permute-start(bf16[2,1,1,2,9,16,128]{6,5,4,3,2,1,0:T(8,128)(2,1)S(1)} %dynamic-slice_convert_fusion.3), channel_id=1, source_target_pairs={{0,8},{4,12},{8,0},{12,4},{16,24},{20,28},{24,16},{28,20},{1,9},{5... | collective-permute-start | bytes 442376 | tf_op jit(solution)/shard_map/ppermute | solution.py:78
  29.8 5.5 %collective-permute-done.14 = bf16[2,16,6,1024]{3,1,2,0:T(8,128)(2,1)S(1)} collective-permute-done((bf16[2,16,6,1024]{3,1,2,0:T(8,128)(2,1)S(1)}, bf16[2,16,6,1024]{3,1,2,0:T(8,128)(2,1)S(1)}, u32[]{:S(2)}, u32[]{:S(2)}) %collective-permute-start.14) | collective-permute-done | bytes 393248 | tf_op jit(solution)/shard_map/ppermute | solution.py:19
  35.4 0.1 copy.50
  35.6 0.9 %copy-done = f32[2,16,3,8,128]{4,3,2,1,0:T(8,128)S(1)} copy-done((f32[2,16,3,8,128]{4,3,2,1,0:T(8,128)S(1)}, f32[2,16,3,8,128]{4,3,2,1,0:T(8,128)}, u32[]{:S(2)}) %copy-start) | copy-done | bytes 393240
  36.6 0.4 add_reduce_fusion
  37.0 0.2 fusion.11
  37.3 23.4 %collective-permute-done.9 = bf16[2,16,6,1024]{3,1,2,0:T(8,128)(2,1)S(1)} collective-permute-done((bf16[2,16,6,1024]{3,1,2,0:T(8,128)(2,1)S(1)}, bf16[2,16,6,1024]{3,1,2,0:T(8,128)(2,1)S(1)}, u32[]{:S(2)}, u32[]{:S(2)}) %collective-permute-start.9) | collective-permute-done | bytes 393248 | tf_op jit(solution)/shard_map/ppermute | solution.py:19
  60.8 0.1 copy.48
  61.0 0.4 add_reduce_fusion.1
  61.5 0.2 fusion.10
  61.9 0.1 copy.46
  62.1 0.4 add_reduce_fusion.2
  62.5 0.2 fusion.9
  62.8 1.6 %collective-permute-start.2 = (bf16[1,1,1,2,9,16,128]{6,5,4,3,2,1,0:T(8,128)(2,1)S(1)}, bf16[1,1,1,2,9,16,128]{6,5,4,3,2,1,0:T(8,128)(2,1)S(1)}, u32[]{:S(2)}, u32[]{:S(2)}) collective-permute-start(bf16[1,1,1,2,9,16,128]{6,5,4,3,2,1,0:T(8,128)(2,1)S(1)} %dynamic-slice_convert_fusion.7), channel_id=1, source_target_pairs={{0,16},{4,20},{8,24},{12,28},{16,0},{20,4},{24,8},{28,12},{1,17},{... | collective-permute-start | bytes 221192 | tf_op jit(solution)/shard_map/ppermute | solution.py:78
  64.4 0.3 collective-permute-start.5
  64.7 2.8 %collective-permute-done.2 = bf16[1,1,1,2,9,16,128]{6,5,4,3,2,1,0:T(8,128)(2,1)S(1)} collective-permute-done((bf16[1,1,1,2,9,16,128]{6,5,4,3,2,1,0:T(8,128)(2,1)S(1)}, bf16[1,1,1,2,9,16,128]{6,5,4,3,2,1,0:T(8,128)(2,1)S(1)}, u32[]{:S(2)}, u32[]{:S(2)}) %collective-permute-start.2) | collective-permute-done | bytes 73760 | tf_op jit(solution)/shard_map/ppermute | solution.py:78
  67.7 1.6 %collective-permute-start.16 = (bf16[1,2,1,2,9,16,128]{6,5,4,3,2,1,0:T(8,128)(2,1)S(1)}, bf16[1,2,1,2,9,16,128]{6,5,4,3,2,1,0:T(8,128)(2,1)S(1)}, u32[]{:S(2)}, u32[]{:S(2)}) collective-permute-start(bf16[1,2,1,2,9,16,128]{6,5,4,3,2,1,0:T(8,128)(2,1)S(1)} %dynamic-slice_convert_fusion), channel_id=1, source_target_pairs={{0,16},{4,20},{8,24},{12,28},{16,0},{20,4},{24,8},{28,12},{1,17},{... | collective-permute-start | bytes 442376 | tf_op jit(solution)/shard_map/ppermute | solution.py:78
  69.4 1.6 %collective-permute-start.11 = (bf16[2,1,1,2,9,16,128]{6,5,4,3,2,1,0:T(8,128)(2,1)S(1)}, bf16[2,1,1,2,9,16,128]{6,5,4,3,2,1,0:T(8,128)(2,1)S(1)}, u32[]{:S(2)}, u32[]{:S(2)}) collective-permute-start(bf16[2,1,1,2,9,16,128]{6,5,4,3,2,1,0:T(8,128)(2,1)S(1)} %dynamic-slice_convert_fusion.1), channel_id=1, source_target_pairs={{0,8},{4,12},{8,0},{12,4},{16,24},{20,28},{24,16},{28,20},{1,9},{5... | collective-permute-start | bytes 442376 | tf_op jit(solution)/shard_map/ppermute | solution.py:78
  71.1 0.6 collective-permute-start.6
  71.6 1.9 %collective-permute-done.16 = bf16[1,2,1,2,9,16,128]{6,5,4,3,2,1,0:T(8,128)(2,1)S(1)} collective-permute-done((bf16[1,2,1,2,9,16,128]{6,5,4,3,2,1,0:T(8,128)(2,1)S(1)}, bf16[1,2,1,2,9,16,128]{6,5,4,3,2,1,0:T(8,128)(2,1)S(1)}, u32[]{:S(2)}, u32[]{:S(2)}) %collective-permute-start.16) | collective-permute-done | bytes 147488 | tf_op jit(solution)/shard_map/ppermute | solution.py:78
  73.6 2.5 %collective-permute-start.17 = (bf16[1,1,1,2,9,16,128]{6,5,4,3,2,1,0:T(8,128)(2,1)S(1)}, bf16[1,1,1,2,9,16,128]{6,5,4,3,2,1,0:T(8,128)(2,1)S(1)}, u32[]{:S(2)}, u32[]{:S(2)}) collective-permute-start(bf16[1,1,1,2,9,16,128]{6,5,4,3,2,1,0:T(8,128)(2,1)S(1)} %dynamic-slice_convert_fusion.4), channel_id=1, source_target_pairs={{0,8},{4,12},{8,0},{12,4},{16,24},{20,28},{24,16},{28,20},{1,9},{5... | collective-permute-start | bytes 221192 | tf_op jit(solution)/shard_map/ppermute | solution.py:78
  76.2 1.6 %collective-permute-start.12 = (bf16[1,1,1,2,9,16,128]{6,5,4,3,2,1,0:T(8,128)(2,1)S(1)}, bf16[1,1,1,2,9,16,128]{6,5,4,3,2,1,0:T(8,128)(2,1)S(1)}, u32[]{:S(2)}, u32[]{:S(2)}) collective-permute-start(bf16[1,1,1,2,9,16,128]{6,5,4,3,2,1,0:T(8,128)(2,1)S(1)} %dynamic-slice_convert_fusion.5), channel_id=1, source_target_pairs={{0,16},{4,20},{8,24},{12,28},{16,0},{20,4},{24,8},{28,12},{1,17},{... | collective-permute-start | bytes 221192 | tf_op jit(solution)/shard_map/ppermute | solution.py:78
  77.8 0.6 collective-permute-start.7
  78.4 0.8 collective-permute-done.17
  79.2 1.3 %collective-permute-done.12 = bf16[1,1,1,2,9,16,128]{6,5,4,3,2,1,0:T(8,128)(2,1)S(1)} collective-permute-done((bf16[1,1,1,2,9,16,128]{6,5,4,3,2,1,0:T(8,128)(2,1)S(1)}, bf16[1,1,1,2,9,16,128]{6,5,4,3,2,1,0:T(8,128)(2,1)S(1)}, u32[]{:S(2)}, u32[]{:S(2)}) %collective-permute-start.12) | collective-permute-done | bytes 73760 | tf_op jit(solution)/shard_map/ppermute | solution.py:78
  80.6 1.6 %collective-permute-done.7 = bf16[1,1,1,2,9,16,128]{6,5,4,3,2,1,0:T(8,128)(2,1)S(1)} collective-permute-done((bf16[1,1,1,2,9,16,128]{6,5,4,3,2,1,0:T(8,128)(2,1)S(1)}, bf16[1,1,1,2,9,16,128]{6,5,4,3,2,1,0:T(8,128)(2,1)S(1)}, u32[]{:S(2)}, u32[]{:S(2)}) %collective-permute-start.7) | collective-permute-done | bytes 73760 | tf_op jit(solution)/shard_map/ppermute | solution.py:78
  82.4 3.1 %fusion.5 = bf16[72,4001]{1,0:T(8,128)(2,1)S(1)} fusion(bf16[2048,4001]{1,0:T(8,128)(2,1)S(1)} %bitcast.155, bf16[9,8,16,128]{3,2,1,0:T(8,128)(2,1)S(1)} %bitcast.172), kind=kOutput, calls=%fused_computation.14 | convolution fusion | flops 1180519168 | bytes 17259152 | tf_op jit(solution)/shard_map/dot_general | solution.py:106
  85.5 0.3 reshape.321
  85.8 1.5 %copy.38 = bf16[1,4,2,9,4001]{4,2,3,1,0:T(2,128)(2,1)} copy(bf16[1,4,2,9,4001]{4,3,2,1,0:T(8,128)(2,1)S(1)} %reshape.321) | data formatting | bytes 1152288 | tf_op jit(solution)/shard_map/reshape | solution.py:108
  (70 shorter events, 2.3 us)
Async XLA Ops:
  0.8 22.6 %collective-permute-start.13 = (s32[16]{0:T(128)S(1)}, s32[16]{0:T(128)S(1)}, u32[]{:S(2)}, u32[]{:S(2)}) collective-permute-start(s32[16]{0:T(128)S(1)} %get-tuple-element.35), channel_id=1, source_target_pairs={{0,1},{1,2},{2,3},{3,0},{4,5},{5,6},{6,7},{7,4},{8,9},{9,10},{10,1... | collective-permute-start | bytes 200 | tf_op jit(solution)/shard_map/ppermute | solution.py:19
  3.9 20.4 %collective-permute-start.8 = (s32[16]{0:T(128)S(1)}, s32[16]{0:T(128)S(1)}, u32[]{:S(2)}, u32[]{:S(2)}) collective-permute-start(s32[16]{0:T(128)S(1)} %get-tuple-element.30), channel_id=1, source_target_pairs={{0,2},{1,3},{2,0},{3,1},{4,6},{5,7},{6,4},{7,5},{8,10},{9,11},{10,... | collective-permute-start | bytes 200 | tf_op jit(solution)/shard_map/ppermute | solution.py:19
  6.4 19.9 %collective-permute-start.3 = (s32[16]{0:T(128)S(1)}, s32[16]{0:T(128)S(1)}, u32[]{:S(2)}, u32[]{:S(2)}) collective-permute-start(s32[16]{0:T(128)S(1)} %get-tuple-element.32), channel_id=1, source_target_pairs={{0,3},{1,0},{2,1},{3,2},{4,7},{5,4},{6,5},{7,6},{8,11},{9,8},{10,9... | collective-permute-start | bytes 200 | tf_op jit(solution)/shard_map/ppermute | solution.py:19
  14.9 0.7 copy-start.1
  19.2 7.8 %collective-permute-start = (bf16[2,2,1,2,9,16,128]{6,5,4,3,2,1,0:T(8,128)(2,1)}, bf16[2,2,1,2,9,16,128]{6,5,4,3,2,1,0:T(8,128)(2,1)}, u32[]{:S(2)}, u32[]{:S(2)}) collective-permute-start(bf16[2,2,1,2,9,16,128]{6,5,4,3,2,1,0:T(8,128)(2,1)} %constant_dynamic-slice_fusion.3), channel_id=1, source_target_pairs={{0,4},{4,0},{8,12},{12,8},{16,20},{20,16},{24,28},{28,24},{1,5},{5... | collective-permute-start | bytes 884744 | tf_op jit(solution)/shard_map/ppermute | solution.py:78
  23.8 11.6 %collective-permute-start.14 = (bf16[2,16,6,1024]{3,1,2,0:T(8,128)(2,1)S(1)}, bf16[2,16,6,1024]{3,1,2,0:T(8,128)(2,1)S(1)}, u32[]{:S(2)}, u32[]{:S(2)}) collective-permute-start(bf16[2,16,6,1024]{3,1,2,0:T(8,128)(2,1)S(1)} %bitcast.186), channel_id=1, source_target_pairs={{0,3},{1,0},{2,1},{3,2},{4,7},{5,4},{6,5},{7,6},{8,11},{9,8},{10,9... | collective-permute-start | bytes 1179656 | tf_op jit(solution)/shard_map/ppermute | solution.py:19
  24.6 36.1 %collective-permute-start.9 = (bf16[2,16,6,1024]{3,1,2,0:T(8,128)(2,1)S(1)}, bf16[2,16,6,1024]{3,1,2,0:T(8,128)(2,1)S(1)}, u32[]{:S(2)}, u32[]{:S(2)}) collective-permute-start(bf16[2,16,6,1024]{3,1,2,0:T(8,128)(2,1)S(1)} %bitcast.185), channel_id=1, source_target_pairs={{0,2},{1,3},{2,0},{3,1},{4,6},{5,7},{6,4},{7,5},{8,10},{9,11},{10,... | collective-permute-start | bytes 1179656 | tf_op jit(solution)/shard_map/ppermute | solution.py:19
  26.7 35.0 %collective-permute-start.4 = (bf16[2,16,6,1024]{3,1,2,0:T(8,128)(2,1)S(1)}, bf16[2,16,6,1024]{3,1,2,0:T(8,128)(2,1)S(1)}, u32[]{:S(2)}, u32[]{:S(2)}) collective-permute-start(bf16[2,16,6,1024]{3,1,2,0:T(8,128)(2,1)S(1)} %bitcast.184), channel_id=1, source_target_pairs={{0,1},{1,2},{2,3},{3,0},{4,5},{5,6},{6,7},{7,4},{8,9},{9,10},{10,1... | collective-permute-start | bytes 1179656 | tf_op jit(solution)/shard_map/ppermute | solution.py:19
  28.1 34.6 %collective-permute-start.1 = (bf16[2,1,1,2,9,16,128]{6,5,4,3,2,1,0:T(8,128)(2,1)S(1)}, bf16[2,1,1,2,9,16,128]{6,5,4,3,2,1,0:T(8,128)(2,1)S(1)}, u32[]{:S(2)}, u32[]{:S(2)}) collective-permute-start(bf16[2,1,1,2,9,16,128]{6,5,4,3,2,1,0:T(8,128)(2,1)S(1)} %dynamic-slice_convert_fusion.3), channel_id=1, source_target_pairs={{0,8},{4,12},{8,0},{12,4},{16,24},{20,28},{24,16},{28,20},{1,9},{5... | collective-permute-start | bytes 442376 | tf_op jit(solution)/shard_map/ppermute | solution.py:78
  35.6 1.0 %copy-start = (f32[2,16,3,8,128]{4,3,2,1,0:T(8,128)S(1)}, f32[2,16,3,8,128]{4,3,2,1,0:T(8,128)}, u32[]{:S(2)}) copy-start(f32[2,16,3,8,128]{4,3,2,1,0:T(8,128)} %get-tuple-element.26) | copy-start | bytes 1179652
  36.6 45.8 %slice-start = ((s8[16777216]{0:T(1024)(128)(4,1)}), s8[4194304]{0:T(1024)(128)(4,1)S(1)}, s32[]{:S(2)}) async-start(s8[16777216]{0:T(1024)(128)(4,1)} %bitcast.154), calls=%async_computation | async-start | bytes 8388608
  37.2 30.3 %collective-permute-start.15 = (bf16[2,2,1,2,9,16,128]{6,5,4,3,2,1,0:T(8,128)(2,1)S(1)}, bf16[2,2,1,2,9,16,128]{6,5,4,3,2,1,0:T(8,128)(2,1)S(1)}, u32[]{:S(2)}, u32[]{:S(2)}) collective-permute-start(bf16[2,2,1,2,9,16,128]{6,5,4,3,2,1,0:T(8,128)(2,1)S(1)} %constant_dynamic-slice_fusion), channel_id=1, source_target_pairs={{0,4},{4,0},{8,12},{12,8},{16,20},{20,16},{24,28},{28,24},{1,5},{5... | collective-permute-start | bytes 884744 | tf_op jit(solution)/shard_map/ppermute | solution.py:78
  60.9 21.4 %slice-start.1 = ((s8[16777216]{0:T(1024)(128)(4,1)}), s8[4194304]{0:T(1024)(128)(4,1)S(1)}, s32[]{:S(2)}) async-start(s8[16777216]{0:T(1024)(128)(4,1)} %bitcast.154), calls=%async_computation.1 | async-start | bytes 8388608
  61.7 7.6 %collective-permute-start.10 = (bf16[2,2,1,2,9,16,128]{6,5,4,3,2,1,0:T(8,128)(2,1)S(1)}, bf16[2,2,1,2,9,16,128]{6,5,4,3,2,1,0:T(8,128)(2,1)S(1)}, u32[]{:S(2)}, u32[]{:S(2)}) collective-permute-start(bf16[2,2,1,2,9,16,128]{6,5,4,3,2,1,0:T(8,128)(2,1)S(1)} %constant_dynamic-slice_fusion.1), channel_id=1, source_target_pairs={{0,4},{4,0},{8,12},{12,8},{16,20},{20,16},{24,28},{28,24},{1,5},{5... | collective-permute-start | bytes 884744 | tf_op jit(solution)/shard_map/ppermute | solution.py:78
  62.0 20.3 %slice-start.2 = ((s8[16777216]{0:T(1024)(128)(4,1)}), s8[4194304]{0:T(1024)(128)(4,1)S(1)}, s32[]{:S(2)}) async-start(s8[16777216]{0:T(1024)(128)(4,1)} %bitcast.154), calls=%async_computation.2 | async-start | bytes 8388608
  62.8 4.7 %collective-permute-start.2 = (bf16[1,1,1,2,9,16,128]{6,5,4,3,2,1,0:T(8,128)(2,1)S(1)}, bf16[1,1,1,2,9,16,128]{6,5,4,3,2,1,0:T(8,128)(2,1)S(1)}, u32[]{:S(2)}, u32[]{:S(2)}) collective-permute-start(bf16[1,1,1,2,9,16,128]{6,5,4,3,2,1,0:T(8,128)(2,1)S(1)} %dynamic-slice_convert_fusion.7), channel_id=1, source_target_pairs={{0,16},{4,20},{8,24},{12,28},{16,0},{20,4},{24,8},{28,12},{1,17},{... | collective-permute-start | bytes 221192 | tf_op jit(solution)/shard_map/ppermute | solution.py:78
  64.4 6.5 %collective-permute-start.5 = (bf16[2,2,1,2,9,16,128]{6,5,4,3,2,1,0:T(8,128)(2,1)S(1)}, bf16[2,2,1,2,9,16,128]{6,5,4,3,2,1,0:T(8,128)(2,1)S(1)}, u32[]{:S(2)}, u32[]{:S(2)}) collective-permute-start(bf16[2,2,1,2,9,16,128]{6,5,4,3,2,1,0:T(8,128)(2,1)S(1)} %constant_dynamic-slice_fusion.2), channel_id=1, source_target_pairs={{0,4},{4,0},{8,12},{12,8},{16,20},{20,16},{24,28},{28,24},{1,5},{5... | collective-permute-start | bytes 884744 | tf_op jit(solution)/shard_map/ppermute | solution.py:78
  67.5 14.8 %slice-start.3 = ((s8[16777216]{0:T(1024)(128)(4,1)}), s8[4194304]{0:T(1024)(128)(4,1)S(1)}, s32[]{:S(2)}) async-start(s8[16777216]{0:T(1024)(128)(4,1)} %bitcast.154), calls=%async_computation.3 | async-start | bytes 8388608
  67.7 5.9 %collective-permute-start.16 = (bf16[1,2,1,2,9,16,128]{6,5,4,3,2,1,0:T(8,128)(2,1)S(1)}, bf16[1,2,1,2,9,16,128]{6,5,4,3,2,1,0:T(8,128)(2,1)S(1)}, u32[]{:S(2)}, u32[]{:S(2)}) collective-permute-start(bf16[1,2,1,2,9,16,128]{6,5,4,3,2,1,0:T(8,128)(2,1)S(1)} %dynamic-slice_convert_fusion), channel_id=1, source_target_pairs={{0,16},{4,20},{8,24},{12,28},{16,0},{20,4},{24,8},{28,12},{1,17},{... | collective-permute-start | bytes 442376 | tf_op jit(solution)/shard_map/ppermute | solution.py:78
  69.4 6.7 %collective-permute-start.11 = (bf16[2,1,1,2,9,16,128]{6,5,4,3,2,1,0:T(8,128)(2,1)S(1)}, bf16[2,1,1,2,9,16,128]{6,5,4,3,2,1,0:T(8,128)(2,1)S(1)}, u32[]{:S(2)}, u32[]{:S(2)}) collective-permute-start(bf16[2,1,1,2,9,16,128]{6,5,4,3,2,1,0:T(8,128)(2,1)S(1)} %dynamic-slice_convert_fusion.1), channel_id=1, source_target_pairs={{0,8},{4,12},{8,0},{12,4},{16,24},{20,28},{24,16},{28,20},{1,9},{5... | collective-permute-start | bytes 442376 | tf_op jit(solution)/shard_map/ppermute | solution.py:78
  71.1 6.7 %collective-permute-start.6 = (bf16[1,2,1,2,9,16,128]{6,5,4,3,2,1,0:T(8,128)(2,1)S(1)}, bf16[1,2,1,2,9,16,128]{6,5,4,3,2,1,0:T(8,128)(2,1)S(1)}, u32[]{:S(2)}, u32[]{:S(2)}) collective-permute-start(bf16[1,2,1,2,9,16,128]{6,5,4,3,2,1,0:T(8,128)(2,1)S(1)} %dynamic-slice_convert_fusion.2), channel_id=1, source_target_pairs={{0,16},{4,20},{8,24},{12,28},{16,0},{20,4},{24,8},{28,12},{1,17},{... | collective-permute-start | bytes 442376 | tf_op jit(solution)/shard_map/ppermute | solution.py:78
  73.6 5.6 %collective-permute-start.17 = (bf16[1,1,1,2,9,16,128]{6,5,4,3,2,1,0:T(8,128)(2,1)S(1)}, bf16[1,1,1,2,9,16,128]{6,5,4,3,2,1,0:T(8,128)(2,1)S(1)}, u32[]{:S(2)}, u32[]{:S(2)}) collective-permute-start(bf16[1,1,1,2,9,16,128]{6,5,4,3,2,1,0:T(8,128)(2,1)S(1)} %dynamic-slice_convert_fusion.4), channel_id=1, source_target_pairs={{0,8},{4,12},{8,0},{12,4},{16,24},{20,28},{24,16},{28,20},{1,9},{5... | collective-permute-start | bytes 221192 | tf_op jit(solution)/shard_map/ppermute | solution.py:78
  76.2 4.4 %collective-permute-start.12 = (bf16[1,1,1,2,9,16,128]{6,5,4,3,2,1,0:T(8,128)(2,1)S(1)}, bf16[1,1,1,2,9,16,128]{6,5,4,3,2,1,0:T(8,128)(2,1)S(1)}, u32[]{:S(2)}, u32[]{:S(2)}) collective-permute-start(bf16[1,1,1,2,9,16,128]{6,5,4,3,2,1,0:T(8,128)(2,1)S(1)} %dynamic-slice_convert_fusion.5), channel_id=1, source_target_pairs={{0,16},{4,20},{8,24},{12,28},{16,0},{20,4},{24,8},{28,12},{1,17},{... | collective-permute-start | bytes 221192 | tf_op jit(solution)/shard_map/ppermute | solution.py:78
  77.8 4.4 %collective-permute-start.7 = (bf16[1,1,1,2,9,16,128]{6,5,4,3,2,1,0:T(8,128)(2,1)S(1)}, bf16[1,1,1,2,9,16,128]{6,5,4,3,2,1,0:T(8,128)(2,1)S(1)}, u32[]{:S(2)}, u32[]{:S(2)}) collective-permute-start(bf16[1,1,1,2,9,16,128]{6,5,4,3,2,1,0:T(8,128)(2,1)S(1)} %dynamic-slice_convert_fusion.6), channel_id=1, source_target_pairs={{0,8},{4,12},{8,0},{12,4},{16,24},{20,28},{24,16},{28,20},{1,9},{5... | collective-permute-start | bytes 221192 | tf_op jit(solution)/shard_map/ppermute | solution.py:78

commit v3 on v2

--- a/solution.py
+++ b/solution.py
@@ -30,11 +30,17 @@
 
 
 def whiten(spectra):
-    lead = spectra.shape[:-2]
-    values = spectra.astype(jnp.float32).reshape(lead + (3, 2, NF // BAND, BAND))
-    power = jnp.mean(values[..., 0, :, :] ** 2 + values[..., 1, :, :] ** 2, axis=-1)
-    scaled = values * lax.rsqrt(power[..., None, :, None] + 1e-06)
-    return scaled.reshape(lead + (6, NF)).astype(jnp.bfloat16)
+    lanes = spectra.shape[-1]
+    per_row = lanes // BAND
+    values = spectra.astype(jnp.float32).reshape(spectra.shape[:2] + (3, 2) + spectra.shape[3:])
+    square = values[:, :, :, 0] ** 2 + values[:, :, :, 1] ** 2
+    band = jnp.arange(lanes, dtype=jnp.int32) // BAND
+    inverse = jnp.zeros_like(square)
+    for index in range(per_row):
+        inside = band == index
+        power = jnp.sum(jnp.where(inside, square, 0.0), axis=-1, keepdims=True) * (1.0 / BAND)
+        inverse = jnp.where(inside, lax.rsqrt(power + 1e-06), inverse)
+    return (values * inverse[:, :, :, None]).astype(jnp.bfloat16)
 
 
 def pick(white, idx):
@@ -42,17 +48,16 @@
     flat = white.reshape(white.shape[0], white.shape[1], -1)
     hot = jnp.broadcast_to(hot[None], (white.shape[0],) + hot.shape)
     out = jnp.einsum("hps,hsx->hpx", hot, flat, preferred_element_type=jnp.float32)
-    return out.astype(jnp.bfloat16).reshape(white.shape[0], idx.shape[0], 6, -1)
+    return out.astype(jnp.bfloat16).reshape(white.shape[0], idx.shape[0], 6, -1, 128)
 
 
 def cross(own_rows, visit_rows):
-    hours_n, slots, bins = (own_rows.shape[0], own_rows.shape[1], own_rows.shape[-1])
-    first = own_rows.astype(jnp.float32).reshape(hours_n, slots, 3, 2, bins // 128, 128)
-    second = visit_rows.astype(jnp.float32).reshape(hours_n, slots, 3, 2, bins // 128, 128)
+    slots, tiles = (own_rows.shape[1], own_rows.shape[-2:])
+    first, second = (own_rows.astype(jnp.float32), visit_rows.astype(jnp.float32))
     are, aim = (first[:, :, :, 0][:, :, :, None], first[:, :, :, 1][:, :, :, None])
     bre, bim = (second[:, :, :, 0][:, :, None], second[:, :, :, 1][:, :, None])
-    real_part = jnp.sum(are * bre + aim * bim, axis=0).reshape(slots, 9, bins // 128, 128)
-    imag_part = jnp.sum(are * bim - aim * bre, axis=0).reshape(slots, 9, bins // 128, 128)
+    real_part = jnp.sum(are * bre + aim * bim, axis=0).reshape((slots, 9) + tiles)
+    imag_part = jnp.sum(are * bim - aim * bre, axis=0).reshape((slots, 9) + tiles)
     return jnp.concatenate([real_part, imag_part], axis=-2)
 
 
@@ -89,14 +94,13 @@
     asked = [pairs[0, 0, 1]] + [
         shifted(pairs[0, step, 1], "sta", -step) for step in range(1, n_sta)
     ]
-    white = whiten(spectra)
-    visits = [pick(white, asked[0])] + [
-        shifted(pick(white, asked[step]), "sta", step) for step in range(1, n_sta)
+    visits = [pick(spectra, asked[0])] + [
+        shifted(pick(spectra, asked[step]), "sta", step) for step in range(1, n_sta)
     ]
 
     def reduce_tile(shift):
         limit = counts[0, shift]
-        value = cross(pick(white, pairs[0, shift, 0]), visits[shift])
+        value = cross(whiten(pick(spectra, pairs[0, shift, 0])), whiten(visits[shift]))
         slots = jnp.arange(p_tile, dtype=jnp.int32)
         value = jnp.where((slots < limit)[:, None, None, None], value, 0.0)
         return sum_at_owner(value.astype(jnp.bfloat16), "tm", shift)

time: 87.6 us -> 155 us (1.77)
  the two profiles are of different devices: /device:TPU:0 before, /device:TPU:8 now
where the time goes in v3:
time: 155 us; the launch traced here: 152 us
  local copies, waits for them, and re-layouts  57.3 us (37%)
  waiting for transfers between devices  34.7 us (22%)
  other arithmetic  34.3 us (22%)
  starting transfers between devices  20 us (13%)
  matrix products  5.07 us (3%)
    ppermute x6, waiting for transfers between devices, shifted(): return lax.ppermute(value, axis, pairs)  29.3 us
    reduce_sum x16, local copies, waits for them, and re-layouts, whiten(): jnp.sum(jnp.where(inside, square, 0.0), axis=-1, keepdims=True)  24.2 us
    rsqrt x16, local copies, waits for them, and re-layouts, whiten(): inverse = jnp.where(inside, lax.rsqrt(power + 1e-06), inverse)  23 us
    rsqrt x16, other arithmetic, whiten(): inverse = jnp.where(inside, lax.rsqrt(power + 1e-06), inverse)  21.5 us
    ppermute x12, starting transfers between devices, sum_at_owner(): got = lax.ppermute(give.astype(jnp.bfloat16), axis, swap)  11.4 us
    ppermute x6, starting transfers between devices, shifted(): return lax.ppermute(value, axis, pairs)  8.61 us
    ppermute x12, waiting for transfers between devices, sum_at_owner(): got = lax.ppermute(give.astype(jnp.bfloat16), axis, swap)  5.37 us
    unnamed x36, local copies, waits for them, and re-layouts  4.96 us
  transfers between devices with their start and end apart: 18, of which 9 were waited for; matrix products, arithmetic and copies ran while one was open for 9% of the time, Pallas kernels for 0%

profile of v3, /device:TPU:8, one launch (start us, length us, event | category | flops | bytes accessed | tf_op | source)
XLA Modules:
  0.0 152.1 jit_solution(17350213974112771367)
XLA Ops:
  0.8 3.0 %collective-permute-start.8 = (s32[16]{0:T(128)S(1)}, s32[16]{0:T(128)S(1)}, u32[]{:S(2)}, u32[]{:S(2)}) collective-permute-start(s32[16]{0:T(128)S(1)} %get-tuple-element.57), channel_id=1, source_target_pairs={{0,2},{1,3},{2,0},{3,1},{4,6},{5,7},{6,4},{7,5},{8,10},{9,11},{10,... | collective-permute-start | bytes 200 | tf_op jit(solution)/shard_map/ppermute | solution.py:19
  3.9 2.5 %collective-permute-start.13 = (s32[16]{0:T(128)S(1)}, s32[16]{0:T(128)S(1)}, u32[]{:S(2)}, u32[]{:S(2)}) collective-permute-start(s32[16]{0:T(128)S(1)} %get-tuple-element.63), channel_id=1, source_target_pairs={{0,1},{1,2},{2,3},{3,0},{4,5},{5,6},{6,7},{7,4},{8,9},{9,10},{10,1... | collective-permute-start | bytes 200 | tf_op jit(solution)/shard_map/ppermute | solution.py:19
  14.2 2.0 %collective-permute-start.9 = (bf16[2,16,6,8,128]{4,3,2,1,0:T(8,128)(2,1)S(1)}, bf16[2,16,6,8,128]{4,3,2,1,0:T(8,128)(2,1)S(1)}, u32[]{:S(2)}, u32[]{:S(2)}) collective-permute-start(bf16[2,16,6,8,128]{4,3,2,1,0:T(8,128)(2,1)S(1)} %bitcast.369), channel_id=1, source_target_pairs={{0,2},{1,3},{2,0},{3,1},{4,6},{5,7},{6,4},{7,5},{8,10},{9,11},{10,... | collective-permute-start | bytes 1179656 | tf_op jit(solution)/shard_map/ppermute | solution.py:19
  19.6 20.5 %collective-permute-done.4 = bf16[2,16,6,8,128]{4,3,2,1,0:T(8,128)(2,1)S(1)} collective-permute-done((bf16[2,16,6,8,128]{4,3,2,1,0:T(8,128)(2,1)S(1)}, bf16[2,16,6,8,128]{4,3,2,1,0:T(8,128)(2,1)S(1)}, u32[]{:S(2)}, u32[]{:S(2)}) %collective-permute-start.4) | collective-permute-done | bytes 393248 | tf_op jit(solution)/shard_map/ppermute | solution.py:19
  40.2 6.7 %collective-permute-done.9 = bf16[2,16,6,8,128]{4,3,2,1,0:T(8,128)(2,1)S(1)} collective-permute-done((bf16[2,16,6,8,128]{4,3,2,1,0:T(8,128)(2,1)S(1)}, bf16[2,16,6,8,128]{4,3,2,1,0:T(8,128)(2,1)S(1)}, u32[]{:S(2)}, u32[]{:S(2)}) %collective-permute-start.9) | collective-permute-done | bytes 393248 | tf_op jit(solution)/shard_map/ppermute | solution.py:19
  47.0 2.1 %collective-permute-done.14 = bf16[2,16,6,8,128]{4,3,2,1,0:T(8,128)(2,1)S(1)} collective-permute-done((bf16[2,16,6,8,128]{4,3,2,1,0:T(8,128)(2,1)S(1)}, bf16[2,16,6,8,128]{4,3,2,1,0:T(8,128)(2,1)S(1)}, u32[]{:S(2)}, u32[]{:S(2)}) %collective-permute-start.14) | collective-permute-done | bytes 393248 | tf_op jit(solution)/shard_map/ppermute | solution.py:19
  49.2 3.0 %select_reduce_fusion.3 = (f32[2,16,3,8]{3,2,1,0:T(4,128)}, f32[2,16,3,8]{3,2,1,0:T(4,128)}, f32[2,16,3,8]{3,2,1,0:T(4,128)}, f32[2,16,3,8]{3,2,1,0:T(4,128)}, f...) fusion(pred[128]{0:T(512)(128)(4,1)S(1)} %get-tuple-element.86,, ...), kind=kLoop, calls=%fused_computation.118 | loop fusion | flops 5492736 | bytes 6340864 | tf_op jit(solution)/shard_map/reduce_sum | solution.py:41
  52.1 1.5 copy.99
  53.7 1.3 add_rsqrt_fusion.8
  55.0 1.4 copy.100
  56.4 1.5 copy.103
  57.9 1.3 add_rsqrt_fusion.7
  59.3 1.4 copy.104
  60.7 1.5 copy.105
  62.3 1.3 add_rsqrt_fusion.6
  63.6 1.4 copy.106
  65.0 1.5 copy.109
  66.6 1.3 add_rsqrt_fusion.5
  67.9 1.4 copy.110
  69.3 1.5 copy.111
  70.9 1.3 add_rsqrt_fusion.4
  72.2 1.4 copy.112
  73.6 1.5 copy.115
  75.1 1.3 add_rsqrt_fusion.3
  76.5 1.4 copy.116
  77.9 1.5 copy.117
  79.4 1.3 add_rsqrt_fusion.2
  80.8 1.4 copy.118
  82.2 1.5 copy.121
  83.7 1.3 add_rsqrt_fusion.1
  85.1 1.4 copy.122
  86.5 1.5 copy.123
  88.0 1.3 add_rsqrt_fusion
  89.4 1.4 copy.124
  90.8 1.5 copy.81
  92.3 1.3 add_rsqrt_fusion.15
  93.7 1.4 copy.82
  95.1 1.5 copy.83
  96.6 1.3 add_rsqrt_fusion.14
  98.0 1.4 copy.84
  99.4 1.5 copy.87
  100.9 1.3 add_rsqrt_fusion.13
  102.3 1.4 copy.88
  103.7 1.5 copy.89
  105.2 1.3 add_rsqrt_fusion.12
  106.6 1.4 copy.90
  108.0 1.5 copy.93
  109.5 1.3 add_rsqrt_fusion.11
  110.9 1.4 copy.94
  112.3 1.5 copy.95
  113.8 1.3 add_rsqrt_fusion.10
  115.2 1.5 copy.96
  116.6 1.5 copy.97
  118.1 1.3 add_rsqrt_fusion.9
  119.5 1.4 copy.98
  120.9 3.0 %select_select_fusion.7 = (f32[2,16,3,8,128]{4,3,2,1,0:T(8,128)S(1)}, f32[2,16,3,8,128]{4,3,2,1,0:T(8,128)S(1)}, f32[2,16,3,8,128]{4,3,2,1,0:T(8,128)S(1)}, f32[...) fusion(f32[2,16,3,8]{3,2,1,0:T(4,128)} %copy.84, ...), kind=kLoop, calls=%fused_computation.134 | loop fusion | flops 1572864 | bytes 3195136 | tf_op jit(solution)/shard_map/jit(_where)/select_n | solution.py:42
  131.0 1.6 %collective-permute-start.1 = (bf16[2,1,1,2,9,16,128]{6,5,4,3,2,1,0:T(8,128)(2,1)S(1)}, bf16[2,1,1,2,9,16,128]{6,5,4,3,2,1,0:T(8,128)(2,1)S(1)}, u32[]{:S(2)}, u32[]{:S(2)}) collective-permute-start(bf16[2,1,1,2,9,16,128]{6,5,4,3,2,1,0:T(8,128)(2,1)S(1)} %dynamic-slice_convert_fusion.3), channel_id=1, source_target_pairs={{0,8},{4,12},{8,0},{12,4},{16,24},{20,28},{24,16},{28,20},{1,9},{5... | collective-permute-start | bytes 442376 | tf_op jit(solution)/shard_map/ppermute | solution.py:83
  132.7 1.6 %collective-permute-start.6 = (bf16[1,2,1,2,9,16,128]{6,5,4,3,2,1,0:T(8,128)(2,1)S(1)}, bf16[1,2,1,2,9,16,128]{6,5,4,3,2,1,0:T(8,128)(2,1)S(1)}, u32[]{:S(2)}, u32[]{:S(2)}) collective-permute-start(bf16[1,2,1,2,9,16,128]{6,5,4,3,2,1,0:T(8,128)(2,1)S(1)} %dynamic-slice_convert_fusion.2), channel_id=1, source_target_pairs={{0,16},{4,20},{8,24},{12,28},{16,0},{20,4},{24,8},{28,12},{1,17},{... | collective-permute-start | bytes 442376 | tf_op jit(solution)/shard_map/ppermute | solution.py:83
  135.7 1.4 collective-permute-done.1
  137.2 2.3 %collective-permute-start.2 = (bf16[1,1,1,2,9,16,128]{6,5,4,3,2,1,0:T(8,128)(2,1)S(1)}, bf16[1,1,1,2,9,16,128]{6,5,4,3,2,1,0:T(8,128)(2,1)S(1)}, u32[]{:S(2)}, u32[]{:S(2)}) collective-permute-start(bf16[1,1,1,2,9,16,128]{6,5,4,3,2,1,0:T(8,128)(2,1)S(1)} %dynamic-slice_convert_fusion.7), channel_id=1, source_target_pairs={{0,16},{4,20},{8,24},{12,28},{16,0},{20,4},{24,8},{28,12},{1,17},{... | collective-permute-start | bytes 221192 | tf_op jit(solution)/shard_map/ppermute | solution.py:83
  139.6 1.5 collective-permute-start.7
  145.5 1.6 %collective-permute-done.17 = bf16[1,1,1,2,9,16,128]{6,5,4,3,2,1,0:T(8,128)(2,1)S(1)} collective-permute-done((bf16[1,1,1,2,9,16,128]{6,5,4,3,2,1,0:T(8,128)(2,1)S(1)}, bf16[1,1,1,2,9,16,128]{6,5,4,3,2,1,0:T(8,128)(2,1)S(1)}, u32[]{:S(2)}, u32[]{:S(2)}) %collective-permute-start.17) | collective-permute-done | bytes 73760 | tf_op jit(solution)/shard_map/ppermute | solution.py:83
  147.3 3.1 %fusion.5 = bf16[72,4001]{1,0:T(8,128)(2,1)S(1)} fusion(bf16[2048,4001]{1,0:T(8,128)(2,1)S(1)} %bitcast.333, bf16[9,8,16,128]{3,2,1,0:T(8,128)(2,1)S(1)} %bitcast.349), kind=kOutput, calls=%fused_computation.14 | convolution fusion | flops 1180519168 | bytes 17259152 | tf_op jit(solution)/shard_map/dot_general | solution.py:110
  150.7 1.5 copy.125
  (136 shorter events, 25.4 us)
Async XLA Ops:
  0.8 12.6 %collective-permute-start.3 = (s32[16]{0:T(128)S(1)}, s32[16]{0:T(128)S(1)}, u32[]{:S(2)}, u32[]{:S(2)}) collective-permute-start(s32[16]{0:T(128)S(1)} %get-tuple-element.59), channel_id=1, source_target_pairs={{0,3},{1,0},{2,1},{3,2},{4,7},{5,4},{6,5},{7,6},{8,11},{9,8},{10,9... | collective-permute-start | bytes 200 | tf_op jit(solution)/shard_map/ppermute | solution.py:19
  0.8 13.0 %collective-permute-start.8 = (s32[16]{0:T(128)S(1)}, s32[16]{0:T(128)S(1)}, u32[]{:S(2)}, u32[]{:S(2)}) collective-permute-start(s32[16]{0:T(128)S(1)} %get-tuple-element.57), channel_id=1, source_target_pairs={{0,2},{1,3},{2,0},{3,1},{4,6},{5,7},{6,4},{7,5},{8,10},{9,11},{10,... | collective-permute-start | bytes 200 | tf_op jit(solution)/shard_map/ppermute | solution.py:19
  3.9 12.3 %collective-permute-start.13 = (s32[16]{0:T(128)S(1)}, s32[16]{0:T(128)S(1)}, u32[]{:S(2)}, u32[]{:S(2)}) collective-permute-start(s32[16]{0:T(128)S(1)} %get-tuple-element.63), channel_id=1, source_target_pairs={{0,1},{1,2},{2,3},{3,0},{4,5},{5,6},{6,7},{7,4},{8,9},{9,10},{10,1... | collective-permute-start | bytes 200 | tf_op jit(solution)/shard_map/ppermute | solution.py:19
  11.4 0.7 copy-start.7
  13.8 26.3 %collective-permute-start.4 = (bf16[2,16,6,8,128]{4,3,2,1,0:T(8,128)(2,1)S(1)}, bf16[2,16,6,8,128]{4,3,2,1,0:T(8,128)(2,1)S(1)}, u32[]{:S(2)}, u32[]{:S(2)}) collective-permute-start(bf16[2,16,6,8,128]{4,3,2,1,0:T(8,128)(2,1)S(1)} %bitcast.368), channel_id=1, source_target_pairs={{0,1},{1,2},{2,3},{3,0},{4,5},{5,6},{6,7},{7,4},{8,9},{9,10},{10,1... | collective-permute-start | bytes 1179656 | tf_op jit(solution)/shard_map/ppermute | solution.py:19
  14.2 32.7 %collective-permute-start.9 = (bf16[2,16,6,8,128]{4,3,2,1,0:T(8,128)(2,1)S(1)}, bf16[2,16,6,8,128]{4,3,2,1,0:T(8,128)(2,1)S(1)}, u32[]{:S(2)}, u32[]{:S(2)}) collective-permute-start(bf16[2,16,6,8,128]{4,3,2,1,0:T(8,128)(2,1)S(1)} %bitcast.369), channel_id=1, source_target_pairs={{0,2},{1,3},{2,0},{3,1},{4,6},{5,7},{6,4},{7,5},{8,10},{9,11},{10,... | collective-permute-start | bytes 1179656 | tf_op jit(solution)/shard_map/ppermute | solution.py:19
  16.6 32.5 %collective-permute-start.14 = (bf16[2,16,6,8,128]{4,3,2,1,0:T(8,128)(2,1)S(1)}, bf16[2,16,6,8,128]{4,3,2,1,0:T(8,128)(2,1)S(1)}, u32[]{:S(2)}, u32[]{:S(2)}) collective-permute-start(bf16[2,16,6,8,128]{4,3,2,1,0:T(8,128)(2,1)S(1)} %bitcast.370), channel_id=1, source_target_pairs={{0,3},{1,0},{2,1},{3,2},{4,7},{5,4},{6,5},{7,6},{8,11},{9,8},{10,9... | collective-permute-start | bytes 1179656 | tf_op jit(solution)/shard_map/ppermute | solution.py:19
  17.7 31.5 %copy-start.8 = (pred[128]{0:T(512)(128)(4,1)}, pred[128]{0:T(512)(128)(4,1)S(1)}, u32[]{:S(2)}) copy-start(pred[128]{0:T(512)(128)(4,1)S(1)} %get-tuple-element.85) | copy-start | bytes 388
  17.7 31.5 %copy-start.9 = (pred[128]{0:T(512)(128)(4,1)}, pred[128]{0:T(512)(128)(4,1)S(1)}, u32[]{:S(2)}) copy-start(pred[128]{0:T(512)(128)(4,1)S(1)} %get-tuple-element.86) | copy-start | bytes 388
  40.1 6.9 %copy-start.5 = (bf16[2,16,6,8,128]{4,3,2,1,0:T(8,128)(2,1)}, bf16[2,16,6,8,128]{4,3,2,1,0:T(8,128)(2,1)S(1)}, u32[]{:S(2)}) copy-start(bf16[2,16,6,8,128]{4,3,2,1,0:T(8,128)(2,1)S(1)} %collective-permute-done.4) | copy-start | bytes 1179652
  46.9 2.2 %copy-start.3 = (bf16[2,16,6,8,128]{4,3,2,1,0:T(8,128)(2,1)}, bf16[2,16,6,8,128]{4,3,2,1,0:T(8,128)(2,1)S(1)}, u32[]{:S(2)}) copy-start(bf16[2,16,6,8,128]{4,3,2,1,0:T(8,128)(2,1)S(1)} %collective-permute-done.9) | copy-start | bytes 1179652
  46.9 2.2 %copy-start = (f32[4,8,48,128]{3,2,1,0:T(8,128)S(1)}, f32[4,8,48,128]{3,2,1,0:T(8,128)}, u32[]{:S(2)}) copy-start(f32[4,8,48,128]{3,2,1,0:T(8,128)} %copy.142) | copy-start | bytes 2359300
  46.9 2.2 %copy-start.1 = (f32[4,8,48,128]{3,2,1,0:T(8,128)S(1)}, f32[4,8,48,128]{3,2,1,0:T(8,128)}, u32[]{:S(2)}) copy-start(f32[4,8,48,128]{3,2,1,0:T(8,128)} %copy.141) | copy-start | bytes 2359300
  120.9 3.0 %copy-start.2 = (f32[4,8,48,128]{3,2,1,0:T(8,128)S(1)}, f32[4,8,48,128]{3,2,1,0:T(8,128)}, u32[]{:S(2)}) copy-start(f32[4,8,48,128]{3,2,1,0:T(8,128)} %copy.141) | copy-start | bytes 2359300
  124.9 5.9 %collective-permute-start = (bf16[2,2,1,2,9,16,128]{6,5,4,3,2,1,0:T(8,128)(2,1)S(1)}, bf16[2,2,1,2,9,16,128]{6,5,4,3,2,1,0:T(8,128)(2,1)S(1)}, u32[]{:S(2)}, u32[]{:S(2)}) collective-permute-start(bf16[2,2,1,2,9,16,128]{6,5,4,3,2,1,0:T(8,128)(2,1)S(1)} %constant_dynamic-slice_fusion.3), channel_id=1, source_target_pairs={{0,4},{4,0},{8,12},{12,8},{16,20},{20,16},{24,28},{28,24},{1,5},{5... | collective-permute-start | bytes 884744 | tf_op jit(solution)/shard_map/ppermute | solution.py:83
  125.1 1.0 copy-start.6
  126.9 5.7 %collective-permute-start.5 = (bf16[2,2,1,2,9,16,128]{6,5,4,3,2,1,0:T(8,128)(2,1)S(1)}, bf16[2,2,1,2,9,16,128]{6,5,4,3,2,1,0:T(8,128)(2,1)S(1)}, u32[]{:S(2)}, u32[]{:S(2)}) collective-permute-start(bf16[2,2,1,2,9,16,128]{6,5,4,3,2,1,0:T(8,128)(2,1)S(1)} %constant_dynamic-slice_fusion.2), channel_id=1, source_target_pairs={{0,4},{4,0},{8,12},{12,8},{16,20},{20,16},{24,28},{28,24},{1,5},{5... | collective-permute-start | bytes 884744 | tf_op jit(solution)/shard_map/ppermute | solution.py:83
  127.5 1.0 copy-start.4
  127.6 19.7 %slice-start = ((s8[16777216]{0:T(1024)(128)(4,1)}), s8[4194304]{0:T(1024)(128)(4,1)S(1)}, s32[]{:S(2)}) async-start(s8[16777216]{0:T(1024)(128)(4,1)} %bitcast.332), calls=%async_computation | async-start | bytes 8388608
  129.0 18.2 %slice-start.1 = ((s8[16777216]{0:T(1024)(128)(4,1)}), s8[4194304]{0:T(1024)(128)(4,1)S(1)}, s32[]{:S(2)}) async-start(s8[16777216]{0:T(1024)(128)(4,1)} %bitcast.332), calls=%async_computation.1 | async-start | bytes 8388608
  129.3 5.0 %collective-permute-start.10 = (bf16[2,2,1,2,9,16,128]{6,5,4,3,2,1,0:T(8,128)(2,1)S(1)}, bf16[2,2,1,2,9,16,128]{6,5,4,3,2,1,0:T(8,128)(2,1)S(1)}, u32[]{:S(2)}, u32[]{:S(2)}) collective-permute-start(bf16[2,2,1,2,9,16,128]{6,5,4,3,2,1,0:T(8,128)(2,1)S(1)} %constant_dynamic-slice_fusion.1), channel_id=1, source_target_pairs={{0,4},{4,0},{8,12},{12,8},{16,20},{20,16},{24,28},{28,24},{1,5},{5... | collective-permute-start | bytes 884744 | tf_op jit(solution)/shard_map/ppermute | solution.py:83
  129.6 17.6 %slice-start.2 = ((s8[16777216]{0:T(1024)(128)(4,1)}), s8[4194304]{0:T(1024)(128)(4,1)S(1)}, s32[]{:S(2)}) async-start(s8[16777216]{0:T(1024)(128)(4,1)} %bitcast.332), calls=%async_computation.2 | async-start | bytes 8388608
  130.3 4.7 %collective-permute-start.15 = (bf16[2,2,1,2,9,16,128]{6,5,4,3,2,1,0:T(8,128)(2,1)S(1)}, bf16[2,2,1,2,9,16,128]{6,5,4,3,2,1,0:T(8,128)(2,1)S(1)}, u32[]{:S(2)}, u32[]{:S(2)}) collective-permute-start(bf16[2,2,1,2,9,16,128]{6,5,4,3,2,1,0:T(8,128)(2,1)S(1)} %constant_dynamic-slice_fusion), channel_id=1, source_target_pairs={{0,4},{4,0},{8,12},{12,8},{16,20},{20,16},{24,28},{28,24},{1,5},{5... | collective-permute-start | bytes 884744 | tf_op jit(solution)/shard_map/ppermute | solution.py:83
  131.0 6.1 %collective-permute-start.1 = (bf16[2,1,1,2,9,16,128]{6,5,4,3,2,1,0:T(8,128)(2,1)S(1)}, bf16[2,1,1,2,9,16,128]{6,5,4,3,2,1,0:T(8,128)(2,1)S(1)}, u32[]{:S(2)}, u32[]{:S(2)}) collective-permute-start(bf16[2,1,1,2,9,16,128]{6,5,4,3,2,1,0:T(8,128)(2,1)S(1)} %dynamic-slice_convert_fusion.3), channel_id=1, source_target_pairs={{0,8},{4,12},{8,0},{12,4},{16,24},{20,28},{24,16},{28,20},{1,9},{5... | collective-permute-start | bytes 442376 | tf_op jit(solution)/shard_map/ppermute | solution.py:83
  132.7 14.6 %slice-start.3 = ((s8[16777216]{0:T(1024)(128)(4,1)}), s8[4194304]{0:T(1024)(128)(4,1)S(1)}, s32[]{:S(2)}) async-start(s8[16777216]{0:T(1024)(128)(4,1)} %bitcast.332), calls=%async_computation.3 | async-start | bytes 8388608
  132.7 6.8 %collective-permute-start.6 = (bf16[1,2,1,2,9,16,128]{6,5,4,3,2,1,0:T(8,128)(2,1)S(1)}, bf16[1,2,1,2,9,16,128]{6,5,4,3,2,1,0:T(8,128)(2,1)S(1)}, u32[]{:S(2)}, u32[]{:S(2)}) collective-permute-start(bf16[1,2,1,2,9,16,128]{6,5,4,3,2,1,0:T(8,128)(2,1)S(1)} %dynamic-slice_convert_fusion.2), channel_id=1, source_target_pairs={{0,16},{4,20},{8,24},{12,28},{16,0},{20,4},{24,8},{28,12},{1,17},{... | collective-permute-start | bytes 442376 | tf_op jit(solution)/shard_map/ppermute | solution.py:83
  134.4 6.7 %collective-permute-start.11 = (bf16[2,1,1,2,9,16,128]{6,5,4,3,2,1,0:T(8,128)(2,1)S(1)}, bf16[2,1,1,2,9,16,128]{6,5,4,3,2,1,0:T(8,128)(2,1)S(1)}, u32[]{:S(2)}, u32[]{:S(2)}) collective-permute-start(bf16[2,1,1,2,9,16,128]{6,5,4,3,2,1,0:T(8,128)(2,1)S(1)} %dynamic-slice_convert_fusion.1), channel_id=1, source_target_pairs={{0,8},{4,12},{8,0},{12,4},{16,24},{20,28},{24,16},{28,20},{1,9},{5... | collective-permute-start | bytes 442376 | tf_op jit(solution)/shard_map/ppermute | solution.py:83
  135.1 7.6 %collective-permute-start.16 = (bf16[1,2,1,2,9,16,128]{6,5,4,3,2,1,0:T(8,128)(2,1)S(1)}, bf16[1,2,1,2,9,16,128]{6,5,4,3,2,1,0:T(8,128)(2,1)S(1)}, u32[]{:S(2)}, u32[]{:S(2)}) collective-permute-start(bf16[1,2,1,2,9,16,128]{6,5,4,3,2,1,0:T(8,128)(2,1)S(1)} %dynamic-slice_convert_fusion), channel_id=1, source_target_pairs={{0,16},{4,20},{8,24},{12,28},{16,0},{20,4},{24,8},{28,12},{1,17},{... | collective-permute-start | bytes 442376 | tf_op jit(solution)/shard_map/ppermute | solution.py:83
  137.2 6.9 %collective-permute-start.2 = (bf16[1,1,1,2,9,16,128]{6,5,4,3,2,1,0:T(8,128)(2,1)S(1)}, bf16[1,1,1,2,9,16,128]{6,5,4,3,2,1,0:T(8,128)(2,1)S(1)}, u32[]{:S(2)}, u32[]{:S(2)}) collective-permute-start(bf16[1,1,1,2,9,16,128]{6,5,4,3,2,1,0:T(8,128)(2,1)S(1)} %dynamic-slice_convert_fusion.7), channel_id=1, source_target_pairs={{0,16},{4,20},{8,24},{12,28},{16,0},{20,4},{24,8},{28,12},{1,17},{... | collective-permute-start | bytes 221192 | tf_op jit(solution)/shard_map/ppermute | solution.py:83
  139.6 5.1 %collective-permute-start.7 = (bf16[1,1,1,2,9,16,128]{6,5,4,3,2,1,0:T(8,128)(2,1)S(1)}, bf16[1,1,1,2,9,16,128]{6,5,4,3,2,1,0:T(8,128)(2,1)S(1)}, u32[]{:S(2)}, u32[]{:S(2)}) collective-permute-start(bf16[1,1,1,2,9,16,128]{6,5,4,3,2,1,0:T(8,128)(2,1)S(1)} %dynamic-slice_convert_fusion.6), channel_id=1, source_target_pairs={{0,8},{4,12},{8,0},{12,4},{16,24},{20,28},{24,16},{28,20},{1,9},{5... | collective-permute-start | bytes 221192 | tf_op jit(solution)/shard_map/ppermute | solution.py:83
  141.1 4.4 %collective-permute-start.12 = (bf16[1,1,1,2,9,16,128]{6,5,4,3,2,1,0:T(8,128)(2,1)S(1)}, bf16[1,1,1,2,9,16,128]{6,5,4,3,2,1,0:T(8,128)(2,1)S(1)}, u32[]{:S(2)}, u32[]{:S(2)}) collective-permute-start(bf16[1,1,1,2,9,16,128]{6,5,4,3,2,1,0:T(8,128)(2,1)S(1)} %dynamic-slice_convert_fusion.5), channel_id=1, source_target_pairs={{0,16},{4,20},{8,24},{12,28},{16,0},{20,4},{24,8},{28,12},{1,17},{... | collective-permute-start | bytes 221192 | tf_op jit(solution)/shard_map/ppermute | solution.py:83
  142.7 4.4 %collective-permute-start.17 = (bf16[1,1,1,2,9,16,128]{6,5,4,3,2,1,0:T(8,128)(2,1)S(1)}, bf16[1,1,1,2,9,16,128]{6,5,4,3,2,1,0:T(8,128)(2,1)S(1)}, u32[]{:S(2)}, u32[]{:S(2)}) collective-permute-start(bf16[1,1,1,2,9,16,128]{6,5,4,3,2,1,0:T(8,128)(2,1)S(1)} %dynamic-slice_convert_fusion.4), channel_id=1, source_target_pairs={{0,8},{4,12},{8,0},{12,4},{16,24},{20,28},{24,16},{28,20},{1,9},{5... | collective-permute-start | bytes 221192 | tf_op jit(solution)/shard_map/ppermute | solution.py:83

commit v4 on v3

--- a/solution.py
+++ b/solution.py
@@ -31,15 +31,12 @@
 
 def whiten(spectra):
     lanes = spectra.shape[-1]
-    per_row = lanes // BAND
     values = spectra.astype(jnp.float32).reshape(spectra.shape[:2] + (3, 2) + spectra.shape[3:])
     square = values[:, :, :, 0] ** 2 + values[:, :, :, 1] ** 2
-    band = jnp.arange(lanes, dtype=jnp.int32) // BAND
-    inverse = jnp.zeros_like(square)
-    for index in range(per_row):
-        inside = band == index
-        power = jnp.sum(jnp.where(inside, square, 0.0), axis=-1, keepdims=True) * (1.0 / BAND)
-        inverse = jnp.where(inside, lax.rsqrt(power + 1e-06), inverse)
+    band = np.arange(lanes) // BAND
+    mean = jnp.asarray((band[:, None] == band[None, :]).astype(np.float32) / BAND)
+    power = jnp.dot(square, mean, precision=lax.Precision.HIGHEST, preferred_element_type=jnp.float32)
+    inverse = lax.rsqrt(power + 1e-06)
     return (values * inverse[:, :, :, None]).astype(jnp.bfloat16)
 
 

time: 155 us -> 82.1 us (0.53); the launches traced: 152 us -> 80.9 us
  local copies, waits for them, and re-layouts: 57.3 us -> 9.69 us
  other arithmetic: 34.3 us -> 7.68 us
  matrix products: 5.07 us -> 8.8 us
    reduce_sum x16 -> x0, local copies, waits for them, and re-layouts: 24.2 us -> none  [whiten(): jnp.sum(jnp.where(inside, square, 0.0), axis=-1, keepdims=True)]
    rsqrt x16 -> x0, local copies, waits for them, and re-layouts: 23 us -> none  [whiten(): inverse = jnp.where(inside, lax.rsqrt(power + 1e-06), inverse)]
    rsqrt x16 -> x0, other arithmetic: 21.5 us -> none  [whiten(): inverse = jnp.where(inside, lax.rsqrt(power + 1e-06), inverse)]
    ppermute x6, waiting for transfers between devices: 29.3 us -> 25.5 us  [shifted(): return lax.ppermute(value, axis, pairs)]
    dot_general x0 -> x8, matrix products: none -> 3.73 us  [whiten(): jnp.dot(square, mean, precision=lax.Precision.HIGHEST, preferred_element_...]
    ppermute x12, waiting for transfers between devices: 5.37 us -> 8.49 us  [sum_at_owner(): got = lax.ppermute(give.astype(jnp.bfloat16), axis, swap)]
    select_n x1 -> x0, other arithmetic: 3.04 us -> none  [whiten(): inverse = jnp.where(inside, lax.rsqrt(power + 1e-06), inverse)]
    reduce_sum x1 -> x0, other arithmetic: 2.98 us -> none  [whiten(): jnp.sum(jnp.where(inside, square, 0.0), axis=-1, keepdims=True)]
  transfers between devices with their start and end apart: 18 -> 18, of which waited for: 9 -> 8; matrix products, arithmetic and copies ran while one was open for 9% -> 15% of each run, Pallas kernels for 0% -> 0%
where the time goes in v4:
time: 82.1 us; the launch traced here: 80.9 us
  waiting for transfers between devices  34 us (41%)
  starting transfers between devices  20 us (24%)
  local copies, waits for them, and re-layouts  9.69 us (12%)
  matrix products  8.8 us (11%)
  other arithmetic  7.68 us (9%)
    ppermute x6, waiting for transfers between devices, shifted(): return lax.ppermute(value, axis, pairs)  25.5 us
    ppermute x12, starting transfers between devices, sum_at_owner(): got = lax.ppermute(give.astype(jnp.bfloat16), axis, swap)  11.2 us
    ppermute x6, starting transfers between devices, shifted(): return lax.ppermute(value, axis, pairs)  8.79 us
    ppermute x12, waiting for transfers between devices, sum_at_owner(): got = lax.ppermute(give.astype(jnp.bfloat16), axis, swap)  8.49 us
    dot_general x8, matrix products, whiten(): jnp.dot(square, mean, precision=lax.Precision.HIGHEST, preferred_element_...  3.73 us
    unnamed x22, local copies, waits for them, and re-layouts  3.11 us
    dot_general x1, matrix products, per_device(): lagged = jnp.dot(rows, table, preferred_element_type=jnp.float32)  3.1 us
    lt x4, other arithmetic, reduce_tile(): value = jnp.where((slots < limit)[:, None, None, None], value, 0.0)  2.61 us
  transfers between devices with their start and end apart: 18, of which 8 were waited for; matrix products, arithmetic and copies ran while one was open for 15% of the time, Pallas kernels for 0%

profile of v4, /device:TPU:8, one launch (start us, length us, event | category | flops | bytes accessed | tf_op | source)
XLA Modules:
  0.0 80.9 jit_solution(18427338090558721593)
XLA Ops:
  0.0 0.8 slice_bitcast_fusion.33
  0.8 1.2 %copy.59 = bf16[2,6,4,8,1024]{4,3,1,2,0:T(8,128)(2,1)S(1)} copy(bf16[2,6,4,8,1024]{4,3,2,1,0:T(8,128)(2,1)} %bitcast.280) | data formatting | bytes 1572864 | tf_op jit(solution)/shard_map/reshape | solution.py:45
  2.1 0.2 fusion.4
  2.3 0.1 copy.60
  2.5 0.7 copy-done
  3.2 0.5 fusion.13
  3.8 0.2 fusion.3
  4.0 0.1 copy.61
  4.2 0.5 fusion.12
  4.8 0.6 copy-done.2
  5.4 0.7 fusion.85
  6.1 0.7 broadcast_compare_fusion.3
  6.7 0.4 add_reduce_fusion.3
  7.1 0.2 fusion.14
  7.3 0.7 constant_dynamic-slice_fusion.3
  8.1 3.0 %collective-permute-start.8 = (s32[16]{0:T(128)S(1)}, s32[16]{0:T(128)S(1)}, u32[]{:S(2)}, u32[]{:S(2)}) collective-permute-start(s32[16]{0:T(128)S(1)} %get-tuple-element.30), channel_id=1, source_target_pairs={{0,2},{1,3},{2,0},{3,1},{4,6},{5,7},{6,4},{7,5},{8,10},{9,11},{10,... | collective-permute-start | bytes 200 | tf_op jit(solution)/shard_map/ppermute | solution.py:19
  11.1 2.5 %collective-permute-start.13 = (s32[16]{0:T(128)S(1)}, s32[16]{0:T(128)S(1)}, u32[]{:S(2)}, u32[]{:S(2)}) collective-permute-start(s32[16]{0:T(128)S(1)} %get-tuple-element.35), channel_id=1, source_target_pairs={{0,1},{1,2},{2,3},{3,0},{4,5},{5,6},{6,7},{7,4},{8,9},{9,10},{10,1... | collective-permute-start | bytes 200 | tf_op jit(solution)/shard_map/ppermute | solution.py:19
  13.6 0.2 fusion.2
  13.9 0.1 copy.62
  14.0 0.5 fusion.11
  14.6 0.8 slice_bitcast_fusion.15
  15.4 0.7 broadcast_compare_fusion.2
  16.1 0.2 fusion.1
  16.5 0.5 fusion.9
  17.1 0.6 broadcast_compare_fusion.1
  17.8 0.2 fusion
  18.1 0.1 copy.66
  18.2 0.5 fusion.7
  18.8 0.6 broadcast_compare_fusion
  19.5 0.2 convolution_convert_fusion.4
  20.0 0.2 convolution_convert_fusion.2
  20.3 2.0 %collective-permute-start.9 = (bf16[2,16,6,8,128]{4,3,2,1,0:T(8,128)(2,1)S(1)}, bf16[2,16,6,8,128]{4,3,2,1,0:T(8,128)(2,1)S(1)}, u32[]{:S(2)}, u32[]{:S(2)}) collective-permute-start(bf16[2,16,6,8,128]{4,3,2,1,0:T(8,128)(2,1)S(1)} %bitcast.282), channel_id=1, source_target_pairs={{0,2},{1,3},{2,0},{3,1},{4,6},{5,7},{6,4},{7,5},{8,10},{9,11},{10,... | collective-permute-start | bytes 1179656 | tf_op jit(solution)/shard_map/ppermute | solution.py:19
  22.4 0.2 convolution_convert_fusion
  22.7 1.3 %collective-permute-start.14 = (bf16[2,16,6,8,128]{4,3,2,1,0:T(8,128)(2,1)S(1)}, bf16[2,16,6,8,128]{4,3,2,1,0:T(8,128)(2,1)S(1)}, u32[]{:S(2)}, u32[]{:S(2)}) collective-permute-start(bf16[2,16,6,8,128]{4,3,2,1,0:T(8,128)(2,1)S(1)} %bitcast.281), channel_id=1, source_target_pairs={{0,3},{1,0},{2,1},{3,2},{4,7},{5,4},{6,5},{7,6},{8,11},{9,8},{10,9... | collective-permute-start | bytes 1179656 | tf_op jit(solution)/shard_map/ppermute | solution.py:19
  23.9 1.0 %convert_add_fusion.3 = f32[2,2,1,2,9,16,128]{6,5,4,3,2,1,0:T(8,128)S(1)} fusion(bf16[2,2,1,2,9,16,128]{6,5,4,3,2,1,0:T(8,128)(2,1)} %collective-permute-done, bf16[2,2,2,2,9,16,128]{6,5,4,3,2,1,0:T(8,128)(2,1)S(1)} %fusion.14, s32[]{:T(128)S(6)} %select_n.54), kind=kLoop, calls=%fused_computation.58 | loop fusion | flops 442368 | bytes 1179652 | tf_op jit(solution)/shard_map/add | solution.py:81
  25.0 1.6 %collective-permute-start.1 = (bf16[2,1,1,2,9,16,128]{6,5,4,3,2,1,0:T(8,128)(2,1)S(1)}, bf16[2,1,1,2,9,16,128]{6,5,4,3,2,1,0:T(8,128)(2,1)S(1)}, u32[]{:S(2)}, u32[]{:S(2)}) collective-permute-start(bf16[2,1,1,2,9,16,128]{6,5,4,3,2,1,0:T(8,128)(2,1)S(1)} %dynamic-slice_convert_fusion.3), channel_id=1, source_target_pairs={{0,8},{4,12},{8,0},{12,4},{16,24},{20,28},{24,16},{28,20},{1,9},{5... | collective-permute-start | bytes 442376 | tf_op jit(solution)/shard_map/ppermute | solution.py:80
  26.6 5.4 %collective-permute-done.4 = bf16[2,16,6,8,128]{4,3,2,1,0:T(8,128)(2,1)S(1)} collective-permute-done((bf16[2,16,6,8,128]{4,3,2,1,0:T(8,128)(2,1)S(1)}, bf16[2,16,6,8,128]{4,3,2,1,0:T(8,128)(2,1)S(1)}, u32[]{:S(2)}, u32[]{:S(2)}) %collective-permute-start.4) | collective-permute-done | bytes 393248 | tf_op jit(solution)/shard_map/ppermute | solution.py:19
  32.0 0.5 fusion.10
  32.6 0.9 %copy-done.1 = f32[2,16,3,8,128]{4,3,2,1,0:T(8,128)S(1)} copy-done((f32[2,16,3,8,128]{4,3,2,1,0:T(8,128)S(1)}, f32[2,16,3,8,128]{4,3,2,1,0:T(8,128)}, u32[]{:S(2)}) %copy-start.1) | copy-done | bytes 393240
  33.6 0.4 add_reduce_fusion.2
  34.0 0.2 fusion.15
  34.3 19.4 %collective-permute-done.9 = bf16[2,16,6,8,128]{4,3,2,1,0:T(8,128)(2,1)S(1)} collective-permute-done((bf16[2,16,6,8,128]{4,3,2,1,0:T(8,128)(2,1)S(1)}, bf16[2,16,6,8,128]{4,3,2,1,0:T(8,128)(2,1)S(1)}, u32[]{:S(2)}, u32[]{:S(2)}) %collective-permute-start.9) | collective-permute-done | bytes 393248 | tf_op jit(solution)/shard_map/ppermute | solution.py:19
  53.7 0.5 fusion.8
  54.4 0.4 add_reduce_fusion.1
  54.8 0.2 fusion.16
  55.1 0.7 collective-permute-done.14
  55.9 0.5 fusion.6
  56.6 0.4 add_reduce_fusion
  57.0 0.2 fusion.17
  57.2 1.6 %collective-permute-start.2 = (bf16[1,1,1,2,9,16,128]{6,5,4,3,2,1,0:T(8,128)(2,1)S(1)}, bf16[1,1,1,2,9,16,128]{6,5,4,3,2,1,0:T(8,128)(2,1)S(1)}, u32[]{:S(2)}, u32[]{:S(2)}) collective-permute-start(bf16[1,1,1,2,9,16,128]{6,5,4,3,2,1,0:T(8,128)(2,1)S(1)} %dynamic-slice_convert_fusion.7), channel_id=1, source_target_pairs={{0,16},{4,20},{8,24},{12,28},{16,0},{20,4},{24,8},{28,12},{1,17},{... | collective-permute-start | bytes 221192 | tf_op jit(solution)/shard_map/ppermute | solution.py:80
  58.9 2.7 %collective-permute-done.2 = bf16[1,1,1,2,9,16,128]{6,5,4,3,2,1,0:T(8,128)(2,1)S(1)} collective-permute-done((bf16[1,1,1,2,9,16,128]{6,5,4,3,2,1,0:T(8,128)(2,1)S(1)}, bf16[1,1,1,2,9,16,128]{6,5,4,3,2,1,0:T(8,128)(2,1)S(1)}, u32[]{:S(2)}, u32[]{:S(2)}) %collective-permute-start.2) | collective-permute-done | bytes 73760 | tf_op jit(solution)/shard_map/ppermute | solution.py:80
  61.8 1.6 %collective-permute-start.6 = (bf16[1,2,1,2,9,16,128]{6,5,4,3,2,1,0:T(8,128)(2,1)S(1)}, bf16[1,2,1,2,9,16,128]{6,5,4,3,2,1,0:T(8,128)(2,1)S(1)}, u32[]{:S(2)}, u32[]{:S(2)}) collective-permute-start(bf16[1,2,1,2,9,16,128]{6,5,4,3,2,1,0:T(8,128)(2,1)S(1)} %dynamic-slice_convert_fusion.2), channel_id=1, source_target_pairs={{0,16},{4,20},{8,24},{12,28},{16,0},{20,4},{24,8},{28,12},{1,17},{... | collective-permute-start | bytes 442376 | tf_op jit(solution)/shard_map/ppermute | solution.py:80
  63.5 1.6 %collective-permute-start.11 = (bf16[2,1,1,2,9,16,128]{6,5,4,3,2,1,0:T(8,128)(2,1)S(1)}, bf16[2,1,1,2,9,16,128]{6,5,4,3,2,1,0:T(8,128)(2,1)S(1)}, u32[]{:S(2)}, u32[]{:S(2)}) collective-permute-start(bf16[2,1,1,2,9,16,128]{6,5,4,3,2,1,0:T(8,128)(2,1)S(1)} %dynamic-slice_convert_fusion.1), channel_id=1, source_target_pairs={{0,8},{4,12},{8,0},{12,4},{16,24},{20,28},{24,16},{28,20},{1,9},{5... | collective-permute-start | bytes 442376 | tf_op jit(solution)/shard_map/ppermute | solution.py:80
  65.2 0.6 collective-permute-start.16
  65.8 2.2 %collective-permute-done.6 = bf16[1,2,1,2,9,16,128]{6,5,4,3,2,1,0:T(8,128)(2,1)S(1)} collective-permute-done((bf16[1,2,1,2,9,16,128]{6,5,4,3,2,1,0:T(8,128)(2,1)S(1)}, bf16[1,2,1,2,9,16,128]{6,5,4,3,2,1,0:T(8,128)(2,1)S(1)}, u32[]{:S(2)}, u32[]{:S(2)}) %collective-permute-start.6) | collective-permute-done | bytes 147488 | tf_op jit(solution)/shard_map/ppermute | solution.py:80
  68.0 2.0 %collective-permute-start.7 = (bf16[1,1,1,2,9,16,128]{6,5,4,3,2,1,0:T(8,128)(2,1)S(1)}, bf16[1,1,1,2,9,16,128]{6,5,4,3,2,1,0:T(8,128)(2,1)S(1)}, u32[]{:S(2)}, u32[]{:S(2)}) collective-permute-start(bf16[1,1,1,2,9,16,128]{6,5,4,3,2,1,0:T(8,128)(2,1)S(1)} %dynamic-slice_convert_fusion.6), channel_id=1, source_target_pairs={{0,8},{4,12},{8,0},{12,4},{16,24},{20,28},{24,16},{28,20},{1,9},{5... | collective-permute-start | bytes 221192 | tf_op jit(solution)/shard_map/ppermute | solution.py:80
  70.0 1.4 %collective-permute-start.12 = (bf16[1,1,1,2,9,16,128]{6,5,4,3,2,1,0:T(8,128)(2,1)S(1)}, bf16[1,1,1,2,9,16,128]{6,5,4,3,2,1,0:T(8,128)(2,1)S(1)}, u32[]{:S(2)}, u32[]{:S(2)}) collective-permute-start(bf16[1,1,1,2,9,16,128]{6,5,4,3,2,1,0:T(8,128)(2,1)S(1)} %dynamic-slice_convert_fusion.5), channel_id=1, source_target_pairs={{0,16},{4,20},{8,24},{12,28},{16,0},{20,4},{24,8},{28,12},{1,17},{... | collective-permute-start | bytes 221192 | tf_op jit(solution)/shard_map/ppermute | solution.py:80
  71.5 0.8 collective-permute-start.17
  72.3 0.8 collective-permute-done.7
  73.0 1.4 %collective-permute-done.12 = bf16[1,1,1,2,9,16,128]{6,5,4,3,2,1,0:T(8,128)(2,1)S(1)} collective-permute-done((bf16[1,1,1,2,9,16,128]{6,5,4,3,2,1,0:T(8,128)(2,1)S(1)}, bf16[1,1,1,2,9,16,128]{6,5,4,3,2,1,0:T(8,128)(2,1)S(1)}, u32[]{:S(2)}, u32[]{:S(2)}) %collective-permute-start.12) | collective-permute-done | bytes 73760 | tf_op jit(solution)/shard_map/ppermute | solution.py:80
  74.5 1.4 %collective-permute-done.17 = bf16[1,1,1,2,9,16,128]{6,5,4,3,2,1,0:T(8,128)(2,1)S(1)} collective-permute-done((bf16[1,1,1,2,9,16,128]{6,5,4,3,2,1,0:T(8,128)(2,1)S(1)}, bf16[1,1,1,2,9,16,128]{6,5,4,3,2,1,0:T(8,128)(2,1)S(1)}, u32[]{:S(2)}, u32[]{:S(2)}) %collective-permute-start.17) | collective-permute-done | bytes 73760 | tf_op jit(solution)/shard_map/ppermute | solution.py:80
  76.0 3.1 %fusion.5 = bf16[72,4001]{1,0:T(8,128)(2,1)S(1)} fusion(bf16[2048,4001]{1,0:T(8,128)(2,1)S(1)} %bitcast.246, bf16[9,8,16,128]{3,2,1,0:T(8,128)(2,1)S(1)} %bitcast.262), kind=kOutput, calls=%fused_computation.14 | convolution fusion | flops 1180519168 | bytes 17259152 | tf_op jit(solution)/shard_map/dot_general | solution.py:107
  79.1 0.3 reshape.337
  79.4 1.5 %copy.47 = bf16[1,4,2,9,4001]{4,2,3,1,0:T(2,128)(2,1)} copy(bf16[1,4,2,9,4001]{4,3,2,1,0:T(8,128)(2,1)S(1)} %reshape.337) | data formatting | bytes 1152288 | tf_op jit(solution)/shard_map/reshape | solution.py:109
  (78 shorter events, 3.0 us)
Async XLA Ops:
  2.3 0.8 %copy-start = (f32[128,128,1,1,1]{1,0,4,3,2:T(8,128)S(1)}, f32[128,128,1,1,1]{1,0,4,3,2:T(8,128)}, u32[]{:S(2)}) copy-start(f32[128,128,1,1,1]{1,0,4,3,2:T(8,128)} %constant.56) | copy-start | bytes 196612
  4.7 0.7 copy-start.2
  8.1 15.9 %collective-permute-start = (bf16[2,2,1,2,9,16,128]{6,5,4,3,2,1,0:T(8,128)(2,1)}, bf16[2,2,1,2,9,16,128]{6,5,4,3,2,1,0:T(8,128)(2,1)}, u32[]{:S(2)}, u32[]{:S(2)}) collective-permute-start(bf16[2,2,1,2,9,16,128]{6,5,4,3,2,1,0:T(8,128)(2,1)} %constant_dynamic-slice_fusion.3), channel_id=1, source_target_pairs={{0,4},{4,0},{8,12},{12,8},{16,20},{20,16},{24,28},{28,24},{1,5},{5... | collective-permute-start | bytes 884744 | tf_op jit(solution)/shard_map/ppermute | solution.py:80
  8.1 11.4 %collective-permute-start.3 = (s32[16]{0:T(128)S(1)}, s32[16]{0:T(128)S(1)}, u32[]{:S(2)}, u32[]{:S(2)}) collective-permute-start(s32[16]{0:T(128)S(1)} %get-tuple-element.32), channel_id=1, source_target_pairs={{0,3},{1,0},{2,1},{3,2},{4,7},{5,4},{6,5},{7,6},{8,11},{9,8},{10,9... | collective-permute-start | bytes 200 | tf_op jit(solution)/shard_map/ppermute | solution.py:19
  8.1 11.9 %collective-permute-start.8 = (s32[16]{0:T(128)S(1)}, s32[16]{0:T(128)S(1)}, u32[]{:S(2)}, u32[]{:S(2)}) collective-permute-start(s32[16]{0:T(128)S(1)} %get-tuple-element.30), channel_id=1, source_target_pairs={{0,2},{1,3},{2,0},{3,1},{4,6},{5,7},{6,4},{7,5},{8,10},{9,11},{10,... | collective-permute-start | bytes 200 | tf_op jit(solution)/shard_map/ppermute | solution.py:19
  11.1 11.2 %collective-permute-start.13 = (s32[16]{0:T(128)S(1)}, s32[16]{0:T(128)S(1)}, u32[]{:S(2)}, u32[]{:S(2)}) collective-permute-start(s32[16]{0:T(128)S(1)} %get-tuple-element.35), channel_id=1, source_target_pairs={{0,1},{1,2},{2,3},{3,0},{4,5},{5,6},{6,7},{7,4},{8,9},{9,10},{10,1... | collective-permute-start | bytes 200 | tf_op jit(solution)/shard_map/ppermute | solution.py:19
  19.9 12.1 %collective-permute-start.4 = (bf16[2,16,6,8,128]{4,3,2,1,0:T(8,128)(2,1)S(1)}, bf16[2,16,6,8,128]{4,3,2,1,0:T(8,128)(2,1)S(1)}, u32[]{:S(2)}, u32[]{:S(2)}) collective-permute-start(bf16[2,16,6,8,128]{4,3,2,1,0:T(8,128)(2,1)S(1)} %bitcast.283), channel_id=1, source_target_pairs={{0,1},{1,2},{2,3},{3,0},{4,5},{5,6},{6,7},{7,4},{8,9},{9,10},{10,1... | collective-permute-start | bytes 1179656 | tf_op jit(solution)/shard_map/ppermute | solution.py:19
  20.3 33.4 %collective-permute-start.9 = (bf16[2,16,6,8,128]{4,3,2,1,0:T(8,128)(2,1)S(1)}, bf16[2,16,6,8,128]{4,3,2,1,0:T(8,128)(2,1)S(1)}, u32[]{:S(2)}, u32[]{:S(2)}) collective-permute-start(bf16[2,16,6,8,128]{4,3,2,1,0:T(8,128)(2,1)S(1)} %bitcast.282), channel_id=1, source_target_pairs={{0,2},{1,3},{2,0},{3,1},{4,6},{5,7},{6,4},{7,5},{8,10},{9,11},{10,... | collective-permute-start | bytes 1179656 | tf_op jit(solution)/shard_map/ppermute | solution.py:19
  22.7 33.1 %collective-permute-start.14 = (bf16[2,16,6,8,128]{4,3,2,1,0:T(8,128)(2,1)S(1)}, bf16[2,16,6,8,128]{4,3,2,1,0:T(8,128)(2,1)S(1)}, u32[]{:S(2)}, u32[]{:S(2)}) collective-permute-start(bf16[2,16,6,8,128]{4,3,2,1,0:T(8,128)(2,1)S(1)} %bitcast.281), channel_id=1, source_target_pairs={{0,3},{1,0},{2,1},{3,2},{4,7},{5,4},{6,5},{7,6},{8,11},{9,8},{10,9... | collective-permute-start | bytes 1179656 | tf_op jit(solution)/shard_map/ppermute | solution.py:19
  25.0 32.2 %collective-permute-start.1 = (bf16[2,1,1,2,9,16,128]{6,5,4,3,2,1,0:T(8,128)(2,1)S(1)}, bf16[2,1,1,2,9,16,128]{6,5,4,3,2,1,0:T(8,128)(2,1)S(1)}, u32[]{:S(2)}, u32[]{:S(2)}) collective-permute-start(bf16[2,1,1,2,9,16,128]{6,5,4,3,2,1,0:T(8,128)(2,1)S(1)} %dynamic-slice_convert_fusion.3), channel_id=1, source_target_pairs={{0,8},{4,12},{8,0},{12,4},{16,24},{20,28},{24,16},{28,20},{1,9},{5... | collective-permute-start | bytes 442376 | tf_op jit(solution)/shard_map/ppermute | solution.py:80
  32.6 1.0 %copy-start.1 = (f32[2,16,3,8,128]{4,3,2,1,0:T(8,128)S(1)}, f32[2,16,3,8,128]{4,3,2,1,0:T(8,128)}, u32[]{:S(2)}) copy-start(f32[2,16,3,8,128]{4,3,2,1,0:T(8,128)} %get-tuple-element.18) | copy-start | bytes 1179652
  34.0 42.0 %slice-start = ((s8[16777216]{0:T(1024)(128)(4,1)}), s8[4194304]{0:T(1024)(128)(4,1)S(1)}, s32[]{:S(2)}) async-start(s8[16777216]{0:T(1024)(128)(4,1)} %bitcast.245), calls=%async_computation | async-start | bytes 8388608
  34.2 27.5 %collective-permute-start.5 = (bf16[2,2,1,2,9,16,128]{6,5,4,3,2,1,0:T(8,128)(2,1)S(1)}, bf16[2,2,1,2,9,16,128]{6,5,4,3,2,1,0:T(8,128)(2,1)S(1)}, u32[]{:S(2)}, u32[]{:S(2)}) collective-permute-start(bf16[2,2,1,2,9,16,128]{6,5,4,3,2,1,0:T(8,128)(2,1)S(1)} %constant_dynamic-slice_fusion.2), channel_id=1, source_target_pairs={{0,4},{4,0},{8,12},{12,8},{16,20},{20,16},{24,28},{28,24},{1,5},{5... | collective-permute-start | bytes 884744 | tf_op jit(solution)/shard_map/ppermute | solution.py:80
  54.4 21.6 %slice-start.1 = ((s8[16777216]{0:T(1024)(128)(4,1)}), s8[4194304]{0:T(1024)(128)(4,1)S(1)}, s32[]{:S(2)}) async-start(s8[16777216]{0:T(1024)(128)(4,1)} %bitcast.245), calls=%async_computation.1 | async-start | bytes 8388608
  55.0 8.4 %collective-permute-start.10 = (bf16[2,2,1,2,9,16,128]{6,5,4,3,2,1,0:T(8,128)(2,1)S(1)}, bf16[2,2,1,2,9,16,128]{6,5,4,3,2,1,0:T(8,128)(2,1)S(1)}, u32[]{:S(2)}, u32[]{:S(2)}) collective-permute-start(bf16[2,2,1,2,9,16,128]{6,5,4,3,2,1,0:T(8,128)(2,1)S(1)} %constant_dynamic-slice_fusion.1), channel_id=1, source_target_pairs={{0,4},{4,0},{8,12},{12,8},{16,20},{20,16},{24,28},{28,24},{1,5},{5... | collective-permute-start | bytes 884744 | tf_op jit(solution)/shard_map/ppermute | solution.py:80
  56.4 19.6 %slice-start.2 = ((s8[16777216]{0:T(1024)(128)(4,1)}), s8[4194304]{0:T(1024)(128)(4,1)S(1)}, s32[]{:S(2)}) async-start(s8[16777216]{0:T(1024)(128)(4,1)} %bitcast.245), calls=%async_computation.2 | async-start | bytes 8388608
  57.2 4.4 %collective-permute-start.2 = (bf16[1,1,1,2,9,16,128]{6,5,4,3,2,1,0:T(8,128)(2,1)S(1)}, bf16[1,1,1,2,9,16,128]{6,5,4,3,2,1,0:T(8,128)(2,1)S(1)}, u32[]{:S(2)}, u32[]{:S(2)}) collective-permute-start(bf16[1,1,1,2,9,16,128]{6,5,4,3,2,1,0:T(8,128)(2,1)S(1)} %dynamic-slice_convert_fusion.7), channel_id=1, source_target_pairs={{0,16},{4,20},{8,24},{12,28},{16,0},{20,4},{24,8},{28,12},{1,17},{... | collective-permute-start | bytes 221192 | tf_op jit(solution)/shard_map/ppermute | solution.py:80
  58.8 6.2 %collective-permute-start.15 = (bf16[2,2,1,2,9,16,128]{6,5,4,3,2,1,0:T(8,128)(2,1)S(1)}, bf16[2,2,1,2,9,16,128]{6,5,4,3,2,1,0:T(8,128)(2,1)S(1)}, u32[]{:S(2)}, u32[]{:S(2)}) collective-permute-start(bf16[2,2,1,2,9,16,128]{6,5,4,3,2,1,0:T(8,128)(2,1)S(1)} %constant_dynamic-slice_fusion), channel_id=1, source_target_pairs={{0,4},{4,0},{8,12},{12,8},{16,20},{20,16},{24,28},{28,24},{1,5},{5... | collective-permute-start | bytes 884744 | tf_op jit(solution)/shard_map/ppermute | solution.py:80
  61.7 14.3 %slice-start.3 = ((s8[16777216]{0:T(1024)(128)(4,1)}), s8[4194304]{0:T(1024)(128)(4,1)S(1)}, s32[]{:S(2)}) async-start(s8[16777216]{0:T(1024)(128)(4,1)} %bitcast.245), calls=%async_computation.3 | async-start | bytes 8388608
  61.8 6.1 %collective-permute-start.6 = (bf16[1,2,1,2,9,16,128]{6,5,4,3,2,1,0:T(8,128)(2,1)S(1)}, bf16[1,2,1,2,9,16,128]{6,5,4,3,2,1,0:T(8,128)(2,1)S(1)}, u32[]{:S(2)}, u32[]{:S(2)}) collective-permute-start(bf16[1,2,1,2,9,16,128]{6,5,4,3,2,1,0:T(8,128)(2,1)S(1)} %dynamic-slice_convert_fusion.2), channel_id=1, source_target_pairs={{0,16},{4,20},{8,24},{12,28},{16,0},{20,4},{24,8},{28,12},{1,17},{... | collective-permute-start | bytes 442376 | tf_op jit(solution)/shard_map/ppermute | solution.py:80
  63.5 6.5 %collective-permute-start.11 = (bf16[2,1,1,2,9,16,128]{6,5,4,3,2,1,0:T(8,128)(2,1)S(1)}, bf16[2,1,1,2,9,16,128]{6,5,4,3,2,1,0:T(8,128)(2,1)S(1)}, u32[]{:S(2)}, u32[]{:S(2)}) collective-permute-start(bf16[2,1,1,2,9,16,128]{6,5,4,3,2,1,0:T(8,128)(2,1)S(1)} %dynamic-slice_convert_fusion.1), channel_id=1, source_target_pairs={{0,8},{4,12},{8,0},{12,4},{16,24},{20,28},{24,16},{28,20},{1,9},{5... | collective-permute-start | bytes 442376 | tf_op jit(solution)/shard_map/ppermute | solution.py:80
  65.2 6.2 %collective-permute-start.16 = (bf16[1,2,1,2,9,16,128]{6,5,4,3,2,1,0:T(8,128)(2,1)S(1)}, bf16[1,2,1,2,9,16,128]{6,5,4,3,2,1,0:T(8,128)(2,1)S(1)}, u32[]{:S(2)}, u32[]{:S(2)}) collective-permute-start(bf16[1,2,1,2,9,16,128]{6,5,4,3,2,1,0:T(8,128)(2,1)S(1)} %dynamic-slice_convert_fusion), channel_id=1, source_target_pairs={{0,16},{4,20},{8,24},{12,28},{16,0},{20,4},{24,8},{28,12},{1,17},{... | collective-permute-start | bytes 442376 | tf_op jit(solution)/shard_map/ppermute | solution.py:80
  68.0 5.0 %collective-permute-start.7 = (bf16[1,1,1,2,9,16,128]{6,5,4,3,2,1,0:T(8,128)(2,1)S(1)}, bf16[1,1,1,2,9,16,128]{6,5,4,3,2,1,0:T(8,128)(2,1)S(1)}, u32[]{:S(2)}, u32[]{:S(2)}) collective-permute-start(bf16[1,1,1,2,9,16,128]{6,5,4,3,2,1,0:T(8,128)(2,1)S(1)} %dynamic-slice_convert_fusion.6), channel_id=1, source_target_pairs={{0,8},{4,12},{8,0},{12,4},{16,24},{20,28},{24,16},{28,20},{1,9},{5... | collective-permute-start | bytes 221192 | tf_op jit(solution)/shard_map/ppermute | solution.py:80
  70.0 4.4 %collective-permute-start.12 = (bf16[1,1,1,2,9,16,128]{6,5,4,3,2,1,0:T(8,128)(2,1)S(1)}, bf16[1,1,1,2,9,16,128]{6,5,4,3,2,1,0:T(8,128)(2,1)S(1)}, u32[]{:S(2)}, u32[]{:S(2)}) collective-permute-start(bf16[1,1,1,2,9,16,128]{6,5,4,3,2,1,0:T(8,128)(2,1)S(1)} %dynamic-slice_convert_fusion.5), channel_id=1, source_target_pairs={{0,16},{4,20},{8,24},{12,28},{16,0},{20,4},{24,8},{28,12},{1,17},{... | collective-permute-start | bytes 221192 | tf_op jit(solution)/shard_map/ppermute | solution.py:80
  71.5 4.4 %collective-permute-start.17 = (bf16[1,1,1,2,9,16,128]{6,5,4,3,2,1,0:T(8,128)(2,1)S(1)}, bf16[1,1,1,2,9,16,128]{6,5,4,3,2,1,0:T(8,128)(2,1)S(1)}, u32[]{:S(2)}, u32[]{:S(2)}) collective-permute-start(bf16[1,1,1,2,9,16,128]{6,5,4,3,2,1,0:T(8,128)(2,1)S(1)} %dynamic-slice_convert_fusion.4), channel_id=1, source_target_pairs={{0,8},{4,12},{8,0},{12,4},{16,24},{20,28},{24,16},{28,20},{1,9},{5... | collective-permute-start | bytes 221192 | tf_op jit(solution)/shard_map/ppermute | solution.py:80

commit v5 on v4

--- a/solution.py
+++ b/solution.py
@@ -88,16 +88,19 @@
     hours_dev = spectra.shape[0]
     p_tile = pairs.shape[3]
     owned = p_tile // n_tm
-    asked = [pairs[0, 0, 1]] + [
-        shifted(pairs[0, step, 1], "sta", -step) for step in range(1, n_sta)
-    ]
-    visits = [pick(spectra, asked[0])] + [
-        shifted(pick(spectra, asked[step]), "sta", step) for step in range(1, n_sta)
+    asked = [None] + [shifted(pairs[0, step, 1], "sta", -step) for step in range(1, n_sta)]
+    own = [None] + [whiten(pick(spectra, pairs[0, step, 0])) for step in range(1, n_sta)]
+    asked, own = lax.optimization_barrier((asked, own))
+    picked = [pick(spectra, asked[step]) for step in range(1, n_sta)]
+    home, *picked = lax.optimization_barrier((pairs[0, 0], *picked))
+    own[0] = whiten(pick(spectra, home[0]))
+    visits = [pick(spectra, home[1])] + [
+        shifted(rows, "sta", step) for step, rows in enumerate(picked, 1)
     ]
 
     def reduce_tile(shift):
         limit = counts[0, shift]
-        value = cross(whiten(pick(spectra, pairs[0, shift, 0])), whiten(visits[shift]))
+        value = cross(own[shift], whiten(visits[shift]))
         slots = jnp.arange(p_tile, dtype=jnp.int32)
         value = jnp.where((slots < limit)[:, None, None, None], value, 0.0)
         return sum_at_owner(value.astype(jnp.bfloat16), "tm", shift)

time: 82.1 us -> 81.7 us (level)
  the two profiles are of different devices: /device:TPU:8 before, /device:TPU:0 now
where the time goes in v5:
time: 81.7 us; the launch traced here: 81.4 us
  waiting for transfers between devices  35.1 us (43%)
  starting transfers between devices  22.4 us (27%)
  matrix products  8.82 us (11%)
  local copies, waits for them, and re-layouts  7.41 us (9%)
  other arithmetic  6.82 us (8%)
    ppermute x6, waiting for transfers between devices, shifted(): return lax.ppermute(value, axis, pairs)  25.5 us
    ppermute x12, starting transfers between devices, sum_at_owner(): got = lax.ppermute(give.astype(jnp.bfloat16), axis, swap)  12 us
    ppermute x6, starting transfers between devices, shifted(): return lax.ppermute(value, axis, pairs)  10.4 us
    ppermute x12, waiting for transfers between devices, sum_at_owner(): got = lax.ppermute(give.astype(jnp.bfloat16), axis, swap)  9.67 us
    dot_general x8, matrix products, whiten(): jnp.dot(square, mean, precision=lax.Precision.HIGHEST, preferred_element_...  3.74 us
    dot_general x1, matrix products, per_device(): lagged = jnp.dot(rows, table, preferred_element_type=jnp.float32)  3.1 us
    lt x4, other arithmetic, reduce_tile(): value = jnp.where((slots < limit)[:, None, None, None], value, 0.0)  2.5 us
    dot_general x8, matrix products, pick(): jnp.einsum('hps,hsx->hpx', hot, flat, preferred_element_type=jnp.float32)  1.98 us
  transfers between devices with their start and end apart: 18, of which 8 were waited for; matrix products, arithmetic and copies ran while one was open for 19% of the time, Pallas kernels for 0%

profile of v5, /device:TPU:0, one launch (start us, length us, event | category | flops | bytes accessed | tf_op | source)
XLA Modules:
  0.0 81.4 jit_solution(9223951323757324949)
XLA Ops:
  0.0 0.8 slice_bitcast_fusion.29
  0.8 5.1 %collective-permute-start = (s32[16]{0:T(128)S(1)}, s32[16]{0:T(128)S(1)}, u32[]{:S(2)}, u32[]{:S(2)}) collective-permute-start(s32[16]{0:T(128)S(1)} %get-tuple-element.53), channel_id=1, source_target_pairs={{0,3},{1,0},{2,1},{3,2},{4,7},{5,4},{6,5},{7,6},{8,11},{9,8},{10,9... | collective-permute-start | bytes 200 | tf_op jit(solution)/shard_map/ppermute | solution.py:19
  5.8 1.0 %collective-permute-start.2 = (s32[16]{0:T(128)S(1)}, s32[16]{0:T(128)S(1)}, u32[]{:S(2)}, u32[]{:S(2)}) collective-permute-start(s32[16]{0:T(128)S(1)} %get-tuple-element.51), channel_id=1, source_target_pairs={{0,1},{1,2},{2,3},{3,0},{4,5},{5,6},{6,7},{7,4},{8,9},{9,10},{10,1... | collective-permute-start | bytes 200 | tf_op jit(solution)/shard_map/ppermute | solution.py:19
  6.9 0.7 slice_bitcast_fusion.26
  7.5 1.2 %copy.59 = bf16[2,6,4,8,1024]{4,3,1,2,0:T(8,128)(2,1)S(1)} copy(bf16[2,6,4,8,1024]{4,3,2,1,0:T(8,128)(2,1)} %bitcast.282) | data formatting | bytes 1572864 | tf_op jit(solution)/shard_map/reshape | solution.py:45
  8.8 0.2 fusion.4
  9.1 0.1 copy.60
  9.2 0.7 copy-done
  9.9 0.5 fusion.13
  10.4 0.1 multiply_convert_fusion.7
  10.5 0.2 fusion.3
  10.7 0.1 copy.61
  10.9 0.5 fusion.12
  11.5 0.2 fusion.2
  11.7 0.1 copy.62
  11.9 0.5 fusion.11
  12.6 0.6 fusion.82
  13.2 0.6 broadcast_compare_fusion
  13.8 0.6 broadcast_compare_fusion.1
  14.5 0.6 broadcast_compare_fusion.2
  15.0 0.7 broadcast_compare_fusion.3
  15.8 0.2 convolution_convert_fusion.4
  16.2 0.2 convolution_convert_fusion.3
  16.6 0.2 convolution_convert_fusion.2
  16.9 2.9 %collective-permute-start.14 = (bf16[2,16,6,8,128]{4,3,2,1,0:T(8,128)(2,1)S(1)}, bf16[2,16,6,8,128]{4,3,2,1,0:T(8,128)(2,1)S(1)}, u32[]{:S(2)}, u32[]{:S(2)}) collective-permute-start(bf16[2,16,6,8,128]{4,3,2,1,0:T(8,128)(2,1)S(1)} %bitcast.285), channel_id=1, source_target_pairs={{0,3},{1,0},{2,1},{3,2},{4,7},{5,4},{6,5},{7,6},{8,11},{9,8},{10,9... | collective-permute-start | bytes 1179656 | tf_op jit(solution)/shard_map/ppermute | solution.py:19
  19.9 1.2 %collective-permute-start.10 = (bf16[2,16,6,8,128]{4,3,2,1,0:T(8,128)(2,1)S(1)}, bf16[2,16,6,8,128]{4,3,2,1,0:T(8,128)(2,1)S(1)}, u32[]{:S(2)}, u32[]{:S(2)}) collective-permute-start(bf16[2,16,6,8,128]{4,3,2,1,0:T(8,128)(2,1)S(1)} %bitcast.284), channel_id=1, source_target_pairs={{0,2},{1,3},{2,0},{3,1},{4,6},{5,7},{6,4},{7,5},{8,10},{9,11},{10,... | collective-permute-start | bytes 1179656 | tf_op jit(solution)/shard_map/ppermute | solution.py:19
  21.2 0.2 fusion
  21.5 0.1 copy.67
  21.6 0.5 fusion.9
  22.3 0.2 fusion.1
  22.6 0.1 copy.66
  22.7 0.5 fusion.10
  23.4 0.4 add_reduce_fusion.3
  23.8 0.2 fusion.14
  24.1 0.2 collective-permute-start.6
  24.5 1.1 %collective-permute-done.3 = bf16[2,2,1,2,9,16,128]{6,5,4,3,2,1,0:T(8,128)(2,1)S(1)} collective-permute-done((bf16[2,2,1,2,9,16,128]{6,5,4,3,2,1,0:T(8,128)(2,1)S(1)}, bf16[2,2,1,2,9,16,128]{6,5,4,3,2,1,0:T(8,128)(2,1)S(1)}, u32[]{:S(2)}, u32[]{:S(2)}) %collective-permute-start.3) | collective-permute-done | bytes 294944 | tf_op jit(solution)/shard_map/ppermute | solution.py:80
  25.8 1.6 %collective-permute-start.4 = (bf16[2,1,1,2,9,16,128]{6,5,4,3,2,1,0:T(8,128)(2,1)S(1)}, bf16[2,1,1,2,9,16,128]{6,5,4,3,2,1,0:T(8,128)(2,1)S(1)}, u32[]{:S(2)}, u32[]{:S(2)}) collective-permute-start(bf16[2,1,1,2,9,16,128]{6,5,4,3,2,1,0:T(8,128)(2,1)S(1)} %dynamic-slice_convert_fusion.3), channel_id=1, source_target_pairs={{0,8},{4,12},{8,0},{12,4},{16,24},{20,28},{24,16},{28,20},{1,9},{5... | collective-permute-start | bytes 442376 | tf_op jit(solution)/shard_map/ppermute | solution.py:80
  27.3 2.0 %collective-permute-done.14 = bf16[2,16,6,8,128]{4,3,2,1,0:T(8,128)(2,1)S(1)} collective-permute-done((bf16[2,16,6,8,128]{4,3,2,1,0:T(8,128)(2,1)S(1)}, bf16[2,16,6,8,128]{4,3,2,1,0:T(8,128)(2,1)S(1)}, u32[]{:S(2)}, u32[]{:S(2)}) %collective-permute-start.14) | collective-permute-done | bytes 393248 | tf_op jit(solution)/shard_map/ppermute | solution.py:19
  29.4 0.5 fusion.6
  30.0 0.4 add_reduce_fusion
  30.4 0.2 fusion.17
  30.8 23.4 %collective-permute-done.10 = bf16[2,16,6,8,128]{4,3,2,1,0:T(8,128)(2,1)S(1)} collective-permute-done((bf16[2,16,6,8,128]{4,3,2,1,0:T(8,128)(2,1)S(1)}, bf16[2,16,6,8,128]{4,3,2,1,0:T(8,128)(2,1)S(1)}, u32[]{:S(2)}, u32[]{:S(2)}) %collective-permute-start.10) | collective-permute-done | bytes 393248 | tf_op jit(solution)/shard_map/ppermute | solution.py:19
  54.2 0.5 fusion.7
  54.9 0.4 add_reduce_fusion.1
  55.3 0.2 fusion.16
  55.7 0.5 fusion.8
  56.3 0.4 add_reduce_fusion.2
  56.7 0.2 fusion.15
  57.0 1.6 %collective-permute-start.5 = (bf16[1,1,1,2,9,16,128]{6,5,4,3,2,1,0:T(8,128)(2,1)S(1)}, bf16[1,1,1,2,9,16,128]{6,5,4,3,2,1,0:T(8,128)(2,1)S(1)}, u32[]{:S(2)}, u32[]{:S(2)}) collective-permute-start(bf16[1,1,1,2,9,16,128]{6,5,4,3,2,1,0:T(8,128)(2,1)S(1)} %dynamic-slice_convert_fusion.7), channel_id=1, source_target_pairs={{0,16},{4,20},{8,24},{12,28},{16,0},{20,4},{24,8},{28,12},{1,17},{... | collective-permute-start | bytes 221192 | tf_op jit(solution)/shard_map/ppermute | solution.py:80
  58.6 0.3 collective-permute-start.7
  58.8 2.8 %collective-permute-done.5 = bf16[1,1,1,2,9,16,128]{6,5,4,3,2,1,0:T(8,128)(2,1)S(1)} collective-permute-done((bf16[1,1,1,2,9,16,128]{6,5,4,3,2,1,0:T(8,128)(2,1)S(1)}, bf16[1,1,1,2,9,16,128]{6,5,4,3,2,1,0:T(8,128)(2,1)S(1)}, u32[]{:S(2)}, u32[]{:S(2)}) %collective-permute-start.5) | collective-permute-done | bytes 73760 | tf_op jit(solution)/shard_map/ppermute | solution.py:80
  61.9 1.6 %collective-permute-start.16 = (bf16[1,2,1,2,9,16,128]{6,5,4,3,2,1,0:T(8,128)(2,1)S(1)}, bf16[1,2,1,2,9,16,128]{6,5,4,3,2,1,0:T(8,128)(2,1)S(1)}, u32[]{:S(2)}, u32[]{:S(2)}) collective-permute-start(bf16[1,2,1,2,9,16,128]{6,5,4,3,2,1,0:T(8,128)(2,1)S(1)} %dynamic-slice_convert_fusion), channel_id=1, source_target_pairs={{0,16},{4,20},{8,24},{12,28},{16,0},{20,4},{24,8},{28,12},{1,17},{... | collective-permute-start | bytes 442376 | tf_op jit(solution)/shard_map/ppermute | solution.py:80
  63.6 1.6 %collective-permute-start.12 = (bf16[2,1,1,2,9,16,128]{6,5,4,3,2,1,0:T(8,128)(2,1)S(1)}, bf16[2,1,1,2,9,16,128]{6,5,4,3,2,1,0:T(8,128)(2,1)S(1)}, u32[]{:S(2)}, u32[]{:S(2)}) collective-permute-start(bf16[2,1,1,2,9,16,128]{6,5,4,3,2,1,0:T(8,128)(2,1)S(1)} %dynamic-slice_convert_fusion.1), channel_id=1, source_target_pairs={{0,8},{4,12},{8,0},{12,4},{16,24},{20,28},{24,16},{28,20},{1,9},{5... | collective-permute-start | bytes 442376 | tf_op jit(solution)/shard_map/ppermute | solution.py:80
  65.2 0.6 collective-permute-start.8
  65.8 1.9 %collective-permute-done.16 = bf16[1,2,1,2,9,16,128]{6,5,4,3,2,1,0:T(8,128)(2,1)S(1)} collective-permute-done((bf16[1,2,1,2,9,16,128]{6,5,4,3,2,1,0:T(8,128)(2,1)S(1)}, bf16[1,2,1,2,9,16,128]{6,5,4,3,2,1,0:T(8,128)(2,1)S(1)}, u32[]{:S(2)}, u32[]{:S(2)}) %collective-permute-start.16) | collective-permute-done | bytes 147488 | tf_op jit(solution)/shard_map/ppermute | solution.py:80
  67.8 2.5 %collective-permute-start.17 = (bf16[1,1,1,2,9,16,128]{6,5,4,3,2,1,0:T(8,128)(2,1)S(1)}, bf16[1,1,1,2,9,16,128]{6,5,4,3,2,1,0:T(8,128)(2,1)S(1)}, u32[]{:S(2)}, u32[]{:S(2)}) collective-permute-start(bf16[1,1,1,2,9,16,128]{6,5,4,3,2,1,0:T(8,128)(2,1)S(1)} %dynamic-slice_convert_fusion.4), channel_id=1, source_target_pairs={{0,8},{4,12},{8,0},{12,4},{16,24},{20,28},{24,16},{28,20},{1,9},{5... | collective-permute-start | bytes 221192 | tf_op jit(solution)/shard_map/ppermute | solution.py:80
  70.4 1.6 %collective-permute-start.13 = (bf16[1,1,1,2,9,16,128]{6,5,4,3,2,1,0:T(8,128)(2,1)S(1)}, bf16[1,1,1,2,9,16,128]{6,5,4,3,2,1,0:T(8,128)(2,1)S(1)}, u32[]{:S(2)}, u32[]{:S(2)}) collective-permute-start(bf16[1,1,1,2,9,16,128]{6,5,4,3,2,1,0:T(8,128)(2,1)S(1)} %dynamic-slice_convert_fusion.5), channel_id=1, source_target_pairs={{0,16},{4,20},{8,24},{12,28},{16,0},{20,4},{24,8},{28,12},{1,17},{... | collective-permute-start | bytes 221192 | tf_op jit(solution)/shard_map/ppermute | solution.py:80
  72.0 0.6 collective-permute-start.9
  72.6 0.8 collective-permute-done.17
  73.4 1.3 %collective-permute-done.13 = bf16[1,1,1,2,9,16,128]{6,5,4,3,2,1,0:T(8,128)(2,1)S(1)} collective-permute-done((bf16[1,1,1,2,9,16,128]{6,5,4,3,2,1,0:T(8,128)(2,1)S(1)}, bf16[1,1,1,2,9,16,128]{6,5,4,3,2,1,0:T(8,128)(2,1)S(1)}, u32[]{:S(2)}, u32[]{:S(2)}) %collective-permute-start.13) | collective-permute-done | bytes 73760 | tf_op jit(solution)/shard_map/ppermute | solution.py:80
  74.8 1.6 %collective-permute-done.9 = bf16[1,1,1,2,9,16,128]{6,5,4,3,2,1,0:T(8,128)(2,1)S(1)} collective-permute-done((bf16[1,1,1,2,9,16,128]{6,5,4,3,2,1,0:T(8,128)(2,1)S(1)}, bf16[1,1,1,2,9,16,128]{6,5,4,3,2,1,0:T(8,128)(2,1)S(1)}, u32[]{:S(2)}, u32[]{:S(2)}) %collective-permute-start.9) | collective-permute-done | bytes 73760 | tf_op jit(solution)/shard_map/ppermute | solution.py:80
  76.5 3.1 %fusion.5 = bf16[72,4001]{1,0:T(8,128)(2,1)S(1)} fusion(bf16[2048,4001]{1,0:T(8,128)(2,1)S(1)} %bitcast.248, bf16[9,8,16,128]{3,2,1,0:T(8,128)(2,1)S(1)} %bitcast.264), kind=kOutput, calls=%fused_computation.14 | convolution fusion | flops 1180519168 | bytes 17259152 | tf_op jit(solution)/shard_map/dot_general | solution.py:110
  79.6 0.3 reshape.335
  79.9 1.5 %copy.47 = bf16[1,4,2,9,4001]{4,2,3,1,0:T(2,128)(2,1)} copy(bf16[1,4,2,9,4001]{4,3,2,1,0:T(8,128)(2,1)S(1)} %reshape.335) | data formatting | bytes 1152288 | tf_op jit(solution)/shard_map/reshape | solution.py:112
  (83 shorter events, 3.2 us)
Async XLA Ops:
  0.8 14.9 %collective-permute-start = (s32[16]{0:T(128)S(1)}, s32[16]{0:T(128)S(1)}, u32[]{:S(2)}, u32[]{:S(2)}) collective-permute-start(s32[16]{0:T(128)S(1)} %get-tuple-element.53), channel_id=1, source_target_pairs={{0,3},{1,0},{2,1},{3,2},{4,7},{5,4},{6,5},{7,6},{8,11},{9,8},{10,9... | collective-permute-start | bytes 200 | tf_op jit(solution)/shard_map/ppermute | solution.py:19
  5.8 9.9 %collective-permute-start.1 = (s32[16]{0:T(128)S(1)}, s32[16]{0:T(128)S(1)}, u32[]{:S(2)}, u32[]{:S(2)}) collective-permute-start(s32[16]{0:T(128)S(1)} %get-tuple-element.52), channel_id=1, source_target_pairs={{0,2},{1,3},{2,0},{3,1},{4,6},{5,7},{6,4},{7,5},{8,10},{9,11},{10,... | collective-permute-start | bytes 200 | tf_op jit(solution)/shard_map/ppermute | solution.py:19
  5.8 9.9 %collective-permute-start.2 = (s32[16]{0:T(128)S(1)}, s32[16]{0:T(128)S(1)}, u32[]{:S(2)}, u32[]{:S(2)}) collective-permute-start(s32[16]{0:T(128)S(1)} %get-tuple-element.51), channel_id=1, source_target_pairs={{0,1},{1,2},{2,3},{3,0},{4,5},{5,6},{6,7},{7,4},{8,9},{9,10},{10,1... | collective-permute-start | bytes 200 | tf_op jit(solution)/shard_map/ppermute | solution.py:19
  9.1 0.8 %copy-start = (f32[128,128,1,1,1]{1,0,4,3,2:T(8,128)S(1)}, f32[128,128,1,1,1]{1,0,4,3,2:T(8,128)}, u32[]{:S(2)}) copy-start(f32[128,128,1,1,1]{1,0,4,3,2:T(8,128)} %constant.56) | copy-start | bytes 196612
  11.9 0.7 copy-start.1
  16.9 12.4 %collective-permute-start.14 = (bf16[2,16,6,8,128]{4,3,2,1,0:T(8,128)(2,1)S(1)}, bf16[2,16,6,8,128]{4,3,2,1,0:T(8,128)(2,1)S(1)}, u32[]{:S(2)}, u32[]{:S(2)}) collective-permute-start(bf16[2,16,6,8,128]{4,3,2,1,0:T(8,128)(2,1)S(1)} %bitcast.285), channel_id=1, source_target_pairs={{0,3},{1,0},{2,1},{3,2},{4,7},{5,4},{6,5},{7,6},{8,11},{9,8},{10,9... | collective-permute-start | bytes 1179656 | tf_op jit(solution)/shard_map/ppermute | solution.py:19
  19.9 34.3 %collective-permute-start.10 = (bf16[2,16,6,8,128]{4,3,2,1,0:T(8,128)(2,1)S(1)}, bf16[2,16,6,8,128]{4,3,2,1,0:T(8,128)(2,1)S(1)}, u32[]{:S(2)}, u32[]{:S(2)}) collective-permute-start(bf16[2,16,6,8,128]{4,3,2,1,0:T(8,128)(2,1)S(1)} %bitcast.284), channel_id=1, source_target_pairs={{0,2},{1,3},{2,0},{3,1},{4,6},{5,7},{6,4},{7,5},{8,10},{9,11},{10,... | collective-permute-start | bytes 1179656 | tf_op jit(solution)/shard_map/ppermute | solution.py:19
  24.0 1.6 %collective-permute-start.3 = (bf16[2,2,1,2,9,16,128]{6,5,4,3,2,1,0:T(8,128)(2,1)S(1)}, bf16[2,2,1,2,9,16,128]{6,5,4,3,2,1,0:T(8,128)(2,1)S(1)}, u32[]{:S(2)}, u32[]{:S(2)}) collective-permute-start(bf16[2,2,1,2,9,16,128]{6,5,4,3,2,1,0:T(8,128)(2,1)S(1)} %constant_dynamic-slice_fusion.3), channel_id=1, source_target_pairs={{0,4},{4,0},{8,12},{12,8},{16,20},{20,16},{24,28},{28,24},{1,5},{5... | collective-permute-start | bytes 884744 | tf_op jit(solution)/shard_map/ppermute | solution.py:80
  24.1 31.4 %collective-permute-start.6 = (bf16[2,16,6,8,128]{4,3,2,1,0:T(8,128)(2,1)S(1)}, bf16[2,16,6,8,128]{4,3,2,1,0:T(8,128)(2,1)S(1)}, u32[]{:S(2)}, u32[]{:S(2)}) collective-permute-start(bf16[2,16,6,8,128]{4,3,2,1,0:T(8,128)(2,1)S(1)} %bitcast.283), channel_id=1, source_target_pairs={{0,1},{1,2},{2,3},{3,0},{4,5},{5,6},{6,7},{7,4},{8,9},{9,10},{10,1... | collective-permute-start | bytes 1179656 | tf_op jit(solution)/shard_map/ppermute | solution.py:19
  25.8 31.1 %collective-permute-start.4 = (bf16[2,1,1,2,9,16,128]{6,5,4,3,2,1,0:T(8,128)(2,1)S(1)}, bf16[2,1,1,2,9,16,128]{6,5,4,3,2,1,0:T(8,128)(2,1)S(1)}, u32[]{:S(2)}, u32[]{:S(2)}) collective-permute-start(bf16[2,1,1,2,9,16,128]{6,5,4,3,2,1,0:T(8,128)(2,1)S(1)} %dynamic-slice_convert_fusion.3), channel_id=1, source_target_pairs={{0,8},{4,12},{8,0},{12,4},{16,24},{20,28},{24,16},{28,20},{1,9},{5... | collective-permute-start | bytes 442376 | tf_op jit(solution)/shard_map/ppermute | solution.py:80
  30.0 46.5 %slice-start = ((s8[16777216]{0:T(1024)(128)(4,1)}), s8[4194304]{0:T(1024)(128)(4,1)S(1)}, s32[]{:S(2)}) async-start(s8[16777216]{0:T(1024)(128)(4,1)} %bitcast.247), calls=%async_computation | async-start | bytes 8388608
  30.7 31.1 %collective-permute-start.15 = (bf16[2,2,1,2,9,16,128]{6,5,4,3,2,1,0:T(8,128)(2,1)S(1)}, bf16[2,2,1,2,9,16,128]{6,5,4,3,2,1,0:T(8,128)(2,1)S(1)}, u32[]{:S(2)}, u32[]{:S(2)}) collective-permute-start(bf16[2,2,1,2,9,16,128]{6,5,4,3,2,1,0:T(8,128)(2,1)S(1)} %constant_dynamic-slice_fusion), channel_id=1, source_target_pairs={{0,4},{4,0},{8,12},{12,8},{16,20},{20,16},{24,28},{28,24},{1,5},{5... | collective-permute-start | bytes 884744 | tf_op jit(solution)/shard_map/ppermute | solution.py:80
  54.8 21.7 %slice-start.1 = ((s8[16777216]{0:T(1024)(128)(4,1)}), s8[4194304]{0:T(1024)(128)(4,1)S(1)}, s32[]{:S(2)}) async-start(s8[16777216]{0:T(1024)(128)(4,1)} %bitcast.247), calls=%async_computation.1 | async-start | bytes 8388608
  55.5 7.9 %collective-permute-start.11 = (bf16[2,2,1,2,9,16,128]{6,5,4,3,2,1,0:T(8,128)(2,1)S(1)}, bf16[2,2,1,2,9,16,128]{6,5,4,3,2,1,0:T(8,128)(2,1)S(1)}, u32[]{:S(2)}, u32[]{:S(2)}) collective-permute-start(bf16[2,2,1,2,9,16,128]{6,5,4,3,2,1,0:T(8,128)(2,1)S(1)} %constant_dynamic-slice_fusion.1), channel_id=1, source_target_pairs={{0,4},{4,0},{8,12},{12,8},{16,20},{20,16},{24,28},{28,24},{1,5},{5... | collective-permute-start | bytes 884744 | tf_op jit(solution)/shard_map/ppermute | solution.py:80
  56.1 20.4 %slice-start.2 = ((s8[16777216]{0:T(1024)(128)(4,1)}), s8[4194304]{0:T(1024)(128)(4,1)S(1)}, s32[]{:S(2)}) async-start(s8[16777216]{0:T(1024)(128)(4,1)} %bitcast.247), calls=%async_computation.2 | async-start | bytes 8388608
  57.0 4.7 %collective-permute-start.5 = (bf16[1,1,1,2,9,16,128]{6,5,4,3,2,1,0:T(8,128)(2,1)S(1)}, bf16[1,1,1,2,9,16,128]{6,5,4,3,2,1,0:T(8,128)(2,1)S(1)}, u32[]{:S(2)}, u32[]{:S(2)}) collective-permute-start(bf16[1,1,1,2,9,16,128]{6,5,4,3,2,1,0:T(8,128)(2,1)S(1)} %dynamic-slice_convert_fusion.7), channel_id=1, source_target_pairs={{0,16},{4,20},{8,24},{12,28},{16,0},{20,4},{24,8},{28,12},{1,17},{... | collective-permute-start | bytes 221192 | tf_op jit(solution)/shard_map/ppermute | solution.py:80
  58.6 6.5 %collective-permute-start.7 = (bf16[2,2,1,2,9,16,128]{6,5,4,3,2,1,0:T(8,128)(2,1)S(1)}, bf16[2,2,1,2,9,16,128]{6,5,4,3,2,1,0:T(8,128)(2,1)S(1)}, u32[]{:S(2)}, u32[]{:S(2)}) collective-permute-start(bf16[2,2,1,2,9,16,128]{6,5,4,3,2,1,0:T(8,128)(2,1)S(1)} %constant_dynamic-slice_fusion.2), channel_id=1, source_target_pairs={{0,4},{4,0},{8,12},{12,8},{16,20},{20,16},{24,28},{28,24},{1,5},{5... | collective-permute-start | bytes 884744 | tf_op jit(solution)/shard_map/ppermute | solution.py:80
  61.7 14.8 %slice-start.3 = ((s8[16777216]{0:T(1024)(128)(4,1)}), s8[4194304]{0:T(1024)(128)(4,1)S(1)}, s32[]{:S(2)}) async-start(s8[16777216]{0:T(1024)(128)(4,1)} %bitcast.247), calls=%async_computation.3 | async-start | bytes 8388608
  61.9 5.9 %collective-permute-start.16 = (bf16[1,2,1,2,9,16,128]{6,5,4,3,2,1,0:T(8,128)(2,1)S(1)}, bf16[1,2,1,2,9,16,128]{6,5,4,3,2,1,0:T(8,128)(2,1)S(1)}, u32[]{:S(2)}, u32[]{:S(2)}) collective-permute-start(bf16[1,2,1,2,9,16,128]{6,5,4,3,2,1,0:T(8,128)(2,1)S(1)} %dynamic-slice_convert_fusion), channel_id=1, source_target_pairs={{0,16},{4,20},{8,24},{12,28},{16,0},{20,4},{24,8},{28,12},{1,17},{... | collective-permute-start | bytes 442376 | tf_op jit(solution)/shard_map/ppermute | solution.py:80
  63.6 6.7 %collective-permute-start.12 = (bf16[2,1,1,2,9,16,128]{6,5,4,3,2,1,0:T(8,128)(2,1)S(1)}, bf16[2,1,1,2,9,16,128]{6,5,4,3,2,1,0:T(8,128)(2,1)S(1)}, u32[]{:S(2)}, u32[]{:S(2)}) collective-permute-start(bf16[2,1,1,2,9,16,128]{6,5,4,3,2,1,0:T(8,128)(2,1)S(1)} %dynamic-slice_convert_fusion.1), channel_id=1, source_target_pairs={{0,8},{4,12},{8,0},{12,4},{16,24},{20,28},{24,16},{28,20},{1,9},{5... | collective-permute-start | bytes 442376 | tf_op jit(solution)/shard_map/ppermute | solution.py:80
  65.2 6.7 %collective-permute-start.8 = (bf16[1,2,1,2,9,16,128]{6,5,4,3,2,1,0:T(8,128)(2,1)S(1)}, bf16[1,2,1,2,9,16,128]{6,5,4,3,2,1,0:T(8,128)(2,1)S(1)}, u32[]{:S(2)}, u32[]{:S(2)}) collective-permute-start(bf16[1,2,1,2,9,16,128]{6,5,4,3,2,1,0:T(8,128)(2,1)S(1)} %dynamic-slice_convert_fusion.2), channel_id=1, source_target_pairs={{0,16},{4,20},{8,24},{12,28},{16,0},{20,4},{24,8},{28,12},{1,17},{... | collective-permute-start | bytes 442376 | tf_op jit(solution)/shard_map/ppermute | solution.py:80
  67.8 5.6 %collective-permute-start.17 = (bf16[1,1,1,2,9,16,128]{6,5,4,3,2,1,0:T(8,128)(2,1)S(1)}, bf16[1,1,1,2,9,16,128]{6,5,4,3,2,1,0:T(8,128)(2,1)S(1)}, u32[]{:S(2)}, u32[]{:S(2)}) collective-permute-start(bf16[1,1,1,2,9,16,128]{6,5,4,3,2,1,0:T(8,128)(2,1)S(1)} %dynamic-slice_convert_fusion.4), channel_id=1, source_target_pairs={{0,8},{4,12},{8,0},{12,4},{16,24},{20,28},{24,16},{28,20},{1,9},{5... | collective-permute-start | bytes 221192 | tf_op jit(solution)/shard_map/ppermute | solution.py:80
  70.4 4.4 %collective-permute-start.13 = (bf16[1,1,1,2,9,16,128]{6,5,4,3,2,1,0:T(8,128)(2,1)S(1)}, bf16[1,1,1,2,9,16,128]{6,5,4,3,2,1,0:T(8,128)(2,1)S(1)}, u32[]{:S(2)}, u32[]{:S(2)}) collective-permute-start(bf16[1,1,1,2,9,16,128]{6,5,4,3,2,1,0:T(8,128)(2,1)S(1)} %dynamic-slice_convert_fusion.5), channel_id=1, source_target_pairs={{0,16},{4,20},{8,24},{12,28},{16,0},{20,4},{24,8},{28,12},{1,17},{... | collective-permute-start | bytes 221192 | tf_op jit(solution)/shard_map/ppermute | solution.py:80
  72.0 4.4 %collective-permute-start.9 = (bf16[1,1,1,2,9,16,128]{6,5,4,3,2,1,0:T(8,128)(2,1)S(1)}, bf16[1,1,1,2,9,16,128]{6,5,4,3,2,1,0:T(8,128)(2,1)S(1)}, u32[]{:S(2)}, u32[]{:S(2)}) collective-permute-start(bf16[1,1,1,2,9,16,128]{6,5,4,3,2,1,0:T(8,128)(2,1)S(1)} %dynamic-slice_convert_fusion.6), channel_id=1, source_target_pairs={{0,8},{4,12},{8,0},{12,4},{16,24},{20,28},{24,16},{28,20},{1,9},{5... | collective-permute-start | bytes 221192 | tf_op jit(solution)/shard_map/ppermute | solution.py:80

commit v6 on v5

--- a/solution.py
+++ b/solution.py
@@ -105,7 +105,14 @@
         value = jnp.where((slots < limit)[:, None, None, None], value, 0.0)
         return sum_at_owner(value.astype(jnp.bfloat16), "tm", shift)
 
-    reduced = [reduce_tile(shift) for shift in range(n_sta)]
+    early = sorted({0, n_sta - 1})
+    reduced = {shift: reduce_tile(shift) for shift in early}
+    late = [shift for shift in range(n_sta) if shift not in early]
+    reduced, arrived = lax.optimization_barrier((reduced, [visits[shift] for shift in late]))
+    for shift, rows in zip(late, arrived):
+        visits[shift] = rows
+        reduced[shift] = reduce_tile(shift)
+    reduced = [reduced[shift] for shift in range(n_sta)]
     rows = jnp.stack(reduced, axis=0).astype(jnp.bfloat16).reshape(n_sta * owned * 9, 2 * NF)
     lagged = jnp.dot(rows, table, preferred_element_type=jnp.float32)
     scale = 1.0 / math.sqrt(hours_dev * n_tm * NF)

time: 81.7 us -> 80 us (0.979)
  the two profiles are of different devices: /device:TPU:0 before, /device:TPU:8 now
where the time goes in v6:
time: 80 us; the launch traced here: 79.7 us
  waiting for transfers between devices  32.6 us (41%)
  starting transfers between devices  23.2 us (29%)
  matrix products  8.81 us (11%)
  local copies, waits for them, and re-layouts  7.43 us (9%)
  other arithmetic  6.9 us (9%)
    ppermute x6, waiting for transfers between devices, shifted(): return lax.ppermute(value, axis, pairs)  20.7 us
    ppermute x12, starting transfers between devices, sum_at_owner(): got = lax.ppermute(give.astype(jnp.bfloat16), axis, swap)  12.7 us
    ppermute x12, waiting for transfers between devices, sum_at_owner(): got = lax.ppermute(give.astype(jnp.bfloat16), axis, swap)  11.9 us
    ppermute x6, starting transfers between devices, shifted(): return lax.ppermute(value, axis, pairs)  10.5 us
    dot_general x8, matrix products, whiten(): jnp.dot(square, mean, precision=lax.Precision.HIGHEST, preferred_element_...  3.73 us
    dot_general x1, matrix products, per_device(): lagged = jnp.dot(rows, table, preferred_element_type=jnp.float32)  3.1 us
    lt x4, other arithmetic, reduce_tile(): value = jnp.where((slots < limit)[:, None, None, None], value, 0.0)  2.5 us
    dot_general x8, matrix products, pick(): jnp.einsum('hps,hsx->hpx', hot, flat, preferred_element_type=jnp.float32)  1.98 us
  transfers between devices with their start and end apart: 18, of which 7 were waited for; matrix products, arithmetic and copies ran while one was open for 18% of the time, Pallas kernels for 0%

profile of v6, /device:TPU:8, one launch (start us, length us, event | category | flops | bytes accessed | tf_op | source)
XLA Modules:
  0.0 79.7 jit_solution(7121425986488282299)
XLA Ops:
  0.0 0.8 slice_bitcast_fusion.29
  0.8 3.0 %collective-permute-start.1 = (s32[16]{0:T(128)S(1)}, s32[16]{0:T(128)S(1)}, u32[]{:S(2)}, u32[]{:S(2)}) collective-permute-start(s32[16]{0:T(128)S(1)} %get-tuple-element.60), channel_id=1, source_target_pairs={{0,2},{1,3},{2,0},{3,1},{4,6},{5,7},{6,4},{7,5},{8,10},{9,11},{10,... | collective-permute-start | bytes 200 | tf_op jit(solution)/shard_map/ppermute | solution.py:19
  3.8 2.5 %collective-permute-start.2 = (s32[16]{0:T(128)S(1)}, s32[16]{0:T(128)S(1)}, u32[]{:S(2)}, u32[]{:S(2)}) collective-permute-start(s32[16]{0:T(128)S(1)} %get-tuple-element.59), channel_id=1, source_target_pairs={{0,1},{1,2},{2,3},{3,0},{4,5},{5,6},{6,7},{7,4},{8,9},{9,10},{10,1... | collective-permute-start | bytes 200 | tf_op jit(solution)/shard_map/ppermute | solution.py:19
  6.3 0.7 slice_bitcast_fusion.26
  7.0 1.2 %copy.59 = bf16[2,6,4,8,1024]{4,3,1,2,0:T(8,128)(2,1)S(1)} copy(bf16[2,6,4,8,1024]{4,3,2,1,0:T(8,128)(2,1)} %bitcast.288) | data formatting | bytes 1572864 | tf_op jit(solution)/shard_map/reshape | solution.py:45
  8.3 0.2 fusion.3
  8.5 0.1 copy.61
  8.7 0.7 copy-done
  9.4 0.5 fusion.12
  9.9 0.2 fusion.4
  10.2 0.1 copy.60
  10.3 0.5 fusion.13
  11.0 0.2 fusion.2
  11.2 0.1 copy.62
  11.4 0.5 fusion.11
  12.0 0.6 fusion.80
  12.6 0.6 broadcast_compare_fusion.2
  13.2 0.6 broadcast_compare_fusion.3
  13.8 0.7 broadcast_compare_fusion.1
  14.5 0.6 broadcast_compare_fusion
  15.3 0.2 convolution_convert_fusion.3
  15.7 0.2 convolution_convert_fusion.2
  16.1 0.2 convolution_convert_fusion.4
  16.7 0.2 fusion.1
  16.9 0.1 copy.66
  17.0 0.5 fusion.10
  17.5 0.1 fusion.18
  17.8 0.2 fusion
  18.0 0.1 copy.67
  18.2 0.5 fusion.9
  18.6 0.1 fusion.19
  18.8 0.4 add_reduce_fusion.3
  19.2 0.2 fusion.14
  19.5 2.3 %collective-permute-start.10 = (bf16[2,16,6,8,128]{4,3,2,1,0:T(8,128)(2,1)S(1)}, bf16[2,16,6,8,128]{4,3,2,1,0:T(8,128)(2,1)S(1)}, u32[]{:S(2)}, u32[]{:S(2)}) collective-permute-start(bf16[2,16,6,8,128]{4,3,2,1,0:T(8,128)(2,1)S(1)} %bitcast.290), channel_id=1, source_target_pairs={{0,1},{1,2},{2,3},{3,0},{4,5},{5,6},{6,7},{7,4},{8,9},{9,10},{10,1... | collective-permute-start | bytes 1179656 | tf_op jit(solution)/shard_map/ppermute | solution.py:19
  21.8 2.7 %collective-permute-start.11 = (bf16[2,16,6,8,128]{4,3,2,1,0:T(8,128)(2,1)S(1)}, bf16[2,16,6,8,128]{4,3,2,1,0:T(8,128)(2,1)S(1)}, u32[]{:S(2)}, u32[]{:S(2)}) collective-permute-start(bf16[2,16,6,8,128]{4,3,2,1,0:T(8,128)(2,1)S(1)} %bitcast.289), channel_id=1, source_target_pairs={{0,2},{1,3},{2,0},{3,1},{4,6},{5,7},{6,4},{7,5},{8,10},{9,11},{10,... | collective-permute-start | bytes 1179656 | tf_op jit(solution)/shard_map/ppermute | solution.py:19
  24.7 20.6 %collective-permute-done.6 = bf16[2,16,6,8,128]{4,3,2,1,0:T(8,128)(2,1)S(1)} collective-permute-done((bf16[2,16,6,8,128]{4,3,2,1,0:T(8,128)(2,1)S(1)}, bf16[2,16,6,8,128]{4,3,2,1,0:T(8,128)(2,1)S(1)}, u32[]{:S(2)}, u32[]{:S(2)}) %collective-permute-start.6) | collective-permute-done | bytes 393248 | tf_op jit(solution)/shard_map/ppermute | solution.py:19
  45.4 0.5 fusion.8
  45.9 0.1 fusion.20
  46.0 0.4 add_reduce_fusion.2
  46.4 0.2 fusion.15
  46.9 1.6 %collective-permute-start.4 = (bf16[2,1,1,2,9,16,128]{6,5,4,3,2,1,0:T(8,128)(2,1)S(1)}, bf16[2,1,1,2,9,16,128]{6,5,4,3,2,1,0:T(8,128)(2,1)S(1)}, u32[]{:S(2)}, u32[]{:S(2)}) collective-permute-start(bf16[2,1,1,2,9,16,128]{6,5,4,3,2,1,0:T(8,128)(2,1)S(1)} %dynamic-slice_convert_fusion.3), channel_id=1, source_target_pairs={{0,8},{4,12},{8,0},{12,4},{16,24},{20,28},{24,16},{28,20},{1,9},{5... | collective-permute-start | bytes 442376 | tf_op jit(solution)/shard_map/ppermute | solution.py:80
  48.5 1.6 %collective-permute-start.8 = (bf16[1,2,1,2,9,16,128]{6,5,4,3,2,1,0:T(8,128)(2,1)S(1)}, bf16[1,2,1,2,9,16,128]{6,5,4,3,2,1,0:T(8,128)(2,1)S(1)}, u32[]{:S(2)}, u32[]{:S(2)}) collective-permute-start(bf16[1,2,1,2,9,16,128]{6,5,4,3,2,1,0:T(8,128)(2,1)S(1)} %dynamic-slice_convert_fusion.2), channel_id=1, source_target_pairs={{0,16},{4,20},{8,24},{12,28},{16,0},{20,4},{24,8},{28,12},{1,17},{... | collective-permute-start | bytes 442376 | tf_op jit(solution)/shard_map/ppermute | solution.py:80
  50.1 3.0 %collective-permute-done.4 = bf16[2,1,1,2,9,16,128]{6,5,4,3,2,1,0:T(8,128)(2,1)S(1)} collective-permute-done((bf16[2,1,1,2,9,16,128]{6,5,4,3,2,1,0:T(8,128)(2,1)S(1)}, bf16[2,1,1,2,9,16,128]{6,5,4,3,2,1,0:T(8,128)(2,1)S(1)}, u32[]{:S(2)}, u32[]{:S(2)}) %collective-permute-start.4) | collective-permute-done | bytes 147488 | tf_op jit(solution)/shard_map/ppermute | solution.py:80
  53.2 1.5 %collective-permute-start.5 = (bf16[1,1,1,2,9,16,128]{6,5,4,3,2,1,0:T(8,128)(2,1)S(1)}, bf16[1,1,1,2,9,16,128]{6,5,4,3,2,1,0:T(8,128)(2,1)S(1)}, u32[]{:S(2)}, u32[]{:S(2)}) collective-permute-start(bf16[1,1,1,2,9,16,128]{6,5,4,3,2,1,0:T(8,128)(2,1)S(1)} %dynamic-slice_convert_fusion.7), channel_id=1, source_target_pairs={{0,16},{4,20},{8,24},{12,28},{16,0},{20,4},{24,8},{28,12},{1,17},{... | collective-permute-start | bytes 221192 | tf_op jit(solution)/shard_map/ppermute | solution.py:80
  54.8 1.6 %collective-permute-start.9 = (bf16[1,1,1,2,9,16,128]{6,5,4,3,2,1,0:T(8,128)(2,1)S(1)}, bf16[1,1,1,2,9,16,128]{6,5,4,3,2,1,0:T(8,128)(2,1)S(1)}, u32[]{:S(2)}, u32[]{:S(2)}) collective-permute-start(bf16[1,1,1,2,9,16,128]{6,5,4,3,2,1,0:T(8,128)(2,1)S(1)} %dynamic-slice_convert_fusion.6), channel_id=1, source_target_pairs={{0,8},{4,12},{8,0},{12,4},{16,24},{20,28},{24,16},{28,20},{1,9},{5... | collective-permute-start | bytes 221192 | tf_op jit(solution)/shard_map/ppermute | solution.py:80
  56.4 1.2 %collective-permute-done.5 = bf16[1,1,1,2,9,16,128]{6,5,4,3,2,1,0:T(8,128)(2,1)S(1)} collective-permute-done((bf16[1,1,1,2,9,16,128]{6,5,4,3,2,1,0:T(8,128)(2,1)S(1)}, bf16[1,1,1,2,9,16,128]{6,5,4,3,2,1,0:T(8,128)(2,1)S(1)}, u32[]{:S(2)}, u32[]{:S(2)}) %collective-permute-start.5) | collective-permute-done | bytes 73760 | tf_op jit(solution)/shard_map/ppermute | solution.py:80
  57.7 1.6 %collective-permute-done.9 = bf16[1,1,1,2,9,16,128]{6,5,4,3,2,1,0:T(8,128)(2,1)S(1)} collective-permute-done((bf16[1,1,1,2,9,16,128]{6,5,4,3,2,1,0:T(8,128)(2,1)S(1)}, bf16[1,1,1,2,9,16,128]{6,5,4,3,2,1,0:T(8,128)(2,1)S(1)}, u32[]{:S(2)}, u32[]{:S(2)}) %collective-permute-start.9) | collective-permute-done | bytes 73760 | tf_op jit(solution)/shard_map/ppermute | solution.py:80
  59.4 0.5 fusion.7
  60.0 0.4 add_reduce_fusion.1
  60.4 0.2 fusion.16
  60.8 0.5 fusion.6
  61.4 0.4 add_reduce_fusion
  61.8 0.2 fusion.17
  62.1 0.6 collective-permute-start.15
  62.7 1.4 %collective-permute-start.13 = (bf16[1,2,1,2,9,16,128]{6,5,4,3,2,1,0:T(8,128)(2,1)S(1)}, bf16[1,2,1,2,9,16,128]{6,5,4,3,2,1,0:T(8,128)(2,1)S(1)}, u32[]{:S(2)}, u32[]{:S(2)}) collective-permute-start(bf16[1,2,1,2,9,16,128]{6,5,4,3,2,1,0:T(8,128)(2,1)S(1)} %dynamic-slice_convert_fusion.1), channel_id=1, source_target_pairs={{0,16},{4,20},{8,24},{12,28},{16,0},{20,4},{24,8},{28,12},{1,17},{... | collective-permute-start | bytes 442376 | tf_op jit(solution)/shard_map/ppermute | solution.py:80
  64.2 1.4 %collective-permute-start.16 = (bf16[2,1,1,2,9,16,128]{6,5,4,3,2,1,0:T(8,128)(2,1)S(1)}, bf16[2,1,1,2,9,16,128]{6,5,4,3,2,1,0:T(8,128)(2,1)S(1)}, u32[]{:S(2)}, u32[]{:S(2)}) collective-permute-start(bf16[2,1,1,2,9,16,128]{6,5,4,3,2,1,0:T(8,128)(2,1)S(1)} %dynamic-slice_convert_fusion), channel_id=1, source_target_pairs={{0,8},{4,12},{8,0},{12,4},{16,24},{20,28},{24,16},{28,20},{1,9},{5... | collective-permute-start | bytes 442376 | tf_op jit(solution)/shard_map/ppermute | solution.py:80
  65.6 3.0 %collective-permute-done.13 = bf16[1,2,1,2,9,16,128]{6,5,4,3,2,1,0:T(8,128)(2,1)S(1)} collective-permute-done((bf16[1,2,1,2,9,16,128]{6,5,4,3,2,1,0:T(8,128)(2,1)S(1)}, bf16[1,2,1,2,9,16,128]{6,5,4,3,2,1,0:T(8,128)(2,1)S(1)}, u32[]{:S(2)}, u32[]{:S(2)}) %collective-permute-start.13) | collective-permute-done | bytes 147488 | tf_op jit(solution)/shard_map/ppermute | solution.py:80
  68.6 1.6 %collective-permute-start.14 = (bf16[1,1,1,2,9,16,128]{6,5,4,3,2,1,0:T(8,128)(2,1)S(1)}, bf16[1,1,1,2,9,16,128]{6,5,4,3,2,1,0:T(8,128)(2,1)S(1)}, u32[]{:S(2)}, u32[]{:S(2)}) collective-permute-start(bf16[1,1,1,2,9,16,128]{6,5,4,3,2,1,0:T(8,128)(2,1)S(1)} %dynamic-slice_convert_fusion.5), channel_id=1, source_target_pairs={{0,8},{4,12},{8,0},{12,4},{16,24},{20,28},{24,16},{28,20},{1,9},{5... | collective-permute-start | bytes 221192 | tf_op jit(solution)/shard_map/ppermute | solution.py:80
  70.3 1.3 %collective-permute-start.17 = (bf16[1,1,1,2,9,16,128]{6,5,4,3,2,1,0:T(8,128)(2,1)S(1)}, bf16[1,1,1,2,9,16,128]{6,5,4,3,2,1,0:T(8,128)(2,1)S(1)}, u32[]{:S(2)}, u32[]{:S(2)}) collective-permute-start(bf16[1,1,1,2,9,16,128]{6,5,4,3,2,1,0:T(8,128)(2,1)S(1)} %dynamic-slice_convert_fusion.4), channel_id=1, source_target_pairs={{0,16},{4,20},{8,24},{12,28},{16,0},{20,4},{24,8},{28,12},{1,17},{... | collective-permute-start | bytes 221192 | tf_op jit(solution)/shard_map/ppermute | solution.py:80
  71.6 1.5 %collective-permute-done.14 = bf16[1,1,1,2,9,16,128]{6,5,4,3,2,1,0:T(8,128)(2,1)S(1)} collective-permute-done((bf16[1,1,1,2,9,16,128]{6,5,4,3,2,1,0:T(8,128)(2,1)S(1)}, bf16[1,1,1,2,9,16,128]{6,5,4,3,2,1,0:T(8,128)(2,1)S(1)}, u32[]{:S(2)}, u32[]{:S(2)}) %collective-permute-start.14) | collective-permute-done | bytes 73760 | tf_op jit(solution)/shard_map/ppermute | solution.py:80
  73.1 1.7 %collective-permute-done.17 = bf16[1,1,1,2,9,16,128]{6,5,4,3,2,1,0:T(8,128)(2,1)S(1)} collective-permute-done((bf16[1,1,1,2,9,16,128]{6,5,4,3,2,1,0:T(8,128)(2,1)S(1)}, bf16[1,1,1,2,9,16,128]{6,5,4,3,2,1,0:T(8,128)(2,1)S(1)}, u32[]{:S(2)}, u32[]{:S(2)}) %collective-permute-start.17) | collective-permute-done | bytes 73760 | tf_op jit(solution)/shard_map/ppermute | solution.py:80
  74.9 3.1 %fusion.5 = bf16[72,4001]{1,0:T(8,128)(2,1)S(1)} fusion(bf16[2048,4001]{1,0:T(8,128)(2,1)S(1)} %bitcast.254, bf16[9,8,16,128]{3,2,1,0:T(8,128)(2,1)S(1)} %bitcast.270), kind=kOutput, calls=%fused_computation.14 | convolution fusion | flops 1180519168 | bytes 17259152 | tf_op jit(solution)/shard_map/dot_general | solution.py:117
  78.0 0.3 reshape.343
  78.3 1.5 %copy.47 = bf16[1,4,2,9,4001]{4,2,3,1,0:T(2,128)(2,1)} copy(bf16[1,4,2,9,4001]{4,3,2,1,0:T(8,128)(2,1)S(1)} %reshape.343) | data formatting | bytes 1152288 | tf_op jit(solution)/shard_map/reshape | solution.py:119
  (83 shorter events, 3.1 us)
Async XLA Ops:
  0.8 14.4 %collective-permute-start = (s32[16]{0:T(128)S(1)}, s32[16]{0:T(128)S(1)}, u32[]{:S(2)}, u32[]{:S(2)}) collective-permute-start(s32[16]{0:T(128)S(1)} %get-tuple-element.61), channel_id=1, source_target_pairs={{0,3},{1,0},{2,1},{3,2},{4,7},{5,4},{6,5},{7,6},{8,11},{9,8},{10,9... | collective-permute-start | bytes 200 | tf_op jit(solution)/shard_map/ppermute | solution.py:19
  0.8 14.4 %collective-permute-start.1 = (s32[16]{0:T(128)S(1)}, s32[16]{0:T(128)S(1)}, u32[]{:S(2)}, u32[]{:S(2)}) collective-permute-start(s32[16]{0:T(128)S(1)} %get-tuple-element.60), channel_id=1, source_target_pairs={{0,2},{1,3},{2,0},{3,1},{4,6},{5,7},{6,4},{7,5},{8,10},{9,11},{10,... | collective-permute-start | bytes 200 | tf_op jit(solution)/shard_map/ppermute | solution.py:19
  3.8 11.4 %collective-permute-start.2 = (s32[16]{0:T(128)S(1)}, s32[16]{0:T(128)S(1)}, u32[]{:S(2)}, u32[]{:S(2)}) collective-permute-start(s32[16]{0:T(128)S(1)} %get-tuple-element.59), channel_id=1, source_target_pairs={{0,1},{1,2},{2,3},{3,0},{4,5},{5,6},{6,7},{7,4},{8,9},{9,10},{10,1... | collective-permute-start | bytes 200 | tf_op jit(solution)/shard_map/ppermute | solution.py:19
  8.5 0.8 %copy-start = (f32[128,128,1,1,1]{1,0,4,3,2:T(8,128)S(1)}, f32[128,128,1,1,1]{1,0,4,3,2:T(8,128)}, u32[]{:S(2)}) copy-start(f32[128,128,1,1,1]{1,0,4,3,2:T(8,128)} %constant.56) | copy-start | bytes 196612
  11.4 0.7 copy-start.1
  16.4 29.0 %collective-permute-start.6 = (bf16[2,16,6,8,128]{4,3,2,1,0:T(8,128)(2,1)S(1)}, bf16[2,16,6,8,128]{4,3,2,1,0:T(8,128)(2,1)S(1)}, u32[]{:S(2)}, u32[]{:S(2)}) collective-permute-start(bf16[2,16,6,8,128]{4,3,2,1,0:T(8,128)(2,1)S(1)} %bitcast.291), channel_id=1, source_target_pairs={{0,3},{1,0},{2,1},{3,2},{4,7},{5,4},{6,5},{7,6},{8,11},{9,8},{10,9... | collective-permute-start | bytes 1179656 | tf_op jit(solution)/shard_map/ppermute | solution.py:19
  19.4 27.3 %collective-permute-start.3 = (bf16[2,2,1,2,9,16,128]{6,5,4,3,2,1,0:T(8,128)(2,1)S(1)}, bf16[2,2,1,2,9,16,128]{6,5,4,3,2,1,0:T(8,128)(2,1)S(1)}, u32[]{:S(2)}, u32[]{:S(2)}) collective-permute-start(bf16[2,2,1,2,9,16,128]{6,5,4,3,2,1,0:T(8,128)(2,1)S(1)} %constant_dynamic-slice_fusion.3), channel_id=1, source_target_pairs={{0,4},{4,0},{8,12},{12,8},{16,20},{20,16},{24,28},{28,24},{1,5},{5... | collective-permute-start | bytes 884744 | tf_op jit(solution)/shard_map/ppermute | solution.py:80
  19.5 39.7 %collective-permute-start.10 = (bf16[2,16,6,8,128]{4,3,2,1,0:T(8,128)(2,1)S(1)}, bf16[2,16,6,8,128]{4,3,2,1,0:T(8,128)(2,1)S(1)}, u32[]{:S(2)}, u32[]{:S(2)}) collective-permute-start(bf16[2,16,6,8,128]{4,3,2,1,0:T(8,128)(2,1)S(1)} %bitcast.290), channel_id=1, source_target_pairs={{0,1},{1,2},{2,3},{3,0},{4,5},{5,6},{6,7},{7,4},{8,9},{9,10},{10,1... | collective-permute-start | bytes 1179656 | tf_op jit(solution)/shard_map/ppermute | solution.py:19
  21.8 37.5 %collective-permute-start.11 = (bf16[2,16,6,8,128]{4,3,2,1,0:T(8,128)(2,1)S(1)}, bf16[2,16,6,8,128]{4,3,2,1,0:T(8,128)(2,1)S(1)}, u32[]{:S(2)}, u32[]{:S(2)}) collective-permute-start(bf16[2,16,6,8,128]{4,3,2,1,0:T(8,128)(2,1)S(1)} %bitcast.289), channel_id=1, source_target_pairs={{0,2},{1,3},{2,0},{3,1},{4,6},{5,7},{6,4},{7,5},{8,10},{9,11},{10,... | collective-permute-start | bytes 1179656 | tf_op jit(solution)/shard_map/ppermute | solution.py:19
  46.4 28.4 %slice-start = ((s8[16777216]{0:T(1024)(128)(4,1)}), s8[4194304]{0:T(1024)(128)(4,1)S(1)}, s32[]{:S(2)}) async-start(s8[16777216]{0:T(1024)(128)(4,1)} %bitcast.253), calls=%async_computation | async-start | bytes 8388608
  46.7 1.8 %collective-permute-start.7 = (bf16[2,2,1,2,9,16,128]{6,5,4,3,2,1,0:T(8,128)(2,1)S(1)}, bf16[2,2,1,2,9,16,128]{6,5,4,3,2,1,0:T(8,128)(2,1)S(1)}, u32[]{:S(2)}, u32[]{:S(2)}) collective-permute-start(bf16[2,2,1,2,9,16,128]{6,5,4,3,2,1,0:T(8,128)(2,1)S(1)} %constant_dynamic-slice_fusion.2), channel_id=1, source_target_pairs={{0,4},{4,0},{8,12},{12,8},{16,20},{20,16},{24,28},{28,24},{1,5},{5... | collective-permute-start | bytes 884744 | tf_op jit(solution)/shard_map/ppermute | solution.py:80
  46.9 6.3 %collective-permute-start.4 = (bf16[2,1,1,2,9,16,128]{6,5,4,3,2,1,0:T(8,128)(2,1)S(1)}, bf16[2,1,1,2,9,16,128]{6,5,4,3,2,1,0:T(8,128)(2,1)S(1)}, u32[]{:S(2)}, u32[]{:S(2)}) collective-permute-start(bf16[2,1,1,2,9,16,128]{6,5,4,3,2,1,0:T(8,128)(2,1)S(1)} %dynamic-slice_convert_fusion.3), channel_id=1, source_target_pairs={{0,8},{4,12},{8,0},{12,4},{16,24},{20,28},{24,16},{28,20},{1,9},{5... | collective-permute-start | bytes 442376 | tf_op jit(solution)/shard_map/ppermute | solution.py:80
  48.5 6.2 %collective-permute-start.8 = (bf16[1,2,1,2,9,16,128]{6,5,4,3,2,1,0:T(8,128)(2,1)S(1)}, bf16[1,2,1,2,9,16,128]{6,5,4,3,2,1,0:T(8,128)(2,1)S(1)}, u32[]{:S(2)}, u32[]{:S(2)}) collective-permute-start(bf16[1,2,1,2,9,16,128]{6,5,4,3,2,1,0:T(8,128)(2,1)S(1)} %dynamic-slice_convert_fusion.2), channel_id=1, source_target_pairs={{0,16},{4,20},{8,24},{12,28},{16,0},{20,4},{24,8},{28,12},{1,17},{... | collective-permute-start | bytes 442376 | tf_op jit(solution)/shard_map/ppermute | solution.py:80
  53.2 4.4 %collective-permute-start.5 = (bf16[1,1,1,2,9,16,128]{6,5,4,3,2,1,0:T(8,128)(2,1)S(1)}, bf16[1,1,1,2,9,16,128]{6,5,4,3,2,1,0:T(8,128)(2,1)S(1)}, u32[]{:S(2)}, u32[]{:S(2)}) collective-permute-start(bf16[1,1,1,2,9,16,128]{6,5,4,3,2,1,0:T(8,128)(2,1)S(1)} %dynamic-slice_convert_fusion.7), channel_id=1, source_target_pairs={{0,16},{4,20},{8,24},{12,28},{16,0},{20,4},{24,8},{28,12},{1,17},{... | collective-permute-start | bytes 221192 | tf_op jit(solution)/shard_map/ppermute | solution.py:80
  54.8 4.4 %collective-permute-start.9 = (bf16[1,1,1,2,9,16,128]{6,5,4,3,2,1,0:T(8,128)(2,1)S(1)}, bf16[1,1,1,2,9,16,128]{6,5,4,3,2,1,0:T(8,128)(2,1)S(1)}, u32[]{:S(2)}, u32[]{:S(2)}) collective-permute-start(bf16[1,1,1,2,9,16,128]{6,5,4,3,2,1,0:T(8,128)(2,1)S(1)} %dynamic-slice_convert_fusion.6), channel_id=1, source_target_pairs={{0,8},{4,12},{8,0},{12,4},{16,24},{20,28},{24,16},{28,20},{1,9},{5... | collective-permute-start | bytes 221192 | tf_op jit(solution)/shard_map/ppermute | solution.py:80
  59.3 15.6 %slice-start.1 = ((s8[16777216]{0:T(1024)(128)(4,1)}), s8[4194304]{0:T(1024)(128)(4,1)S(1)}, s32[]{:S(2)}) async-start(s8[16777216]{0:T(1024)(128)(4,1)} %bitcast.253), calls=%async_computation.1 | async-start | bytes 8388608
  60.6 14.3 %slice-start.2 = ((s8[16777216]{0:T(1024)(128)(4,1)}), s8[4194304]{0:T(1024)(128)(4,1)S(1)}, s32[]{:S(2)}) async-start(s8[16777216]{0:T(1024)(128)(4,1)} %bitcast.253), calls=%async_computation.2 | async-start | bytes 8388608
  60.6 2.0 %collective-permute-start.12 = (bf16[2,2,1,2,9,16,128]{6,5,4,3,2,1,0:T(8,128)(2,1)S(1)}, bf16[2,2,1,2,9,16,128]{6,5,4,3,2,1,0:T(8,128)(2,1)S(1)}, u32[]{:S(2)}, u32[]{:S(2)}) collective-permute-start(bf16[2,2,1,2,9,16,128]{6,5,4,3,2,1,0:T(8,128)(2,1)S(1)} %constant_dynamic-slice_fusion.1), channel_id=1, source_target_pairs={{0,4},{4,0},{8,12},{12,8},{16,20},{20,16},{24,28},{28,24},{1,5},{5... | collective-permute-start | bytes 884744 | tf_op jit(solution)/shard_map/ppermute | solution.py:80
  61.4 13.5 %slice-start.3 = ((s8[16777216]{0:T(1024)(128)(4,1)}), s8[4194304]{0:T(1024)(128)(4,1)S(1)}, s32[]{:S(2)}) async-start(s8[16777216]{0:T(1024)(128)(4,1)} %bitcast.253), calls=%async_computation.3 | async-start | bytes 8388608
  62.1 2.1 %collective-permute-start.15 = (bf16[2,2,1,2,9,16,128]{6,5,4,3,2,1,0:T(8,128)(2,1)S(1)}, bf16[2,2,1,2,9,16,128]{6,5,4,3,2,1,0:T(8,128)(2,1)S(1)}, u32[]{:S(2)}, u32[]{:S(2)}) collective-permute-start(bf16[2,2,1,2,9,16,128]{6,5,4,3,2,1,0:T(8,128)(2,1)S(1)} %constant_dynamic-slice_fusion), channel_id=1, source_target_pairs={{0,4},{4,0},{8,12},{12,8},{16,20},{20,16},{24,28},{28,24},{1,5},{5... | collective-permute-start | bytes 884744 | tf_op jit(solution)/shard_map/ppermute | solution.py:80
  62.7 5.8 %collective-permute-start.13 = (bf16[1,2,1,2,9,16,128]{6,5,4,3,2,1,0:T(8,128)(2,1)S(1)}, bf16[1,2,1,2,9,16,128]{6,5,4,3,2,1,0:T(8,128)(2,1)S(1)}, u32[]{:S(2)}, u32[]{:S(2)}) collective-permute-start(bf16[1,2,1,2,9,16,128]{6,5,4,3,2,1,0:T(8,128)(2,1)S(1)} %dynamic-slice_convert_fusion.1), channel_id=1, source_target_pairs={{0,16},{4,20},{8,24},{12,28},{16,0},{20,4},{24,8},{28,12},{1,17},{... | collective-permute-start | bytes 442376 | tf_op jit(solution)/shard_map/ppermute | solution.py:80
  64.2 6.0 %collective-permute-start.16 = (bf16[2,1,1,2,9,16,128]{6,5,4,3,2,1,0:T(8,128)(2,1)S(1)}, bf16[2,1,1,2,9,16,128]{6,5,4,3,2,1,0:T(8,128)(2,1)S(1)}, u32[]{:S(2)}, u32[]{:S(2)}) collective-permute-start(bf16[2,1,1,2,9,16,128]{6,5,4,3,2,1,0:T(8,128)(2,1)S(1)} %dynamic-slice_convert_fusion), channel_id=1, source_target_pairs={{0,8},{4,12},{8,0},{12,4},{16,24},{20,28},{24,16},{28,20},{1,9},{5... | collective-permute-start | bytes 442376 | tf_op jit(solution)/shard_map/ppermute | solution.py:80
  68.6 4.4 %collective-permute-start.14 = (bf16[1,1,1,2,9,16,128]{6,5,4,3,2,1,0:T(8,128)(2,1)S(1)}, bf16[1,1,1,2,9,16,128]{6,5,4,3,2,1,0:T(8,128)(2,1)S(1)}, u32[]{:S(2)}, u32[]{:S(2)}) collective-permute-start(bf16[1,1,1,2,9,16,128]{6,5,4,3,2,1,0:T(8,128)(2,1)S(1)} %dynamic-slice_convert_fusion.5), channel_id=1, source_target_pairs={{0,8},{4,12},{8,0},{12,4},{16,24},{20,28},{24,16},{28,20},{1,9},{5... | collective-permute-start | bytes 221192 | tf_op jit(solution)/shard_map/ppermute | solution.py:80
  70.3 4.4 %collective-permute-start.17 = (bf16[1,1,1,2,9,16,128]{6,5,4,3,2,1,0:T(8,128)(2,1)S(1)}, bf16[1,1,1,2,9,16,128]{6,5,4,3,2,1,0:T(8,128)(2,1)S(1)}, u32[]{:S(2)}, u32[]{:S(2)}) collective-permute-start(bf16[1,1,1,2,9,16,128]{6,5,4,3,2,1,0:T(8,128)(2,1)S(1)} %dynamic-slice_convert_fusion.4), channel_id=1, source_target_pairs={{0,16},{4,20},{8,24},{12,28},{16,0},{20,4},{24,8},{28,12},{1,17},{... | collective-permute-start | bytes 221192 | tf_op jit(solution)/shard_map/ppermute | solution.py:80

commit v7 on v6

--- a/solution.py
+++ b/solution.py
@@ -40,8 +40,10 @@
     return (values * inverse[:, :, :, None]).astype(jnp.bfloat16)
 
 
-def pick(white, idx):
+def pick(white, idx, limit=None):
     hot = (idx[:, None] == jnp.arange(white.shape[1], dtype=jnp.int32)[None, :]).astype(jnp.bfloat16)
+    if limit is not None:
+        hot = hot * (jnp.arange(idx.shape[0], dtype=jnp.int32) < limit).astype(hot.dtype)[:, None]
     flat = white.reshape(white.shape[0], white.shape[1], -1)
     hot = jnp.broadcast_to(hot[None], (white.shape[0],) + hot.shape)
     out = jnp.einsum("hps,hsx->hpx", hot, flat, preferred_element_type=jnp.float32)
@@ -86,23 +88,18 @@
     n_tm = lax.axis_size("tm")
     n_sta = lax.axis_size("sta")
     hours_dev = spectra.shape[0]
-    p_tile = pairs.shape[3]
-    owned = p_tile // n_tm
+    owned = pairs.shape[3] // n_tm
     asked = [None] + [shifted(pairs[0, step, 1], "sta", -step) for step in range(1, n_sta)]
-    own = [None] + [whiten(pick(spectra, pairs[0, step, 0])) for step in range(1, n_sta)]
+    own = [None] + [whiten(pick(spectra, pairs[0, step, 0], counts[0, step])) for step in range(1, n_sta)]
     asked, own = lax.optimization_barrier((asked, own))
     picked = [pick(spectra, asked[step]) for step in range(1, n_sta)]
-    home, *picked = lax.optimization_barrier((pairs[0, 0], *picked))
-    own[0] = whiten(pick(spectra, home[0]))
-    visits = [pick(spectra, home[1])] + [
-        shifted(rows, "sta", step) for step, rows in enumerate(picked, 1)
-    ]
+    visits = [None] + [shifted(rows, "sta", step) for step, rows in enumerate(picked, 1)]
+    home, visits[-1] = lax.optimization_barrier((pairs[0, 0], visits[-1]))
+    own[0] = whiten(pick(spectra, home[0], counts[0, 0]))
+    visits[0] = pick(spectra, home[1])
 
     def reduce_tile(shift):
-        limit = counts[0, shift]
         value = cross(own[shift], whiten(visits[shift]))
-        slots = jnp.arange(p_tile, dtype=jnp.int32)
-        value = jnp.where((slots < limit)[:, None, None, None], value, 0.0)
         return sum_at_owner(value.astype(jnp.bfloat16), "tm", shift)
 
     early = sorted({0, n_sta - 1})

time: 80 us -> 82.2 us (1.028)
  starting transfers between devices: 23.2 us -> 24.3 us
  waiting for transfers between devices: 32.6 us -> 33.6 us
    lt x4 -> x0, other arithmetic: 2.5 us -> none  [reduce_tile(): value = jnp.where((slots < limit)[:, None, None, None], value, 0.0)]
    ppermute x6, waiting for transfers between devices: 20.7 us -> 22.7 us  [shifted(): return lax.ppermute(value, axis, pairs)]
    convert_element_type x4, other arithmetic: 0.75 us -> 2.53 us  [pick(): (jnp.arange(idx.shape[0], dtype=jnp.int32) < limit).astype(hot.dtype)]
    ppermute x12, waiting for transfers between devices: 11.9 us -> 10.9 us  [sum_at_owner(): got = lax.ppermute(give.astype(jnp.bfloat16), axis, swap)]
    ppermute x12, starting transfers between devices: 12.7 us -> 13.7 us  [sum_at_owner(): got = lax.ppermute(give.astype(jnp.bfloat16), axis, swap)]
    slice x1, local copies, waits for them, and re-layouts: 0.62 us -> 1.46 us  [per_device(): own[0] = whiten(pick(spectra, home[0], counts[0, 0]))]
    unnamed x20 -> x18, local copies, waits for them, and re-layouts: 1.67 us -> 1.59 us
  transfers between devices with their start and end apart: 18 -> 18, of which waited for: 7 -> 7; matrix products, arithmetic and copies ran while one was open for 18% -> 19% of each run, Pallas kernels for 0% -> 0%
where the time goes in v7:
time: 82.2 us; the launch traced here: 82 us
  waiting for transfers between devices  33.6 us (41%)
  starting transfers between devices  24.3 us (30%)
  matrix products  8.82 us (11%)
  local copies, waits for them, and re-layouts  8.07 us (10%)
  other arithmetic  6.44 us (8%)
    ppermute x6, waiting for transfers between devices, shifted(): return lax.ppermute(value, axis, pairs)  22.7 us
    ppermute x12, starting transfers between devices, sum_at_owner(): got = lax.ppermute(give.astype(jnp.bfloat16), axis, swap)  13.7 us
    ppermute x12, waiting for transfers between devices, sum_at_owner(): got = lax.ppermute(give.astype(jnp.bfloat16), axis, swap)  10.9 us
    ppermute x6, starting transfers between devices, shifted(): return lax.ppermute(value, axis, pairs)  10.6 us
    dot_general x8, matrix products, whiten(): jnp.dot(square, mean, precision=lax.Precision.HIGHEST, preferred_element_...  3.73 us
    dot_general x1, matrix products, per_device(): lagged = jnp.dot(rows, table, preferred_element_type=jnp.float32)  3.1 us
    convert_element_type x4, other arithmetic, pick(): (jnp.arange(idx.shape[0], dtype=jnp.int32) < limit).astype(hot.dtype)  2.53 us
    dot_general x8, matrix products, pick(): jnp.einsum('hps,hsx->hpx', hot, flat, preferred_element_type=jnp.float32)  1.98 us
  transfers between devices with their start and end apart: 18, of which 7 were waited for; matrix products, arithmetic and copies ran while one was open for 19% of the time, Pallas kernels for 0%

profile of v7, /device:TPU:8, one launch (start us, length us, event | category | flops | bytes accessed | tf_op | source)
XLA Modules:
  0.0 82.0 jit_solution(17422652213631766924)
XLA Ops:
  0.0 0.8 slice_bitcast_fusion.29
  0.8 3.0 %collective-permute-start.1 = (s32[16]{0:T(128)S(1)}, s32[16]{0:T(128)S(1)}, u32[]{:S(2)}, u32[]{:S(2)}) collective-permute-start(s32[16]{0:T(128)S(1)} %get-tuple-element.56), channel_id=1, source_target_pairs={{0,2},{1,3},{2,0},{3,1},{4,6},{5,7},{6,4},{7,5},{8,10},{9,11},{10,... | collective-permute-start | bytes 200 | tf_op jit(solution)/shard_map/ppermute | solution.py:19
  3.8 2.5 %collective-permute-start.2 = (s32[16]{0:T(128)S(1)}, s32[16]{0:T(128)S(1)}, u32[]{:S(2)}, u32[]{:S(2)}) collective-permute-start(s32[16]{0:T(128)S(1)} %get-tuple-element.55), channel_id=1, source_target_pairs={{0,1},{1,2},{2,3},{3,0},{4,5},{5,6},{6,7},{7,4},{8,9},{9,10},{10,1... | collective-permute-start | bytes 200 | tf_op jit(solution)/shard_map/ppermute | solution.py:19
  6.3 0.7 slice_bitcast_fusion.26
  7.0 1.5 %fusion.84 = (s32[1,1]{1,0:T(1,128)}, s32[1,1]{1,0:T(1,128)}, s32[1,1]{1,0:T(1,128)}, s32[1,1]{1,0:T(1,128)}) fusion(s32[1,4]{1,0:T(1,128)} %param.14), kind=kLoop, calls=%fused_computation.197 | loop fusion | bytes 32 | tf_op jit(solution)/shard_map/slice | solution.py:98
  8.4 0.7 compare_convert_fusion.2
  9.1 0.6 compare_convert_fusion.3
  9.7 1.2 %copy.59 = bf16[2,6,4,8,1024]{4,3,1,2,0:T(8,128)(2,1)S(1)} copy(bf16[2,6,4,8,1024]{4,3,2,1,0:T(8,128)(2,1)} %bitcast.296) | data formatting | bytes 1572864 | tf_op jit(solution)/shard_map/reshape | solution.py:47
  11.0 0.3 fusion.3
  11.3 0.1 copy.61
  11.4 0.7 copy-done
  12.1 0.5 fusion.12
  12.6 0.1 multiply_convert_fusion.6
  12.7 0.2 fusion.4
  12.9 0.1 copy.60
  13.1 0.5 fusion.13
  13.5 0.1 multiply_convert_fusion.7
  13.6 0.6 compare_convert_fusion.1
  14.3 0.2 fusion.2
  14.6 0.1 copy.62
  14.7 0.5 fusion.11
  15.2 0.1 multiply_convert_fusion.5
  15.3 0.7 compare_convert_fusion
  16.1 0.3 convolution_convert_fusion.4
  16.7 0.2 convolution_convert_fusion.1
  17.0 2.2 %collective-permute-start.10 = (bf16[2,16,6,8,128]{4,3,2,1,0:T(8,128)(2,1)S(1)}, bf16[2,16,6,8,128]{4,3,2,1,0:T(8,128)(2,1)S(1)}, u32[]{:S(2)}, u32[]{:S(2)}) collective-permute-start(bf16[2,16,6,8,128]{4,3,2,1,0:T(8,128)(2,1)S(1)} %bitcast.297), channel_id=1, source_target_pairs={{0,1},{1,2},{2,3},{3,0},{4,5},{5,6},{6,7},{7,4},{8,9},{9,10},{10,1... | collective-permute-start | bytes 1179656 | tf_op jit(solution)/shard_map/ppermute | solution.py:19
  19.3 0.2 convolution_convert_fusion
  19.6 2.8 %collective-permute-start.11 = (bf16[2,16,6,8,128]{4,3,2,1,0:T(8,128)(2,1)S(1)}, bf16[2,16,6,8,128]{4,3,2,1,0:T(8,128)(2,1)S(1)}, u32[]{:S(2)}, u32[]{:S(2)}) collective-permute-start(bf16[2,16,6,8,128]{4,3,2,1,0:T(8,128)(2,1)S(1)} %bitcast.298), channel_id=1, source_target_pairs={{0,2},{1,3},{2,0},{3,1},{4,6},{5,7},{6,4},{7,5},{8,10},{9,11},{10,... | collective-permute-start | bytes 1179656 | tf_op jit(solution)/shard_map/ppermute | solution.py:19
  22.6 22.7 %collective-permute-done.3 = bf16[2,16,6,8,128]{4,3,2,1,0:T(8,128)(2,1)S(1)} collective-permute-done((bf16[2,16,6,8,128]{4,3,2,1,0:T(8,128)(2,1)S(1)}, bf16[2,16,6,8,128]{4,3,2,1,0:T(8,128)(2,1)S(1)}, u32[]{:S(2)}, u32[]{:S(2)}) %collective-permute-start.3) | collective-permute-done | bytes 393248 | tf_op jit(solution)/shard_map/ppermute | solution.py:19
  45.4 0.5 fusion.8
  45.9 0.1 fusion.16
  46.0 0.4 subtract_reduce_fusion.2
  46.7 0.2 fusion.1
  46.9 0.1 copy.64
  47.1 0.5 fusion.10
  47.8 0.2 fusion
  48.0 0.1 copy.65
  48.2 0.5 fusion.9
  48.6 0.1 fusion.15
  48.8 0.4 subtract_reduce_fusion.3
  49.3 0.6 collective-permute-start.4
  50.0 1.6 %collective-permute-start.8 = (bf16[1,2,1,2,9,16,128]{6,5,4,3,2,1,0:T(8,128)(2,1)S(1)}, bf16[1,2,1,2,9,16,128]{6,5,4,3,2,1,0:T(8,128)(2,1)S(1)}, u32[]{:S(2)}, u32[]{:S(2)}) collective-permute-start(bf16[1,2,1,2,9,16,128]{6,5,4,3,2,1,0:T(8,128)(2,1)S(1)} %dynamic-slice_convert_fusion.2), channel_id=1, source_target_pairs={{0,16},{4,20},{8,24},{12,28},{16,0},{20,4},{24,8},{28,12},{1,17},{... | collective-permute-start | bytes 442376 | tf_op jit(solution)/shard_map/ppermute | solution.py:82
  51.7 1.6 %collective-permute-start.5 = (bf16[2,1,1,2,9,16,128]{6,5,4,3,2,1,0:T(8,128)(2,1)S(1)}, bf16[2,1,1,2,9,16,128]{6,5,4,3,2,1,0:T(8,128)(2,1)S(1)}, u32[]{:S(2)}, u32[]{:S(2)}) collective-permute-start(bf16[2,1,1,2,9,16,128]{6,5,4,3,2,1,0:T(8,128)(2,1)S(1)} %dynamic-slice_convert_fusion.3), channel_id=1, source_target_pairs={{0,8},{4,12},{8,0},{12,4},{16,24},{20,28},{24,16},{28,20},{1,9},{5... | collective-permute-start | bytes 442376 | tf_op jit(solution)/shard_map/ppermute | solution.py:82
  53.2 2.6 %collective-permute-done.8 = bf16[1,2,1,2,9,16,128]{6,5,4,3,2,1,0:T(8,128)(2,1)S(1)} collective-permute-done((bf16[1,2,1,2,9,16,128]{6,5,4,3,2,1,0:T(8,128)(2,1)S(1)}, bf16[1,2,1,2,9,16,128]{6,5,4,3,2,1,0:T(8,128)(2,1)S(1)}, u32[]{:S(2)}, u32[]{:S(2)}) %collective-permute-start.8) | collective-permute-done | bytes 147488 | tf_op jit(solution)/shard_map/ppermute | solution.py:82
  55.9 1.6 %collective-permute-start.9 = (bf16[1,1,1,2,9,16,128]{6,5,4,3,2,1,0:T(8,128)(2,1)S(1)}, bf16[1,1,1,2,9,16,128]{6,5,4,3,2,1,0:T(8,128)(2,1)S(1)}, u32[]{:S(2)}, u32[]{:S(2)}) collective-permute-start(bf16[1,1,1,2,9,16,128]{6,5,4,3,2,1,0:T(8,128)(2,1)S(1)} %dynamic-slice_convert_fusion.6), channel_id=1, source_target_pairs={{0,8},{4,12},{8,0},{12,4},{16,24},{20,28},{24,16},{28,20},{1,9},{5... | collective-permute-start | bytes 221192 | tf_op jit(solution)/shard_map/ppermute | solution.py:82
  57.5 1.6 %collective-permute-start.6 = (bf16[1,1,1,2,9,16,128]{6,5,4,3,2,1,0:T(8,128)(2,1)S(1)}, bf16[1,1,1,2,9,16,128]{6,5,4,3,2,1,0:T(8,128)(2,1)S(1)}, u32[]{:S(2)}, u32[]{:S(2)}) collective-permute-start(bf16[1,1,1,2,9,16,128]{6,5,4,3,2,1,0:T(8,128)(2,1)S(1)} %dynamic-slice_convert_fusion.7), channel_id=1, source_target_pairs={{0,16},{4,20},{8,24},{12,28},{16,0},{20,4},{24,8},{28,12},{1,17},{... | collective-permute-start | bytes 221192 | tf_op jit(solution)/shard_map/ppermute | solution.py:82
  59.1 1.2 %collective-permute-done.9 = bf16[1,1,1,2,9,16,128]{6,5,4,3,2,1,0:T(8,128)(2,1)S(1)} collective-permute-done((bf16[1,1,1,2,9,16,128]{6,5,4,3,2,1,0:T(8,128)(2,1)S(1)}, bf16[1,1,1,2,9,16,128]{6,5,4,3,2,1,0:T(8,128)(2,1)S(1)}, u32[]{:S(2)}, u32[]{:S(2)}) %collective-permute-start.9) | collective-permute-done | bytes 73760 | tf_op jit(solution)/shard_map/ppermute | solution.py:82
  60.3 1.6 %collective-permute-done.6 = bf16[1,1,1,2,9,16,128]{6,5,4,3,2,1,0:T(8,128)(2,1)S(1)} collective-permute-done((bf16[1,1,1,2,9,16,128]{6,5,4,3,2,1,0:T(8,128)(2,1)S(1)}, bf16[1,1,1,2,9,16,128]{6,5,4,3,2,1,0:T(8,128)(2,1)S(1)}, u32[]{:S(2)}, u32[]{:S(2)}) %collective-permute-start.6) | collective-permute-done | bytes 73760 | tf_op jit(solution)/shard_map/ppermute | solution.py:82
  62.0 0.5 fusion.7
  62.5 0.1 fusion.17
  62.7 0.4 subtract_reduce_fusion.1
  63.3 0.5 fusion.6
  63.9 0.4 subtract_reduce_fusion
  64.4 0.6 collective-permute-start.15
  65.1 1.6 %collective-permute-start.13 = (bf16[1,2,1,2,9,16,128]{6,5,4,3,2,1,0:T(8,128)(2,1)S(1)}, bf16[1,2,1,2,9,16,128]{6,5,4,3,2,1,0:T(8,128)(2,1)S(1)}, u32[]{:S(2)}, u32[]{:S(2)}) collective-permute-start(bf16[1,2,1,2,9,16,128]{6,5,4,3,2,1,0:T(8,128)(2,1)S(1)} %dynamic-slice_convert_fusion.1), channel_id=1, source_target_pairs={{0,16},{4,20},{8,24},{12,28},{16,0},{20,4},{24,8},{28,12},{1,17},{... | collective-permute-start | bytes 442376 | tf_op jit(solution)/shard_map/ppermute | solution.py:82
  66.8 1.5 %collective-permute-start.16 = (bf16[2,1,1,2,9,16,128]{6,5,4,3,2,1,0:T(8,128)(2,1)S(1)}, bf16[2,1,1,2,9,16,128]{6,5,4,3,2,1,0:T(8,128)(2,1)S(1)}, u32[]{:S(2)}, u32[]{:S(2)}) collective-permute-start(bf16[2,1,1,2,9,16,128]{6,5,4,3,2,1,0:T(8,128)(2,1)S(1)} %dynamic-slice_convert_fusion), channel_id=1, source_target_pairs={{0,8},{4,12},{8,0},{12,4},{16,24},{20,28},{24,16},{28,20},{1,9},{5... | collective-permute-start | bytes 442376 | tf_op jit(solution)/shard_map/ppermute | solution.py:82
  68.3 2.7 %collective-permute-done.13 = bf16[1,2,1,2,9,16,128]{6,5,4,3,2,1,0:T(8,128)(2,1)S(1)} collective-permute-done((bf16[1,2,1,2,9,16,128]{6,5,4,3,2,1,0:T(8,128)(2,1)S(1)}, bf16[1,2,1,2,9,16,128]{6,5,4,3,2,1,0:T(8,128)(2,1)S(1)}, u32[]{:S(2)}, u32[]{:S(2)}) %collective-permute-start.13) | collective-permute-done | bytes 147488 | tf_op jit(solution)/shard_map/ppermute | solution.py:82
  71.0 1.5 %collective-permute-start.14 = (bf16[1,1,1,2,9,16,128]{6,5,4,3,2,1,0:T(8,128)(2,1)S(1)}, bf16[1,1,1,2,9,16,128]{6,5,4,3,2,1,0:T(8,128)(2,1)S(1)}, u32[]{:S(2)}, u32[]{:S(2)}) collective-permute-start(bf16[1,1,1,2,9,16,128]{6,5,4,3,2,1,0:T(8,128)(2,1)S(1)} %dynamic-slice_convert_fusion.5), channel_id=1, source_target_pairs={{0,8},{4,12},{8,0},{12,4},{16,24},{20,28},{24,16},{28,20},{1,9},{5... | collective-permute-start | bytes 221192 | tf_op jit(solution)/shard_map/ppermute | solution.py:82
  72.6 1.6 %collective-permute-start.17 = (bf16[1,1,1,2,9,16,128]{6,5,4,3,2,1,0:T(8,128)(2,1)S(1)}, bf16[1,1,1,2,9,16,128]{6,5,4,3,2,1,0:T(8,128)(2,1)S(1)}, u32[]{:S(2)}, u32[]{:S(2)}) collective-permute-start(bf16[1,1,1,2,9,16,128]{6,5,4,3,2,1,0:T(8,128)(2,1)S(1)} %dynamic-slice_convert_fusion.4), channel_id=1, source_target_pairs={{0,16},{4,20},{8,24},{12,28},{16,0},{20,4},{24,8},{28,12},{1,17},{... | collective-permute-start | bytes 221192 | tf_op jit(solution)/shard_map/ppermute | solution.py:82
  74.2 1.3 %collective-permute-done.14 = bf16[1,1,1,2,9,16,128]{6,5,4,3,2,1,0:T(8,128)(2,1)S(1)} collective-permute-done((bf16[1,1,1,2,9,16,128]{6,5,4,3,2,1,0:T(8,128)(2,1)S(1)}, bf16[1,1,1,2,9,16,128]{6,5,4,3,2,1,0:T(8,128)(2,1)S(1)}, u32[]{:S(2)}, u32[]{:S(2)}) %collective-permute-start.14) | collective-permute-done | bytes 73760 | tf_op jit(solution)/shard_map/ppermute | solution.py:82
  75.5 1.5 %collective-permute-done.17 = bf16[1,1,1,2,9,16,128]{6,5,4,3,2,1,0:T(8,128)(2,1)S(1)} collective-permute-done((bf16[1,1,1,2,9,16,128]{6,5,4,3,2,1,0:T(8,128)(2,1)S(1)}, bf16[1,1,1,2,9,16,128]{6,5,4,3,2,1,0:T(8,128)(2,1)S(1)}, u32[]{:S(2)}, u32[]{:S(2)}) %collective-permute-start.17) | collective-permute-done | bytes 73760 | tf_op jit(solution)/shard_map/ppermute | solution.py:82
  77.1 3.1 %fusion.5 = bf16[72,4001]{1,0:T(8,128)(2,1)S(1)} fusion(bf16[2048,4001]{1,0:T(8,128)(2,1)S(1)} %bitcast.254, bf16[9,8,16,128]{3,2,1,0:T(8,128)(2,1)S(1)} %bitcast.286), kind=kOutput, calls=%fused_computation.14 | convolution fusion | flops 1180519168 | bytes 17259152 | tf_op jit(solution)/shard_map/dot_general | solution.py:114
  80.2 0.3 reshape.395
  80.5 1.5 %copy.47 = bf16[1,4,2,9,4001]{4,2,3,1,0:T(2,128)(2,1)} copy(bf16[1,4,2,9,4001]{4,3,2,1,0:T(8,128)(2,1)S(1)} %reshape.395) | data formatting | bytes 1152288 | tf_op jit(solution)/shard_map/reshape | solution.py:116
  (77 shorter events, 2.9 us)
Async XLA Ops:
  0.8 15.2 %collective-permute-start = (s32[16]{0:T(128)S(1)}, s32[16]{0:T(128)S(1)}, u32[]{:S(2)}, u32[]{:S(2)}) collective-permute-start(s32[16]{0:T(128)S(1)} %get-tuple-element.57), channel_id=1, source_target_pairs={{0,3},{1,0},{2,1},{3,2},{4,7},{5,4},{6,5},{7,6},{8,11},{9,8},{10,9... | collective-permute-start | bytes 200 | tf_op jit(solution)/shard_map/ppermute | solution.py:19
  0.8 15.2 %collective-permute-start.1 = (s32[16]{0:T(128)S(1)}, s32[16]{0:T(128)S(1)}, u32[]{:S(2)}, u32[]{:S(2)}) collective-permute-start(s32[16]{0:T(128)S(1)} %get-tuple-element.56), channel_id=1, source_target_pairs={{0,2},{1,3},{2,0},{3,1},{4,6},{5,7},{6,4},{7,5},{8,10},{9,11},{10,... | collective-permute-start | bytes 200 | tf_op jit(solution)/shard_map/ppermute | solution.py:19
  3.8 12.2 %collective-permute-start.2 = (s32[16]{0:T(128)S(1)}, s32[16]{0:T(128)S(1)}, u32[]{:S(2)}, u32[]{:S(2)}) collective-permute-start(s32[16]{0:T(128)S(1)} %get-tuple-element.55), channel_id=1, source_target_pairs={{0,1},{1,2},{2,3},{3,0},{4,5},{5,6},{6,7},{7,4},{8,9},{9,10},{10,1... | collective-permute-start | bytes 200 | tf_op jit(solution)/shard_map/ppermute | solution.py:19
  11.3 0.8 %copy-start = (f32[128,128,1,1,1]{1,0,4,3,2:T(8,128)S(1)}, f32[128,128,1,1,1]{1,0,4,3,2:T(8,128)}, u32[]{:S(2)}) copy-start(f32[128,128,1,1,1]{1,0,4,3,2:T(8,128)} %constant.47) | copy-start | bytes 196612
  16.4 29.0 %collective-permute-start.3 = (bf16[2,16,6,8,128]{4,3,2,1,0:T(8,128)(2,1)S(1)}, bf16[2,16,6,8,128]{4,3,2,1,0:T(8,128)(2,1)S(1)}, u32[]{:S(2)}, u32[]{:S(2)}) collective-permute-start(bf16[2,16,6,8,128]{4,3,2,1,0:T(8,128)(2,1)S(1)} %bitcast.299), channel_id=1, source_target_pairs={{0,3},{1,0},{2,1},{3,2},{4,7},{5,4},{6,5},{7,6},{8,11},{9,8},{10,9... | collective-permute-start | bytes 1179656 | tf_op jit(solution)/shard_map/ppermute | solution.py:19
  17.0 45.0 %collective-permute-start.10 = (bf16[2,16,6,8,128]{4,3,2,1,0:T(8,128)(2,1)S(1)}, bf16[2,16,6,8,128]{4,3,2,1,0:T(8,128)(2,1)S(1)}, u32[]{:S(2)}, u32[]{:S(2)}) collective-permute-start(bf16[2,16,6,8,128]{4,3,2,1,0:T(8,128)(2,1)S(1)} %bitcast.297), channel_id=1, source_target_pairs={{0,1},{1,2},{2,3},{3,0},{4,5},{5,6},{6,7},{7,4},{8,9},{9,10},{10,1... | collective-permute-start | bytes 1179656 | tf_op jit(solution)/shard_map/ppermute | solution.py:19
  19.6 42.4 %collective-permute-start.11 = (bf16[2,16,6,8,128]{4,3,2,1,0:T(8,128)(2,1)S(1)}, bf16[2,16,6,8,128]{4,3,2,1,0:T(8,128)(2,1)S(1)}, u32[]{:S(2)}, u32[]{:S(2)}) collective-permute-start(bf16[2,16,6,8,128]{4,3,2,1,0:T(8,128)(2,1)S(1)} %bitcast.298), channel_id=1, source_target_pairs={{0,2},{1,3},{2,0},{3,1},{4,6},{5,7},{6,4},{7,5},{8,10},{9,11},{10,... | collective-permute-start | bytes 1179656 | tf_op jit(solution)/shard_map/ppermute | solution.py:19
  46.5 3.3 %collective-permute-start.7 = (bf16[2,2,1,2,9,16,128]{6,5,4,3,2,1,0:T(8,128)(2,1)S(1)}, bf16[2,2,1,2,9,16,128]{6,5,4,3,2,1,0:T(8,128)(2,1)S(1)}, u32[]{:S(2)}, u32[]{:S(2)}) collective-permute-start(bf16[2,2,1,2,9,16,128]{6,5,4,3,2,1,0:T(8,128)(2,1)S(1)} %fusion.62), channel_id=1, source_target_pairs={{0,4},{4,0},{8,12},{12,8},{16,20},{20,16},{24,28},{28,24},{1,5},{5... | collective-permute-start | bytes 884744 | tf_op jit(solution)/shard_map/ppermute | solution.py:82
  48.8 28.2 %slice-start = ((s8[16777216]{0:T(1024)(128)(4,1)}), s8[4194304]{0:T(1024)(128)(4,1)S(1)}, s32[]{:S(2)}) async-start(s8[16777216]{0:T(1024)(128)(4,1)} %bitcast.253), calls=%async_computation | async-start | bytes 8388608
  49.3 2.3 %collective-permute-start.4 = (bf16[2,2,1,2,9,16,128]{6,5,4,3,2,1,0:T(8,128)(2,1)S(1)}, bf16[2,2,1,2,9,16,128]{6,5,4,3,2,1,0:T(8,128)(2,1)S(1)}, u32[]{:S(2)}, u32[]{:S(2)}) collective-permute-start(bf16[2,2,1,2,9,16,128]{6,5,4,3,2,1,0:T(8,128)(2,1)S(1)} %fusion.64), channel_id=1, source_target_pairs={{0,4},{4,0},{8,12},{12,8},{16,20},{20,16},{24,28},{28,24},{1,5},{5... | collective-permute-start | bytes 884744 | tf_op jit(solution)/shard_map/ppermute | solution.py:82
  50.0 5.8 %collective-permute-start.8 = (bf16[1,2,1,2,9,16,128]{6,5,4,3,2,1,0:T(8,128)(2,1)S(1)}, bf16[1,2,1,2,9,16,128]{6,5,4,3,2,1,0:T(8,128)(2,1)S(1)}, u32[]{:S(2)}, u32[]{:S(2)}) collective-permute-start(bf16[1,2,1,2,9,16,128]{6,5,4,3,2,1,0:T(8,128)(2,1)S(1)} %dynamic-slice_convert_fusion.2), channel_id=1, source_target_pairs={{0,16},{4,20},{8,24},{12,28},{16,0},{20,4},{24,8},{28,12},{1,17},{... | collective-permute-start | bytes 442376 | tf_op jit(solution)/shard_map/ppermute | solution.py:82
  51.7 5.8 %collective-permute-start.5 = (bf16[2,1,1,2,9,16,128]{6,5,4,3,2,1,0:T(8,128)(2,1)S(1)}, bf16[2,1,1,2,9,16,128]{6,5,4,3,2,1,0:T(8,128)(2,1)S(1)}, u32[]{:S(2)}, u32[]{:S(2)}) collective-permute-start(bf16[2,1,1,2,9,16,128]{6,5,4,3,2,1,0:T(8,128)(2,1)S(1)} %dynamic-slice_convert_fusion.3), channel_id=1, source_target_pairs={{0,8},{4,12},{8,0},{12,4},{16,24},{20,28},{24,16},{28,20},{1,9},{5... | collective-permute-start | bytes 442376 | tf_op jit(solution)/shard_map/ppermute | solution.py:82
  55.9 21.2 %slice-start.1 = ((s8[16777216]{0:T(1024)(128)(4,1)}), s8[4194304]{0:T(1024)(128)(4,1)S(1)}, s32[]{:S(2)}) async-start(s8[16777216]{0:T(1024)(128)(4,1)} %bitcast.253), calls=%async_computation.1 | async-start | bytes 8388608
  55.9 4.4 %collective-permute-start.9 = (bf16[1,1,1,2,9,16,128]{6,5,4,3,2,1,0:T(8,128)(2,1)S(1)}, bf16[1,1,1,2,9,16,128]{6,5,4,3,2,1,0:T(8,128)(2,1)S(1)}, u32[]{:S(2)}, u32[]{:S(2)}) collective-permute-start(bf16[1,1,1,2,9,16,128]{6,5,4,3,2,1,0:T(8,128)(2,1)S(1)} %dynamic-slice_convert_fusion.6), channel_id=1, source_target_pairs={{0,8},{4,12},{8,0},{12,4},{16,24},{20,28},{24,16},{28,20},{1,9},{5... | collective-permute-start | bytes 221192 | tf_op jit(solution)/shard_map/ppermute | solution.py:82
  57.5 4.4 %collective-permute-start.6 = (bf16[1,1,1,2,9,16,128]{6,5,4,3,2,1,0:T(8,128)(2,1)S(1)}, bf16[1,1,1,2,9,16,128]{6,5,4,3,2,1,0:T(8,128)(2,1)S(1)}, u32[]{:S(2)}, u32[]{:S(2)}) collective-permute-start(bf16[1,1,1,2,9,16,128]{6,5,4,3,2,1,0:T(8,128)(2,1)S(1)} %dynamic-slice_convert_fusion.7), channel_id=1, source_target_pairs={{0,16},{4,20},{8,24},{12,28},{16,0},{20,4},{24,8},{28,12},{1,17},{... | collective-permute-start | bytes 221192 | tf_op jit(solution)/shard_map/ppermute | solution.py:82
  62.7 14.4 %slice-start.2 = ((s8[16777216]{0:T(1024)(128)(4,1)}), s8[4194304]{0:T(1024)(128)(4,1)S(1)}, s32[]{:S(2)}) async-start(s8[16777216]{0:T(1024)(128)(4,1)} %bitcast.253), calls=%async_computation.2 | async-start | bytes 8388608
  63.1 1.8 %collective-permute-start.12 = (bf16[2,2,1,2,9,16,128]{6,5,4,3,2,1,0:T(8,128)(2,1)S(1)}, bf16[2,2,1,2,9,16,128]{6,5,4,3,2,1,0:T(8,128)(2,1)S(1)}, u32[]{:S(2)}, u32[]{:S(2)}) collective-permute-start(bf16[2,2,1,2,9,16,128]{6,5,4,3,2,1,0:T(8,128)(2,1)S(1)} %fusion.60), channel_id=1, source_target_pairs={{0,4},{4,0},{8,12},{12,8},{16,20},{20,16},{24,28},{28,24},{1,5},{5... | collective-permute-start | bytes 884744 | tf_op jit(solution)/shard_map/ppermute | solution.py:82
  63.9 13.2 %slice-start.3 = ((s8[16777216]{0:T(1024)(128)(4,1)}), s8[4194304]{0:T(1024)(128)(4,1)S(1)}, s32[]{:S(2)}) async-start(s8[16777216]{0:T(1024)(128)(4,1)} %bitcast.253), calls=%async_computation.3 | async-start | bytes 8388608
  64.4 2.3 %collective-permute-start.15 = (bf16[2,2,1,2,9,16,128]{6,5,4,3,2,1,0:T(8,128)(2,1)S(1)}, bf16[2,2,1,2,9,16,128]{6,5,4,3,2,1,0:T(8,128)(2,1)S(1)}, u32[]{:S(2)}, u32[]{:S(2)}) collective-permute-start(bf16[2,2,1,2,9,16,128]{6,5,4,3,2,1,0:T(8,128)(2,1)S(1)} %fusion.58), channel_id=1, source_target_pairs={{0,4},{4,0},{8,12},{12,8},{16,20},{20,16},{24,28},{28,24},{1,5},{5... | collective-permute-start | bytes 884744 | tf_op jit(solution)/shard_map/ppermute | solution.py:82
  65.1 5.8 %collective-permute-start.13 = (bf16[1,2,1,2,9,16,128]{6,5,4,3,2,1,0:T(8,128)(2,1)S(1)}, bf16[1,2,1,2,9,16,128]{6,5,4,3,2,1,0:T(8,128)(2,1)S(1)}, u32[]{:S(2)}, u32[]{:S(2)}) collective-permute-start(bf16[1,2,1,2,9,16,128]{6,5,4,3,2,1,0:T(8,128)(2,1)S(1)} %dynamic-slice_convert_fusion.1), channel_id=1, source_target_pairs={{0,16},{4,20},{8,24},{12,28},{16,0},{20,4},{24,8},{28,12},{1,17},{... | collective-permute-start | bytes 442376 | tf_op jit(solution)/shard_map/ppermute | solution.py:82
  66.8 5.7 %collective-permute-start.16 = (bf16[2,1,1,2,9,16,128]{6,5,4,3,2,1,0:T(8,128)(2,1)S(1)}, bf16[2,1,1,2,9,16,128]{6,5,4,3,2,1,0:T(8,128)(2,1)S(1)}, u32[]{:S(2)}, u32[]{:S(2)}) collective-permute-start(bf16[2,1,1,2,9,16,128]{6,5,4,3,2,1,0:T(8,128)(2,1)S(1)} %dynamic-slice_convert_fusion), channel_id=1, source_target_pairs={{0,8},{4,12},{8,0},{12,4},{16,24},{20,28},{24,16},{28,20},{1,9},{5... | collective-permute-start | bytes 442376 | tf_op jit(solution)/shard_map/ppermute | solution.py:82
  71.0 4.4 %collective-permute-start.14 = (bf16[1,1,1,2,9,16,128]{6,5,4,3,2,1,0:T(8,128)(2,1)S(1)}, bf16[1,1,1,2,9,16,128]{6,5,4,3,2,1,0:T(8,128)(2,1)S(1)}, u32[]{:S(2)}, u32[]{:S(2)}) collective-permute-start(bf16[1,1,1,2,9,16,128]{6,5,4,3,2,1,0:T(8,128)(2,1)S(1)} %dynamic-slice_convert_fusion.5), channel_id=1, source_target_pairs={{0,8},{4,12},{8,0},{12,4},{16,24},{20,28},{24,16},{28,20},{1,9},{5... | collective-permute-start | bytes 221192 | tf_op jit(solution)/shard_map/ppermute | solution.py:82
  72.6 4.4 %collective-permute-start.17 = (bf16[1,1,1,2,9,16,128]{6,5,4,3,2,1,0:T(8,128)(2,1)S(1)}, bf16[1,1,1,2,9,16,128]{6,5,4,3,2,1,0:T(8,128)(2,1)S(1)}, u32[]{:S(2)}, u32[]{:S(2)}) collective-permute-start(bf16[1,1,1,2,9,16,128]{6,5,4,3,2,1,0:T(8,128)(2,1)S(1)} %dynamic-slice_convert_fusion.4), channel_id=1, source_target_pairs={{0,16},{4,20},{8,24},{12,28},{16,0},{20,4},{24,8},{28,12},{1,17},{... | collective-permute-start | bytes 221192 | tf_op jit(solution)/shard_map/ppermute | solution.py:82
